TPU v7x, 32 devices: a whole 2x2x4 slice. The times are simulated.
32 devices in a mesh: seq: 2 (over core), head: 4 (over y, x), dp: 4 (over z).
Axes of the slice: x: 2, y: 2, z: 4, core: 2. Of those that a mesh axis runs over, the one named last changes fastest.
Arguments:
- tokens: bfloat16 [4, 4096, 768], P('dp', 'seq', 'head'), may hold values from -6 to 6
- attn_gain: bfloat16 [768], replicated, may hold values from 0.099609375 to 1.8984375
- attn_shift: bfloat16 [768], replicated, may hold values from -3 to 3
- qkv_weight: bfloat16 [768, 2304], P(None, 'head'), may hold values from -0.21875 to 0.21875
- qkv_bias: bfloat16 [2304], P('head'), may hold values from -3 to 3
- query_map: bfloat16 [12, 64, 64], P('head'), may hold values from -1.5 to 1.5
- key_map: bfloat16 [12, 64, 64], P('head'), may hold values from -1.5 to 1.5
- out_weight: bfloat16 [768, 768], P('head'), may hold values from -0.4375 to 0.4375
- out_bias: bfloat16 [768], P('head'), may hold values from -3 to 3
- mlp_gain: bfloat16 [768], replicated, may hold values from 0.099609375 to 1.8984375
- mlp_shift: bfloat16 [768], replicated, may hold values from -3 to 3
- up_weight: bfloat16 [768, 3072], P(None, 'head'), may hold values from -1 to 1
- up_bias: bfloat16 [3072], P('head'), may hold values from -3 to 3
- down_weight: bfloat16 [3072, 768], P('head'), may hold values from -0.4375 to 0.4375
- down_bias: bfloat16 [768], P('head'), may hold values from -3 to 3
- positions: int32 [4, 4096], P('dp', 'seq'), may hold values from 0 to 2048, as said below
- out_grad: bfloat16 [4, 4096, 768], P('dp', 'seq', 'head'), may hold values from -6 to 6
Outputs:
- block_out: bfloat16 [4, 4096, 768], P('dp', 'seq', 'head')
- tokens_grad: bfloat16 [4, 4096, 768], P('dp', 'seq', 'head')
- attngain_grad: float32 [768], P('head')
- attnshift_grad: float32 [768], P('head')
- qkvweight_grad: float32 [768, 2304], P(None, 'head')
- qkvbias_grad: float32 [2304], P('head')
- querymap_grad: float32 [12, 64, 64], P('head')
- keymap_grad: float32 [12, 64, 64], P('head')
- outweight_grad: float32 [768, 768], P('head')
- outbias_grad: float32 [768], P('head')
- mlpgain_grad: float32 [768], P('head')
- mlpshift_grad: float32 [768], P('head')
- upweight_grad: float32 [768, 3072], P(None, 'head')
- upbias_grad: float32 [3072], P('head')
- downweight_grad: float32 [3072, 768], P('head')
- downbias_grad: float32 [768], P('head')
Inputs may be any that keep to these rules, and one draw needn't show every extreme that they name: positions[s, t] is 0 where a document begins, which includes t = 0, and one more than positions[s, t - 1] elsewhere.
All inputs are finite; a program needn't handle non-finite values.
Results may differ from a plain program's by a relative error of at most 0.029.
Values may be sent and summed in bfloat16 or wider, within the bound.
No kernel may reach another device: no remote copies, remote signals or barrier semaphores. Data moves between devices by JAX's collectives and lax.ppermute only.
A program may use at most 192 MiB of HBM per device.

v0:
```python
import jax
import jax.numpy as jnp
from jax import lax
from jax.sharding import PartitionSpec as P

BLOCK = 64


eps = 1e-05
gelu_scale = 0.7978845608028654
highest = lax.Precision.HIGHEST


def entering(part, axis, combine, identity, reverse):
    count = lax.axis_size(axis)
    place = lax.axis_index(axis)
    ahead = count - 1 - place if reverse else place
    gathered = jax.tree.map(lambda a: lax.all_gather(a, axis), part)
    state = jax.tree.map(lambda a, e: jnp.zeros_like(a) + jnp.asarray(e, a.dtype), part, identity)

    def one(lap, state):
        source = count - 1 - lap if reverse else lap
        return combine(
            state, jax.tree.map(lambda a: lax.dynamic_index_in_dim(a, source, 0, False), gathered)
        )

    return lax.fori_loop(0, ahead, one, state)


def widen(part):
    return lax.all_gather(part, "head", axis=2, tiled=True)


def narrow(part):
    return lax.psum_scatter(part, "head", scatter_dimension=2, tiled=True)


def norm_rows(values):
    center = values - jnp.mean(values, axis=-1, keepdims=True)
    inv_std = lax.rsqrt(jnp.mean(center * center, axis=-1, keepdims=True) + eps)
    return (center * inv_std, inv_std)


def gelu_pair(up_pre):
    tanh_value = jnp.tanh(gelu_scale * (up_pre + 0.044715 * up_pre * up_pre * up_pre))
    gelu_value = 0.5 * up_pre * (1.0 + tanh_value)
    gelu_slope = 0.5 * (1.0 + tanh_value) + 0.5 * up_pre * (
        1.0 - tanh_value * tanh_value
    ) * gelu_scale * (1.0 + 3.0 * 0.044715 * up_pre * up_pre)
    return (gelu_value, gelu_slope)


def feature_maps(logits):
    return jnp.concatenate(
        [jax.nn.softmax(logits, axis=-1), jax.nn.softmax(-logits, axis=-1)], axis=-1
    )


def feature_back(logits, feat_grad):
    half_width = logits.shape[-1]
    plus_soft = jax.nn.softmax(logits, axis=-1)
    minus_soft = jax.nn.softmax(-logits, axis=-1)
    plus_grad = feat_grad[..., :half_width]
    minus_grad = feat_grad[..., half_width:]
    plus_part = plus_soft * (plus_grad - jnp.sum(plus_grad * plus_soft, axis=-1, keepdims=True))
    minus_part = minus_soft * (
        minus_grad - jnp.sum(minus_grad * minus_soft, axis=-1, keepdims=True)
    )
    return plus_part - minus_part


def chain(earlier, later):
    keep_later = 1.0 - later[0]
    return (
        earlier[0] + later[0] - earlier[0] * later[0],
        later[1] + keep_later[:, None, None, None] * earlier[1],
        later[2] + keep_later[:, None, None] * earlier[2],
    )


def block_tables(positions):
    seq_count, length = positions.shape
    nblock = length // BLOCK
    token_index = jnp.arange(length, dtype=jnp.int32)
    doc_start = (token_index[None, :] - positions).reshape(seq_count, nblock, BLOCK)
    block_index = token_index.reshape(nblock, BLOCK)
    block_first = block_index[:, 0]
    pair_mask = (block_index[None, :, None, :] <= block_index[None, :, :, None]) & (
        block_index[None, :, None, :] >= doc_start[:, :, :, None]
    )
    included = (doc_start == doc_start[:, :, -1:]).astype(jnp.float32)
    resets = (doc_start[:, :, -1] >= block_first[None, :]).astype(jnp.float32)
    uses_state = (doc_start < block_first[None, :, None]).astype(jnp.float32)
    counts = jnp.cumsum(resets, axis=1)
    counts_before = counts - resets
    block_order = jnp.arange(nblock)
    earlier_mask = (
        (block_order[None, :, None] > block_order[None, None, :])
        & (counts_before[:, :, None] == counts[:, None, :])
    ).astype(jnp.float32)
    later_mask = (
        (block_order[None, :, None] < block_order[None, None, :])
        & (counts_before[:, None, :] == counts[:, :, None])
    ).astype(jnp.float32)
    keep_mask = (counts_before == 0.0).astype(jnp.float32)
    end_mask = (counts == counts[:, -1:]).astype(jnp.float32)
    reset_flag = (counts[:, -1] > 0.0).astype(jnp.float32)
    return (
        pair_mask,
        included,
        uses_state,
        earlier_mask,
        later_mask,
        keep_mask,
        end_mask,
        reset_flag,
    )


def mixer_forward(query_feat, key_feat, value_part, tables):
    pair_mask, included, uses_state, earlier_mask, later_mask, keep_mask, end_mask, reset_flag = (
        tables
    )
    scores = jnp.einsum(
        "bnihf,bnjhf->bnhij", query_feat, key_feat, preferred_element_type=jnp.float32
    )
    scores = jnp.where(pair_mask[:, :, None], scores, 0.0).astype(jnp.bfloat16)
    numer = jnp.einsum("bnhij,bnjhe->bnihe", scores, value_part, preferred_element_type=jnp.float32)
    denom = jnp.transpose(jnp.sum(scores.astype(jnp.float32), axis=-1), (0, 1, 3, 2))
    masked_keys = key_feat * included[..., None, None].astype(jnp.bfloat16)
    block_sums = jnp.einsum(
        "bnjhf,bnjhe->bnhfe", masked_keys, value_part, preferred_element_type=jnp.float32
    )
    block_totals = jnp.sum(masked_keys.astype(jnp.float32), axis=2)
    device_sum = jnp.einsum("bc,bchfe->bhfe", end_mask, block_sums, precision=highest)
    device_total = jnp.einsum("bc,bchf->bhf", end_mask, block_totals, precision=highest)
    identity = (
        jnp.zeros_like(reset_flag),
        jnp.zeros_like(device_sum),
        jnp.zeros_like(device_total),
    )
    entered = entering((reset_flag, device_sum, device_total), "seq", chain, identity, False)
    states = (
        jnp.einsum("bcd,bdhfe->bchfe", earlier_mask, block_sums, precision=highest)
        + keep_mask[:, :, None, None, None] * entered[1][:, None]
    )
    norm_states = (
        jnp.einsum("bcd,bdhf->bchf", earlier_mask, block_totals, precision=highest)
        + keep_mask[:, :, None, None] * entered[2][:, None]
    )
    query_float = query_feat.astype(jnp.float32)
    numer = numer + uses_state[..., None, None] * jnp.einsum(
        "bnihf,bnhfe->bnihe", query_float, states, precision=highest
    )
    denom = denom + uses_state[..., None] * jnp.einsum(
        "bnihf,bnhf->bnih", query_float, norm_states, precision=highest
    )
    mixture = numer / denom[..., None]
    return (mixture, denom, scores, masked_keys, states, norm_states)


def mixer_backward(query_feat, key_feat, value_part, tables, saved, mixture_grad):
    pair_mask, included, uses_state, earlier_mask, later_mask, keep_mask, end_mask, reset_flag = (
        tables
    )
    mixture, denom, scores, masked_keys, states, norm_states = saved
    num_grad = (mixture_grad / denom[..., None]).astype(jnp.bfloat16)
    den_grad = -jnp.sum(mixture_grad * mixture, axis=-1) / denom
    score_grad = jnp.einsum(
        "bnihe,bnjhe->bnhij", num_grad, value_part, preferred_element_type=jnp.float32
    )
    score_grad = score_grad + jnp.transpose(den_grad, (0, 1, 3, 2))[..., None]
    score_grad = jnp.where(pair_mask[:, :, None], score_grad, 0.0).astype(jnp.bfloat16)
    value_grad = jnp.einsum(
        "bnhij,bnihe->bnjhe", scores, num_grad, preferred_element_type=jnp.float32
    )
    qfeat_grad = jnp.einsum(
        "bnhij,bnjhf->bnihf", score_grad, key_feat, preferred_element_type=jnp.float32
    )
    kfeat_grad = jnp.einsum(
        "bnhij,bnihf->bnjhf", score_grad, query_feat, preferred_element_type=jnp.float32
    )
    used_query = query_feat * uses_state[..., None, None].astype(jnp.bfloat16)
    state_grads = jnp.einsum(
        "bnihf,bnihe->bnhfe", used_query, num_grad, preferred_element_type=jnp.float32
    )
    norm_grads = jnp.einsum(
        "bnihf,bnih->bnhf", used_query.astype(jnp.float32), den_grad, precision=highest
    )
    num_float = num_grad.astype(jnp.float32)
    qfeat_grad = qfeat_grad + uses_state[..., None, None] * (
        jnp.einsum("bnihe,bnhfe->bnihf", num_float, states, precision=highest)
        + den_grad[..., None] * norm_states[:, :, None]
    )
    device_sum = jnp.einsum("bc,bchfe->bhfe", keep_mask, state_grads, precision=highest)
    device_total = jnp.einsum("bc,bchf->bhf", keep_mask, norm_grads, precision=highest)
    identity = (
        jnp.zeros_like(reset_flag),
        jnp.zeros_like(device_sum),
        jnp.zeros_like(device_total),
    )
    later = entering((reset_flag, device_sum, device_total), "seq", chain, identity, True)
    block_grad = (
        jnp.einsum("bcd,bdhfe->bchfe", later_mask, state_grads, precision=highest)
        + end_mask[:, :, None, None, None] * later[1][:, None]
    )
    total_grad = (
        jnp.einsum("bcd,bdhf->bchf", later_mask, norm_grads, precision=highest)
        + end_mask[:, :, None, None] * later[2][:, None]
    )
    kfeat_grad = kfeat_grad + included[..., None, None] * (
        jnp.einsum(
            "bnjhe,bnhfe->bnjhf", value_part.astype(jnp.float32), block_grad, precision=highest
        )
        + total_grad[:, :, None]
    )
    value_grad = value_grad + jnp.einsum(
        "bnjhf,bnhfe->bnjhe", masked_keys.astype(jnp.float32), block_grad, precision=highest
    )
    return (qfeat_grad, kfeat_grad, value_grad)


def norm_back(partial_value, normed, inv_std, gain):
    full_width = gain.shape[0]
    local_width = full_width // lax.axis_size("head")
    head_index = lax.axis_index("head")
    summed = lax.psum(partial_value, "head")
    scaled = summed * gain.astype(jnp.float32)
    normed_grad = inv_std * (
        scaled
        - jnp.mean(scaled, axis=-1, keepdims=True)
        - normed * jnp.mean(scaled * normed, axis=-1, keepdims=True)
    )
    gain_grad = jnp.sum(summed * normed, axis=(0, 1))
    shift_grad = jnp.sum(summed, axis=(0, 1))
    result = (
        lax.dynamic_slice_in_dim(normed_grad, head_index * local_width, local_width, 2),
        lax.dynamic_slice_in_dim(gain_grad, head_index * local_width, local_width, 0),
        lax.dynamic_slice_in_dim(shift_grad, head_index * local_width, local_width, 0),
    )
    return result


def local(
    tokens,
    attn_gain,
    attn_shift,
    qkv_weight,
    qkv_bias,
    query_map,
    key_map,
    out_weight,
    out_bias,
    mlp_gain,
    mlp_shift,
    up_weight,
    up_bias,
    down_weight,
    down_bias,
    positions,
    out_grad,
):
    seq_count, length, local_width = tokens.shape
    head_count = query_map.shape[0]
    head_size = query_map.shape[1]
    nblock = length // BLOCK
    tables = block_tables(positions)
    tokens_full = widen(tokens)
    first_normed, first_std = norm_rows(tokens_full.astype(jnp.float32))
    first_hidden = (first_normed * attn_gain + attn_shift).astype(jnp.bfloat16)
    projected = (
        jnp.einsum("bld,dc->blc", first_hidden, qkv_weight, preferred_element_type=jnp.float32)
        + qkv_bias
    )
    projected = projected.reshape(seq_count, nblock, BLOCK, head_count, 3, head_size).astype(
        jnp.bfloat16
    )
    query_part = projected[..., 0, :]
    key_part = projected[..., 1, :]
    value_part = projected[..., 2, :]
    query_logit = jnp.einsum(
        "bnihe,hef->bnihf", query_part, query_map, preferred_element_type=jnp.float32
    )
    key_logit = jnp.einsum(
        "bnihe,hef->bnihf", key_part, key_map, preferred_element_type=jnp.float32
    )
    query_feat = feature_maps(query_logit).astype(jnp.bfloat16)
    key_feat = feature_maps(key_logit).astype(jnp.bfloat16)
    saved = mixer_forward(query_feat, key_feat, value_part, tables)
    mixture_low = saved[0].astype(jnp.bfloat16).reshape(seq_count, length, head_count * head_size)
    attn_out = (
        narrow(
            jnp.einsum("blo,od->bld", mixture_low, out_weight, preferred_element_type=jnp.float32)
        )
        + out_bias
    )
    residual = tokens.astype(jnp.float32) + attn_out
    midfull = widen(residual.astype(jnp.bfloat16))
    second_normed, second_std = norm_rows(midfull.astype(jnp.float32))
    second_hidden = (second_normed * mlp_gain + mlp_shift).astype(jnp.bfloat16)
    up_pre = (
        jnp.einsum("bld,df->blf", second_hidden, up_weight, preferred_element_type=jnp.float32)
        + up_bias
    )
    gelu_value, gelu_slope = gelu_pair(up_pre)
    activated = gelu_value.astype(jnp.bfloat16)
    mlp_out = (
        narrow(
            jnp.einsum("blf,fd->bld", activated, down_weight, preferred_element_type=jnp.float32)
        )
        + down_bias
    )
    block_out = (residual + mlp_out).astype(jnp.bfloat16)
    grad_full = widen(out_grad)
    downweight_grad = jnp.einsum(
        "blf,bld->fd", activated, grad_full, preferred_element_type=jnp.float32
    )
    downbias_grad = jnp.sum(out_grad.astype(jnp.float32), axis=(0, 1))
    up_grad = (
        jnp.einsum("bld,fd->blf", grad_full, down_weight, preferred_element_type=jnp.float32)
        * gelu_slope
    ).astype(jnp.bfloat16)
    upbias_grad = jnp.sum(up_grad.astype(jnp.float32), axis=(0, 1))
    upweight_grad = jnp.einsum(
        "bld,blf->df", second_hidden, up_grad, preferred_element_type=jnp.float32
    )
    second_grad = jnp.einsum("blf,df->bld", up_grad, up_weight, preferred_element_type=jnp.float32)
    residual_part, mlpgain_grad, mlpshift_grad = norm_back(
        second_grad, second_normed, second_std, mlp_gain
    )
    mlp_grads = (
        mlpgain_grad,
        mlpshift_grad,
        upweight_grad,
        upbias_grad,
        downweight_grad,
        downbias_grad,
    )
    residual_grad = out_grad.astype(jnp.float32) + residual_part
    attn_grad = residual_grad.astype(jnp.bfloat16)
    outbias_grad = jnp.sum(attn_grad.astype(jnp.float32), axis=(0, 1))
    attn_full = widen(attn_grad)
    outweight_grad = jnp.einsum(
        "blo,bld->od", mixture_low, attn_full, preferred_element_type=jnp.float32
    )
    mixture_grad = jnp.einsum(
        "bld,od->blo", attn_full, out_weight, preferred_element_type=jnp.float32
    )
    mixture_grad = mixture_grad.reshape(seq_count, nblock, BLOCK, head_count, head_size)
    qfeat_grad, kfeat_grad, value_grad = mixer_backward(
        query_feat, key_feat, value_part, tables, saved, mixture_grad
    )
    qlogit_grad = feature_back(query_logit, qfeat_grad).astype(jnp.bfloat16)
    klogit_grad = feature_back(key_logit, kfeat_grad).astype(jnp.bfloat16)
    querymap_grad = jnp.einsum(
        "bnihe,bnihf->hef", query_part, qlogit_grad, preferred_element_type=jnp.float32
    )
    keymap_grad = jnp.einsum(
        "bnihe,bnihf->hef", key_part, klogit_grad, preferred_element_type=jnp.float32
    )
    query_back = jnp.einsum(
        "bnihf,hef->bnihe", qlogit_grad, query_map, preferred_element_type=jnp.float32
    ).astype(jnp.bfloat16)
    key_back = jnp.einsum(
        "bnihf,hef->bnihe", klogit_grad, key_map, preferred_element_type=jnp.float32
    ).astype(jnp.bfloat16)
    projected_grad = jnp.stack([query_back, key_back, value_grad.astype(jnp.bfloat16)], axis=4)
    projected_grad = projected_grad.reshape(seq_count, length, 3 * head_count * head_size)
    qkvbias_grad = jnp.sum(projected_grad.astype(jnp.float32), axis=(0, 1))
    qkvweight_grad = jnp.einsum(
        "bld,blc->dc", first_hidden, projected_grad, preferred_element_type=jnp.float32
    )
    first_grad = jnp.einsum(
        "blc,dc->bld", projected_grad, qkv_weight, preferred_element_type=jnp.float32
    )
    tokens_part, attngain_grad, attnshift_grad = norm_back(
        first_grad, first_normed, first_std, attn_gain
    )
    tokens_grad = (residual_grad + tokens_part).astype(jnp.bfloat16)
    summed = lax.psum(
        (
            attngain_grad,
            attnshift_grad,
            qkvweight_grad,
            qkvbias_grad,
            querymap_grad,
            keymap_grad,
            outweight_grad,
            outbias_grad,
            mlp_grads[0],
            mlp_grads[1],
            mlp_grads[2],
            mlp_grads[3],
            mlp_grads[4],
            mlp_grads[5],
        ),
        ("seq", "dp"),
    )
    return (
        block_out,
        tokens_grad,
        summed[0],
        summed[1],
        summed[2],
        summed[3],
        summed[4],
        summed[5],
        summed[6],
        summed[7],
        summed[8],
        summed[9],
        summed[10],
        summed[11],
        summed[12],
        summed[13],
    )


def solution(mesh):
    return jax.shard_map(
        local,
        mesh=mesh,
        in_specs=(
            P("dp", "seq", "head"),
            P(),
            P(),
            P(None, "head"),
            P("head"),
            P("head", None, None),
            P("head", None, None),
            P("head", None),
            P("head"),
            P(),
            P(),
            P(None, "head"),
            P("head"),
            P("head", None),
            P("head"),
            P("dp", "seq"),
            P("dp", "seq", "head"),
        ),
        out_specs=(
            P("dp", "seq", "head"),
            P("dp", "seq", "head"),
            P("head"),
            P("head"),
            P(None, "head"),
            P("head"),
            P("head", None, None),
            P("head", None, None),
            P("head", None),
            P("head"),
            P("head"),
            P("head"),
            P(None, "head"),
            P("head"),
            P("head", None),
            P("head"),
        ),
        check_vma=False,
    )
```

profile of v0, /device:TPU:0, one launch (start us, length us, event | category | flops | bytes accessed | tf_op | source)
XLA Modules:
  0.0 1202.4 jit_solution(11086940653539757207)
XLA Ops:
  12.3 3.1 all-reduce
  22.9 33.7 %all-gather.11.cloned.1.call-done = bf16[1,2048,768]{1,2,0:T(8,128)(2,1)} async-done(((bf16[1,2048,192]{1,2,0:T(8,128)(2,1)}), bf16[1,2048,768]{1,2,0:T(8,128)(2,1)}) %all-gather.11.cloned.1.call-update) | async-done | bytes 3145744 | tf_op jit(solution)/shard_map/all_gather | solution.py:31
  56.6 4.7 copy.288
  61.3 2.5 convert_reduce_fusion.2
  65.8 2.7 add_convert_fusion.2
  68.5 6.0 convert_element_type.324
  74.5 5.8 slice_bitcast_fusion.1
  82.7 3.8 copy.392
  88.4 3.7 fusion.54
  92.8 3.9 fusion.89
  98.6 3.9 fusion.52
  102.5 3.9 convert_bitcast_fusion.1
  107.8 3.4 broadcast_multiply_fusion.2
  114.0 3.5 fusion.43
  122.6 5.5 multiply_add_fusion.2
  128.4 4.7 fusion.33
  133.1 2.5 fusion.107
  137.1 3.2 fusion.181
  142.6 4.7 convolution_bitcast_fusion.1
  147.3 15.9 %copy.306 = f32[1,2048,768]{1,0,2:T(1,128)} copy(f32[1,2048,768]{2,1,0:T(8,128)} %convolution_bitcast_fusion.1) | data formatting | bytes 12582912 | tf_op jit(solution)/shard_map/blo,od->bld/dot_general | solution.py:293
  165.1 138.7 %all-reduce.14.cloned.1.call-done = f32[1,2048,768]{1,0,2:T(1,128)} async-done(((f32[1,2048,768]{1,0,2:T(1,128)}), f32[1,2048,768]{1,0,2:T(1,128)}) %all-reduce.14.cloned.1.call-update) | async-done | bytes 6291472
  309.9 43.4 %all-gather.13.cloned.1.call-done = bf16[1,2048,768]{1,2,0:T(8,128)(2,1)} async-done(((bf16[1,2048,192]{1,2,0:T(8,128)(2,1)}), bf16[1,2048,768]{1,2,0:T(8,128)(2,1)}) %all-gather.13.cloned.1.call-update) | async-done | bytes 3145744 | tf_op jit(solution)/shard_map/all_gather | solution.py:31
  353.3 4.7 copy.308
  358.0 2.5 convert_reduce_fusion.1
  361.9 5.1 fusion.119
  367.0 32.0 %all-gather.15.cloned.1.call-done = bf16[1,2048,768]{1,2,0:T(8,128)(2,1)} async-done(((bf16[1,2048,192]{1,2,0:T(8,128)(2,1)}), bf16[1,2048,768]{1,2,0:T(8,128)(2,1)}) %all-gather.15.cloned.1.call-update) | async-done | bytes 3145744 | tf_op jit(solution)/shard_map/all_gather | solution.py:31
  399.0 10.7 convert_reduce_fusion.3
  411.4 4.5 convolution_bitcast_fusion.2
  417.4 137.1 %all-reduce.12.cloned.1.call-done = f32[1,2048,768]{2,1,0:T(8,128)} async-done(((f32[1,2048,768]{2,1,0:T(8,128)}), f32[1,2048,768]{2,1,0:T(8,128)}) %all-reduce.12.cloned.1.call-update) | async-done | bytes 6291472 | tf_op jit(solution)/shard_map/psum | solution.py:227
  554.5 6.6 fusion.172
  561.1 3.9 convert_reduce_fusion.7
  567.7 9.4 convolution_bitcast_fusion.3
  577.1 15.9 %copy.309 = f32[1,2048,768]{1,0,2:T(1,128)} copy(f32[1,2048,768]{2,1,0:T(8,128)} %convolution_bitcast_fusion.3) | data formatting | bytes 12582912 | tf_op jit(solution)/shard_map/blf,fd->bld/dot_general | solution.py:309
  593.0 18.3 %all-gather.17.cloned.1.call-done = bf16[1,2048,768]{1,2,0:T(8,128)(2,1)} async-done(((bf16[1,2048,192]{1,2,0:T(8,128)(2,1)}), bf16[1,2048,768]{1,2,0:T(8,128)(2,1)}) %all-gather.17.cloned.1.call-update) | async-done | bytes 3145744 | tf_op jit(solution)/shard_map/all_gather | solution.py:31
  611.3 2.7 fusion.24
  618.9 5.1 fusion.32
  624.1 3.9 copy.313
  628.0 2.5 divide_convert_fusion
  636.1 5.5 fusion.16
  641.7 6.7 multiply_reduce_fusion.7
  648.4 6.8 fusion.71
  661.8 2.9 fusion.39
  669.2 5.7 multiply_add_fusion.1
  674.9 4.5 fusion.35
  679.6 5.5 fusion.19
  685.1 6.7 multiply_reduce_fusion.5
  691.8 6.7 fusion.72
  702.4 3.0 convert_reduce_fusion
  705.5 7.3 copy.338
  712.8 7.7 reshape.1128
  720.6 7.0 convolution_bitcast_fusion
  728.3 7.5 fusion.117
  735.8 8.9 fusion.26
  747.1 3.6 fusion.121
  754.6 3.2 fusion.110
  757.8 2.9 fusion.113
  760.7 207.3 %all-reduce.20.cloned.1.call-done = (f32[1,2048,768]{1,0,2:T(1,128)}, f32[1,2048,768]{2,1,0:T(8,128)}) async-done(((f32[1,2048,768]{1,0,2:T(1,128)}, f32[1,2048,768]{2,1,0:T(8,128)}), (f32[1,2048,768]{1,0,2:T(1,128)}, f32[1,2048,768]{2,1,0:T(8,128)})) %all-reduce.20.cloned.1.call-update) | async-done | bytes 12582928
  968.0 8.4 fusion.173
  977.7 2.5 constant_dynamic-slice_fusion.4
  980.3 2.6 fusion.84
  982.9 4.0 fusion.60
  988.1 135.7 %all-reduce.18.cloned.1.call-done = (f32[768,576]{0,1:T(8,128)}, f32[192,768]{1,0:T(8,128)}, f32[768,768]{1,0:T(8,128)}, f32[768,768]{1,0:T(8,128)}) async-done(((f32[768,576]{0,1:T(8,128)}, f32[192,768]{1,0:T(8,128)}, f32[768,768]{1,0:T(8,128)}, f32[768,768]{1,0:T(8,128)}), (f32[768,576]{0,1:T(8,128)}, f32[192,768]{1,0:T(8,128)}, f32[768,768]{1,0:T(8,128)}, ...) | async-done | bytes 7077904 | tf_op jit(solution)/shard_map/psum | solution.py:380
  1123.8 58.1 %all-reduce.16.cloned.1.call-done = (f32[192]{0:T(256)}, f32[192]{0:T(256)}, f32[576]{0:T(1024)}, f32[3,64,64]{2,1,0:T(8,128)}, f32[3,64,64]{2,1,0:T(8,128)}, /*...) async-done(((f32[192]{0:T(256)}, f32[192]{0:T(256)}, f32[576]{0:T(1024)}, f32[3,64,64]{2,1,0:T(8,128)}, f32[3,64,64]{2,1,0:T(8,128)}, ...) | async-done | bytes 108304 | tf_op jit(solution)/shard_map/psum | solution.py:380
  1184.4 2.8 copy.532
  (378 shorter events, 95.9 us)
Async XLA Ops:
  7.2 391.8 %copy-start = (bf16[768,768]{1,0:T(8,128)(2,1)S(1)}, bf16[768,768]{1,0:T(8,128)(2,1)}, u32[]{:S(2)}) copy-start(bf16[768,768]{1,0:T(8,128)(2,1)} %param.34) | copy-start | bytes 3538948
  7.2 49.4 %all-gather.11.cloned.1.call-start = ((), (), s32[]{:S(2)}) async-start(), calls=%async_computation | async-start | bytes 3932160 | tf_op jit(solution)/shard_map/all_gather | solution.py:31
  7.9 295.9 %all-reduce.14.cloned.1.call-start = ((), (), s32[]{:S(2)}) async-start(), calls=%async_computation.5 | async-start | bytes 12582912
  9.2 52.1 %copy-start.87 = (f32[1,32]{1,0:T(1,128)}, f32[1,32]{1,0:T(1,128)S(1)}, u32[]{:S(2)}) copy-start(f32[1,32]{1,0:T(1,128)S(1)} %reduce_window_sum.13) | copy-start | bytes 388
  80.2 6.3 copy-start.68
  82.7 5.7 copy-start.13
  88.4 8.3 copy-start.2
  98.6 7.9 copy-start.4
  98.6 7.9 copy-start.46
  98.6 7.9 copy-start.48
  111.2 24.5 %copy-start.22 = (bf16[32,64,3,128]{3,1,0,2:T(8,128)(2,1)}, bf16[32,64,3,128]{3,1,0,2:T(8,128)(2,1)S(1)}, u32[]{:S(2)}) copy-start(bf16[32,64,3,128]{3,1,0,2:T(8,128)(2,1)S(1)} %get-tuple-element.401) | copy-start | bytes 4718596
  114.0 8.1 copy-start.123
  128.1 5.0 copy-start.11
  128.4 4.7 copy-start.84
  128.4 7.3 copy-start.30
  128.4 7.3 copy-start.62
  163.2 144.3 %copy-start.27 = (bf16[1,2048,192]{1,2,0:T(8,128)(2,1)S(1)}, bf16[1,2048,192]{1,2,0:T(8,128)(2,1)}, u32[]{:S(2)}) copy-start(bf16[1,2048,192]{1,2,0:T(8,128)(2,1)} %param.21) | copy-start | bytes 2359300
  163.3 190.1 %all-gather.13.cloned.1.call-start = ((), (), s32[]{:S(2)}) async-start(), calls=%async_computation.1 | async-start | bytes 3932160 | tf_op jit(solution)/shard_map/all_gather | solution.py:31
  163.9 145.3 %copy-start.104 = (f32[192]{0:T(256)}, f32[192]{0:T(256)S(1)}, u32[]{:S(2)}) copy-start(f32[192]{0:T(256)S(1)} %convert_element_type.337) | copy-start | bytes 2308
  309.2 89.8 %all-gather.15.cloned.1.call-start = ((), (), s32[]{:S(2)}) async-start(), calls=%async_computation.2 | async-start | bytes 3932160 | tf_op jit(solution)/shard_map/all_gather | solution.py:31
  309.8 244.8 %all-reduce.12.cloned.1.call-start = ((), (), s32[]{:S(2)}) async-start(), calls=%async_computation.3 | async-start | bytes 12582912 | tf_op jit(solution)/shard_map/psum | solution.py:227
  309.8 244.7 %copy-start.92 = (f32[768]{0:T(1024)}, f32[768]{0:T(1024)S(1)}, u32[]{:S(2)}) copy-start(f32[768]{0:T(1024)S(1)} %convert_element_type.340) | copy-start | bytes 9220
  309.9 52.0 %copy-start.99 = (f32[768]{0:T(1024)}, f32[768]{0:T(1024)S(1)}, u32[]{:S(2)}) copy-start(f32[768]{0:T(1024)S(1)} %convert_element_type.341) | copy-start | bytes 9220
  309.9 257.8 %copy-start.97 = (f32[768]{0:T(1024)}, f32[768]{0:T(1024)S(1)}, u32[]{:S(2)}) copy-start(f32[768]{0:T(1024)S(1)} %convert_element_type.343) | copy-start | bytes 9220
  360.8 193.7 %copy-start.78 = (f32[2048]{0:T(1024)}, f32[2048]{0:T(1024)S(1)}, u32[]{:S(2)}) copy-start(f32[2048]{0:T(1024)S(1)} %broadcast_multiply_fusion.8) | copy-start | bytes 24580
  361.9 199.2 %copy-start.81 = (f32[2048]{0:T(1024)}, f32[2048]{0:T(1024)S(1)}, u32[]{:S(2)}) copy-start(f32[2048]{0:T(1024)S(1)} %add_rsqrt_fusion) | copy-start | bytes 24580
  399.0 12.4 %copy-start.118 = (bf16[768,768]{1,0:T(8,128)(2,1)S(1)}, bf16[768,768]{1,0:T(8,128)(2,1)}, u32[]{:S(2)}) copy-start(bf16[768,768]{1,0:T(8,128)(2,1)} %param.32) | copy-start | bytes 3538948
  415.9 195.4 %all-gather.17.cloned.1.call-start = ((), (), s32[]{:S(2)}) async-start(), calls=%async_computation.4 | async-start | bytes 3932160 | tf_op jit(solution)/shard_map/all_gather | solution.py:31
  567.2 400.8 %all-reduce.20.cloned.1.call-start = ((), (), s32[]{:S(2)}) async-start(), calls=%async_computation.8 | async-start | bytes 25165824
  577.1 34.2 %copy-start.50 = (bf16[192,768]{1,0:T(8,128)(2,1)S(1)}, bf16[192,768]{1,0:T(8,128)(2,1)}, u32[]{:S(2)}) copy-start(bf16[192,768]{1,0:T(8,128)(2,1)} %param.28) | copy-start | bytes 884740
  618.9 5.1 copy-start.65
  618.9 5.1 copy-start.71
  636.1 5.6 copy-start.5
  636.1 5.6 copy-start.47
  636.1 5.6 copy-start.49
  636.1 5.6 copy-start.56
  636.1 5.6 copy-start.58
  648.4 6.9 copy-start.67
  658.5 8.1 copy-start.124
  669.2 5.7 copy-start.21
  679.5 5.5 copy-start.3
  679.5 5.5 copy-start.43
  679.5 5.5 copy-start.45
  679.5 5.5 copy-start.52
  679.5 5.5 copy-start.54
  691.8 7.8 copy-start.69
  712.8 7.7 copy-start.120
  727.6 8.1 copy-start.98
  727.6 396.2 %all-reduce.18.cloned.1.call-start = ((), (), s32[]{:S(2)}) async-start(), calls=%async_computation.7 | async-start | bytes 14155776 | tf_op jit(solution)/shard_map/psum | solution.py:380
  728.3 7.5 copy-start.116
  735.8 8.9 copy-start.24
  735.8 11.0 copy-start.37
  750.7 7.1 copy-start.14
  750.7 431.2 %all-reduce.16.cloned.1.call-start = ((), (), s32[]{:S(2)}) async-start(), calls=%async_computation.6 | async-start | bytes 421888 | tf_op jit(solution)/shard_map/psum | solution.py:380
  1123.8 65.3 %copy-start.59 = (f32[192,768]{1,0:T(8,128)S(1)}, f32[192,768]{1,0:T(8,128)}, u32[]{:S(2)}) copy-start(f32[192,768]{1,0:T(8,128)} %get-tuple-element.599) | copy-start | bytes 1769476
  1123.8 67.9 %copy-start.39 = (f32[768,768]{1,0:T(8,128)S(1)}, f32[768,768]{1,0:T(8,128)}, u32[]{:S(2)}) copy-start(f32[768,768]{1,0:T(8,128)} %get-tuple-element.603) | copy-start | bytes 7077892
  1181.9 5.3 copy-start.103
  1181.9 5.9 copy-start.73
  1181.9 6.6 copy-start.72
  1181.9 8.0 copy-start.115
  1181.9 8.6 copy-start.114
  1181.9 9.2 copy-start.113
  1187.8 5.2 copy-start.102
  1187.8 5.8 copy-start.38
  (72 other events, 183.9 us)
Sparse Core Ops, SparseCore 0:
  9.9 46.6 all-gather.10
  163.4 140.4 all-reduce.13
  309.3 43.9 all-gather.12
  355.0 43.9 all-gather.14
  416.0 138.4 all-reduce.11
  567.4 43.9 all-gather.16
  727.7 240.2 all-reduce.19
  971.8 151.9 all-reduce.17
  1128.1 53.7 all-reduce.15
where the time goes:
time: 1210 us; the launch traced here: 1200 us
  waiting for transfers between devices  806 us (67%)
  matrix products  135 us (11%)
  local copies, waits for them, and re-layouts  131 us (11%)
  other arithmetic  102 us (8%)
  between operations  16.9 us (1%)
    unnamed x11, waiting for transfers between devices  347 us
    psum x2, waiting for transfers between devices, local(): lax.psum((attngain_grad, attnshift_grad, qkvweight_grad, qkvbias_grad, qu...  194 us
    psum x1, waiting for transfers between devices, norm_back(): summed = lax.psum(partial_value, 'head')  137 us
    all_gather x4, waiting for transfers between devices, widen(): return lax.all_gather(part, 'head', axis=2, tiled=True)  127 us
    unnamed x279, local copies, waits for them, and re-layouts  43.9 us
  transfers between devices with their start and end apart: 9, of which 9 were waited for; matrix products, arithmetic and copies ran while one was open for 9% of the time, Pallas kernels for 0%

commit v1 on v0

v1 whole, which is shorter than its diff:
```python
import functools

import jax
import jax.numpy as jnp
from jax import lax
from jax.experimental import pallas as pl
from jax.experimental.pallas import tpu as pltpu
from jax.sharding import PartitionSpec as P

eps = 1e-05
gelu_scale = 0.7978845608028654
bf = jnp.bfloat16
f32 = jnp.float32
AUG = 80


def nn(a, b):
    return lax.dot_general(a, b, (((1,), (0,)), ((), ())), preferred_element_type=f32)


def nt(a, b):
    return lax.dot_general(a, b, (((1,), (1,)), ((), ())), preferred_element_type=f32)


def tn(a, b):
    return lax.dot_general(a, b, (((0,), (0,)), ((), ())), preferred_element_type=f32)


def run_kernel(body, name, outs, scalars, *ins, flops=0, trans=0):
    moved = sum(a.size * a.dtype.itemsize for a in ins)
    moved += sum(o.size * jnp.dtype(o.dtype).itemsize for o in outs)
    return pl.pallas_call(
        body,
        out_shape=outs,
        in_specs=[pl.BlockSpec(memory_space=pltpu.SMEM)]
        + [pl.BlockSpec(memory_space=pltpu.VMEM)] * len(ins),
        out_specs=[pl.BlockSpec(memory_space=pltpu.VMEM)] * len(outs),
        compiler_params=pltpu.CompilerParams(vmem_limit_bytes=48 * 2**20),
        cost_estimate=pl.CostEstimate(flops=flops, bytes_accessed=moved, transcendentals=trans),
        name=name,
    )(scalars, *ins)


def half_rows(ref, half, size):
    return ref[pl.ds(pl.multiple_of(half * size, size), size), :]


def norm_columns(values):
    center = values - jnp.mean(values, axis=0, keepdims=True)
    inv_std = lax.rsqrt(jnp.mean(center * center, axis=0, keepdims=True) + eps)
    return center * inv_std, inv_std


def norm_columns_back(grad, normed, inv_std, gain):
    scaled = grad * gain
    return inv_std * (
        scaled
        - jnp.mean(scaled, axis=0, keepdims=True)
        - normed * jnp.mean(scaled * normed, axis=0, keepdims=True)
    )


def gelu_pair(up_pre):
    square = up_pre * up_pre
    tanh_value = jnp.tanh(gelu_scale * (up_pre + 0.044715 * square * up_pre))
    half_one = 0.5 * (1.0 + tanh_value)
    slope = half_one + 0.5 * up_pre * (1.0 - tanh_value * tanh_value) * gelu_scale * (
        1.0 + 3.0 * 0.044715 * square
    )
    return up_pre * half_one, slope


def soft_columns(logits):
    top = jnp.exp(logits - jnp.max(logits, axis=0, keepdims=True))
    return top / jnp.sum(top, axis=0, keepdims=True)


def ahead_mask(starts, rows, first_column, columns):
    j = lax.broadcasted_iota(jnp.int32, (rows, columns), 0)
    i = lax.broadcasted_iota(jnp.int32, (rows, columns), 1) + first_column
    return (j <= i) & (j >= starts[0:1, first_column : first_column + columns])


def first_norm_body(sc, x_ref, col_ref, hid_ref):
    normed, _ = norm_columns(x_ref[...].astype(f32))
    hid_ref[...] = (normed * col_ref[:, 0:1] + col_ref[:, 1:2]).astype(bf)


def turn_body(sc, a_ref, o_ref):
    o_ref[...] = a_ref[...].T


def project_body(hp, hs, sc, hid_ref, wm_ref, wt_ref, bias_ref, maps_ref, starts_ref,
                 proj_ref, qf_ref, kf_ref, va_ref, st_ref):
    s = sc[0]
    half = wm_ref.shape[1]
    proj = nn(wm_ref[...], half_rows(hid_ref, s, half)) + nn(wt_ref[...], half_rows(hid_ref, 1 - s, half))
    proj_ref[...] = (proj + bias_ref[...]).astype(bf)
    tokens = hid_ref.shape[1]
    starts = starts_ref[0:1, :]
    included = (starts == sc[1]).astype(f32)
    for i in range(hp):
        row = 3 * hs * i
        for part, out in ((0, qf_ref), (1, kf_ref)):
            own_map = maps_ref[(part * hp + i) * hs : (part * hp + i + 1) * hs, :]
            logits = tn(own_map, proj_ref[row + part * hs : row + (part + 1) * hs, :])
            out[i, 0:hs, :] = soft_columns(logits).astype(bf)
            out[i, hs : 2 * hs, :] = soft_columns(-logits).astype(bf)
        va_ref[i, 0:hs, :] = proj_ref[row + 2 * hs : row + 3 * hs, :]
        extra = lax.broadcasted_iota(jnp.int32, (AUG - hs, tokens), 0)
        va_ref[i, hs:AUG, :] = jnp.where(extra < 2, 1.0, 0.0).astype(bf)
        kept = (va_ref[i].astype(f32) * included).astype(bf)
        st_ref[i] = nt(kept, kf_ref[i]).astype(bf)


def causal_pieces(tokens):
    step = tokens // 2
    return ((0, step, step), (step, step, tokens))


def local_mix_body(hp, sc, qf_ref, kf_ref, va_ref, starts_ref, num_ref):
    tokens = qf_ref.shape[2]
    starts = starts_ref[...]
    for first, width, rows in causal_pieces(tokens):
        mask = ahead_mask(starts, rows, first, width)
        for i in range(hp):
            scores = tn(kf_ref[i, :, 0:rows], qf_ref[i, :, first : first + width])
            scores = jnp.where(mask, scores, 0.0).astype(bf)
            num_ref[i, :, first : first + width] = nn(va_ref[i, :, 0:rows], scores)


def weighted_states(sc, slots, own, refs, last, hp, piece, i):
    total = jnp.where(sc[last] > 0, refs[-1][piece * hp + i].astype(f32), 0.0)
    for m, (slot, ref) in enumerate(zip(slots, refs[:-1]), 1):
        total += jnp.where(sc[slot] > 0, ref[(piece ^ m) * hp + i].astype(f32), 0.0)
    return total.astype(bf)


def mix_out_body(hp, hs, nh, sc, *refs):
    num_refs, qf_refs, state_refs = refs[0:nh], refs[nh : 2 * nh], refs[2 * nh : 3 * nh]
    wm_refs, wt_refs = refs[3 * nh : 4 * nh], refs[4 * nh : 5 * nh]
    starts_ref, x_ref, col_ref, sin_ref, mixd_ref, mix_ref, res_ref, hidt_ref, hid_ref = refs[5 * nh :]
    s = sc[0]
    uses = starts_ref[0:1, :] < 0
    rows = hp * hs
    for j in range(nh):
        for i in range(hp):
            state = weighted_states(sc, range(2, 1 + nh), None, state_refs, 1 + nh, hp, j, i)
            sin_ref[j * hp + i] = state
            num = num_refs[j][i] + jnp.where(uses, nn(state, qf_refs[j][i]), 0.0)
            denom = num[hs : hs + 1, :]
            mixture = num[0:hs, :] / denom
            mixd_ref[j * hp + i, 0:hs, :] = mixture
            mixd_ref[j * hp + i, hs : hs + 8, :] = num[hs : hs + 8, :]
            mix_ref[j * rows + i * hs : j * rows + (i + 1) * hs, :] = mixture.astype(bf)
    half = wm_refs[0].shape[1]
    for which, w_refs in ((s, wm_refs), (1 - s, wt_refs)):
        out = tn(w_refs[0][...], mix_ref[0:rows, :])
        for j in range(1, nh):
            out += tn(w_refs[j][...], mix_ref[j * rows : (j + 1) * rows, :])
        at = pl.ds(pl.multiple_of(which * half, half), half)
        res_ref[at, :] = x_ref[at, :].astype(f32) + out + col_ref[at, 4:5]
    normed, _ = norm_columns(res_ref[...].astype(bf).astype(f32))
    hidden = (normed * col_ref[:, 2:3] + col_ref[:, 3:4]).astype(bf)
    hidt_ref[...] = hidden
    hid_ref[...] = hidden.T


def feed_body(first, sc, hid_ref, gy_ref, bm_ref, bt_ref, bias_ref, *refs):
    if first:
        out_ref, sg_ref = refs[0:2]
        rest = refs[2:]
    else:
        out_in, sg_in, out_ref, sg_ref = refs[0:4]
        rest = refs[4:]
    ub_ref = rest[-1]
    s = sc[0]
    half = bm_ref.shape[1] // 2
    out_total, sg_total = None, None
    for b, (which, blk) in enumerate(((s, bm_ref), (1 - s, bt_ref))):
        act_ref, ug_ref = rest[2 * b], rest[2 * b + 1]
        at = pl.ds(pl.multiple_of(which * half, half), half)
        up_pre = nn(hid_ref[...], blk[:, 0:half]) + bias_ref[0:1, at]
        value, slope = gelu_pair(up_pre)
        act_ref[...] = value.astype(bf)
        back = nt(gy_ref[:, 0:half], blk[0:half, half:]) + nt(gy_ref[:, half:], blk[half:, half:])
        up_grad = (back * slope).astype(bf)
        ug_ref[...] = up_grad
        ub_ref[0:8, at] = jnp.broadcast_to(jnp.sum(up_grad.astype(f32), axis=0, keepdims=True), (8, half))
        if b == 0 and first:
            out_ref[:, 0:half] = nn(act_ref[...], blk[0:half, half:])
            out_ref[:, half:] = nn(act_ref[...], blk[half:, half:])
            sg_ref[...] = nt(blk[:, 0:half], ug_ref[...])
        else:
            left, grad = (out_in, sg_in) if b == 0 else (out_ref, sg_ref)
            out_ref[:, 0:half] = left[:, 0:half] + nn(act_ref[...], blk[0:half, half:])
            out_ref[:, half:] = left[:, half:] + nn(act_ref[...], blk[half:, half:])
            sg_ref[...] = grad[...] + nt(blk[:, 0:half], ug_ref[...])


def block_out_body(sc, res_ref, out_ref, col_ref, o_ref):
    o_ref[...] = (res_ref[...] + out_ref[...].T + col_ref[:, 5:6]).astype(bf)


def sums_across(values):
    lane = lax.broadcasted_iota(jnp.int32, (values[0].shape[0], 128), 1)
    total = jnp.zeros((values[0].shape[0], 128), f32)
    for at, value in enumerate(values):
        total = jnp.where(lane == at, jnp.sum(value, axis=1, keepdims=True), total)
    return total


def second_back_body(hp, hs, nh, sc, *refs):
    sg_ref, res_ref, gyt_ref, col_ref, mixd_ref, starts_ref = refs[0:6]
    wm_refs, wt_refs, qf_refs = refs[6 : 6 + nh], refs[6 + nh : 6 + 2 * nh], refs[6 + 2 * nh : 6 + 3 * nh]
    rg_ref, ag_ref, vec_ref, na_ref, sgt_ref = refs[6 + 3 * nh :]
    s = sc[0]
    normed, inv_std = norm_columns(res_ref[...].astype(bf).astype(f32))
    sg = sg_ref[...]
    gy = gyt_ref[...].astype(f32)
    res_grad = gy + norm_columns_back(sg, normed, inv_std, col_ref[:, 2:3])
    rg_ref[...] = res_grad
    ag_ref[...] = res_grad.astype(bf)
    vec_ref[...] = sums_across((sg * normed, sg, ag_ref[...].astype(f32), gy))
    half = wm_refs[0].shape[1]
    tokens = sg_ref.shape[1]
    uses = (starts_ref[0:1, :] < 0).astype(f32)
    for j in range(nh):
        mg = nn(wm_refs[j][...], half_rows(ag_ref, s, half)) + nn(wt_refs[j][...], half_rows(ag_ref, 1 - s, half))
        for i in range(hp):
            own = mg[i * hs : (i + 1) * hs, :]
            num = own / mixd_ref[j * hp + i, hs : hs + 1, :]
            den = -jnp.sum(num * mixd_ref[j * hp + i, 0:hs, :], axis=0, keepdims=True)
            high = den.astype(bf).astype(f32)
            extra = lax.broadcasted_iota(jnp.int32, (AUG - hs, tokens), 0)
            extra = jnp.where(extra == 0, high, jnp.where(extra == 1, den - high, 0.0))
            na_ref[j * hp + i, 0:hs, :] = num.astype(bf)
            na_ref[j * hp + i, hs:AUG, :] = extra.astype(bf)
            kept = (na_ref[j * hp + i].astype(f32) * uses).astype(bf)
            grad = nt(kept, qf_refs[j][i])
            sgt_ref[j * hp + i] = grad.astype(bf)


def join_extra(state, hs):
    row = lax.broadcasted_iota(jnp.int32, state.shape, 0)
    both = state[hs : hs + 1, :] + state[hs + 1 : hs + 2, :]
    return jnp.where(row < hs, state, jnp.where(row == hs, both, 0.0))


def halves_back(feat, grad, hs):
    parts = []
    for k in range(2):
        soft = feat[k * hs : (k + 1) * hs, :].astype(f32)
        own = grad[k * hs : (k + 1) * hs, :]
        weight = jnp.sum(soft * own, axis=0, keepdims=True) / jnp.sum(soft, axis=0, keepdims=True)
        parts.append(soft * (own - weight))
    return (parts[0] - parts[1]).astype(bf)


def local_back_body(hp, hs, j, sc, qf_ref, kf_ref, va_ref, na_ref, sin_ref, starts_ref, ql_ref, kfg_ref, vg_ref):
    tokens = qf_ref.shape[2]
    starts = starts_ref[...]
    step = tokens // 2
    uses = starts[0:1, :] < 0
    masks = [ahead_mask(starts, rows, first, width) for first, width, rows in causal_pieces(tokens)]
    for i in range(hp):
        na = na_ref[j * hp + i]
        state = sin_ref[j * hp + i]
        through = tn(state, na)
        for which, (first, width, rows) in enumerate(causal_pieces(tokens)):
            at = slice(first, first + width)
            mask = masks[which]
            scores = jnp.where(mask, tn(kf_ref[i, :, 0:rows], qf_ref[i, :, at]), 0.0).astype(bf)
            sgrad = jnp.where(mask, tn(va_ref[i, :, 0:rows], na[:, at]), 0.0).astype(bf)
            qfg = nn(kf_ref[i, :, 0:rows], sgrad) + jnp.where(uses[:, at], through[:, at], 0.0)
            ql_ref[i, :, at] = halves_back(qf_ref[i, :, at], qfg, hs)
            kfg = nt(qf_ref[i, :, at], sgrad)
            vg = nt(na[:, at], scores)[0:hs, :]
            if which == 0:
                kfg_ref[i, :, 0:rows] = kfg
                vg_ref[i, :, 0:rows] = vg
            else:
                kfg_ref[i, :, 0:step] += kfg[:, 0:step]
                vg_ref[i, :, 0:step] += vg[:, 0:step]
                kfg_ref[i, :, step:] = kfg[:, step:]
                vg_ref[i, :, step:] = vg[:, step:]


def project_back_body(hp, hs, nh, j, first, sc, *refs):
    state_refs = refs[0:nh]
    kf_ref, va_ref, ql_ref, kfg_ref, vg_ref, proj_ref, maps_ref, wm_ref, wt_ref, starts_ref = refs[nh : nh + 10]
    rest = refs[nh + 10 :]
    if first:
        pg_ref, fg_ref, mg_ref, pb_ref = rest
    else:
        fg_in, pg_ref, fg_ref, mg_ref, pb_ref = rest
    s = sc[0]
    included = starts_ref[0:1, :] == sc[1]
    for i in range(hp):
        state = weighted_states(sc, range(2 + nh, 1 + 2 * nh), None, state_refs, 1 + 2 * nh, hp, j, i)
        state = join_extra(state.astype(f32), hs).astype(bf)
        kfg = kfg_ref[i] + jnp.where(included, tn(state, va_ref[i]), 0.0)
        vg = vg_ref[i] + jnp.where(included, nn(state, kf_ref[i])[0:hs, :], 0.0)
        klg = halves_back(kf_ref[i], kfg, hs)
        qlg = ql_ref[i]
        row = 3 * hs * i
        q_map = maps_ref[i * hs : (i + 1) * hs, :]
        k_map = maps_ref[(hp + i) * hs : (hp + i + 1) * hs, :]
        pg_ref[row : row + hs, :] = nn(q_map, qlg).astype(bf)
        pg_ref[row + hs : row + 2 * hs, :] = nn(k_map, klg).astype(bf)
        pg_ref[row + 2 * hs : row + 3 * hs, :] = vg.astype(bf)
        mg_ref[i * hs : (i + 1) * hs, :] = nt(proj_ref[row : row + hs, :], qlg)
        mg_ref[(hp + i) * hs : (hp + i + 1) * hs, :] = nt(proj_ref[row + hs : row + 2 * hs, :], klg)
    pb_ref[...] = sums_across((pg_ref[...].astype(f32),))
    half = wm_ref.shape[1]
    for which, w_ref in ((s, wm_ref), (1 - s, wt_ref)):
        at = pl.ds(pl.multiple_of(which * half, half), half)
        grad = tn(w_ref[...], pg_ref[...])
        fg_ref[at, :] = grad if first else fg_in[at, :] + grad


def first_back_body(sc, fg_ref, x_ref, rg_ref, col_ref, tg_ref, vec_ref):
    normed, inv_std = norm_columns(x_ref[...].astype(f32))
    fg = fg_ref[...]
    tg_ref[...] = (rg_ref[...] + norm_columns_back(fg, normed, inv_std, col_ref[:, 0:1])).astype(bf)
    vec_ref[...] = sums_across((fg * normed, fg))


def feed_grads_body(sc, hidt_ref, gyt_ref, ug_ref, act_ref, hidt2_ref, gyt2_ref, ug2_ref, act2_ref, o_ref):
    half = o_ref.shape[1] // 2
    o_ref[:, 0:half] = (nn(hidt_ref[...], ug_ref[...]) + nn(hidt2_ref[...], ug2_ref[...])).astype(bf)
    o_ref[:, half:] = (nn(gyt_ref[...], act_ref[...]) + nn(gyt2_ref[...], act2_ref[...])).astype(bf)


def rows_grads_body(sc, a_ref, b_ref, a2_ref, b2_ref, o_ref):
    half = b2_ref.shape[0]
    o_ref[...] = (nt(a_ref[...], half_rows(b_ref, sc[0], half)) + nt(a2_ref[...], b2_ref[...])).astype(bf)


def shape(dims, dtype):
    return jax.ShapeDtypeStruct(tuple(dims), dtype)


def swap(a, axis, k):
    n = lax.axis_size(axis)
    return lax.ppermute(a, axis, [(i, i ^ k) for i in range(n)])


def pieces_to_owners(a, axis):
    return lax.all_to_all(a, axis, 0, 0, tiled=True)


def chain_seq(part, forward, weight_of):
    n = lax.axis_size("seq")
    total = None
    for k in range(1, n):
        pairs = [(i, i + k) if forward else (i + k, i) for i in range(n - k)]
        sent = part if forward else part * weight_of(k).astype(part.dtype)
        got = lax.ppermute(sent, "seq", pairs)
        if n == 2:
            return got
        got = got.astype(f32) * (weight_of(k) if forward else 1.0)
        total = got if total is None else total + got
    return total.astype(bf)


def local(tokens, attn_gain, attn_shift, qkv_weight, qkv_bias, query_map, key_map, out_weight, out_bias,
          mlp_gain, mlp_shift, up_weight, up_bias, down_weight, down_bias, positions, out_grad):
    nh, ns, nz = lax.axis_size("head"), lax.axis_size("seq"), lax.axis_size("dp")
    length, width = tokens.shape[1], tokens.shape[2]
    model = width * nh
    half = model // 2
    hp, hs = query_map.shape[0], query_map.shape[1]
    heads = hp * nh
    pc = qkv_weight.shape[1]
    hidden = up_weight.shape[1]
    tok = length // nh
    h = lax.axis_index("head")
    s2 = lax.axis_index("seq") % 2
    peers = range(1, nh)

    def mine(a, axis):
        return lax.dynamic_slice_in_dim(a, s2 * (a.shape[axis] // 2), a.shape[axis] // 2, axis)

    def theirs(a, axis):
        return lax.dynamic_slice_in_dim(a, (1 - s2) * (a.shape[axis] // 2), a.shape[axis] // 2, axis)

    def to_chunks(a):
        a = a[0].T.reshape(width, nh, tok).transpose(1, 0, 2)
        return pieces_to_owners(a, "head").reshape(model, tok)

    x = to_chunks(tokens)
    small = jnp.concatenate(
        [query_map.reshape(-1, hs), key_map.reshape(-1, hs)]
        + [jnp.concatenate([qkv_bias, up_bias, out_bias, down_bias]).reshape(-1, hs)]
    )
    small = jnp.pad(small, ((0, -small.shape[0] % 16), (0, 0)))
    smalls = [small] + [swap(small, "head", m) for m in peers]

    qkv_t = qkv_weight.T
    qkv_m, qkv_o = [mine(qkv_t, 1)], [theirs(qkv_t, 1)]
    for m in peers:
        qkv_m.append(swap(qkv_m[0], "head", m))
        qkv_o.append(swap(qkv_m[m], "seq", 1))
    out_m, out_o = [mine(out_weight, 1)], [theirs(out_weight, 1)]
    blocks = []
    for pick in (mine, theirs):
        down = pick(down_weight, 0)
        blocks.append(
            jnp.concatenate([pick(up_weight, 1), jnp.concatenate([down[:, :half], down[:, half:]], axis=0)], axis=1)
        )
    tied, out_first, qkv_m[nh - 1] = lax.optimization_barrier((blocks[0], out_m[0], qkv_m[nh - 1]))
    for m in peers:
        out_m.append(swap(out_first, "head", m))
        out_o.append(swap(out_m[m], "seq", 1))
    blk_m, blk_o = [blocks[0]], [blocks[1]]
    for m in peers:
        blk_m.append(swap(tied, "head", m))
        blk_o.append(swap(blk_m[m], "seq", 1))
    gyt = to_chunks(out_grad)

    maps = [a[: 2 * hp * hs] for a in smalls]
    flat = [a[2 * hp * hs :].reshape(-1) for a in smalls]
    qkv_cols = [a[:pc].astype(f32)[:, None] for a in flat]
    up_rows = [a[pc : pc + hidden].astype(f32)[None, :] for a in flat]
    order = h ^ jnp.arange(nh)
    tail = jnp.stack([a[pc + hidden : pc + hidden + 2 * width] for a in flat])[order]
    cols = jnp.stack(
        [attn_gain, attn_shift, mlp_gain, mlp_shift, tail[:, :width].reshape(-1), tail[:, width:].reshape(-1)]
        + [jnp.zeros_like(attn_gain)] * 2,
        axis=1,
    ).astype(f32)

    run = positions[0]
    start_of = jnp.arange(length, dtype=jnp.int32) - run
    chunk_starts = lax.dynamic_slice_in_dim(start_of, h * tok, tok, 0) - h * tok
    starts = jnp.broadcast_to(chunk_starts[None, :], (8, tok))
    firsts = start_of[::tok]
    run_last = start_of[length - 1]
    other = [h ^ m for m in range(nh)]
    fwd = [(other[m] < h) & (firsts[h] <= (other[m] + 1) * tok - 1) for m in peers]
    bwd = [(other[m] > h) & (firsts[other[m]] <= (h + 1) * tok - 1) for m in peers]
    sc = jnp.stack(
        [s2, chunk_starts[tok - 1]]
        + [a.astype(jnp.int32) for a in fwd]
        + [(firsts[h] < 0).astype(jnp.int32)]
        + [a.astype(jnp.int32) for a in bwd]
        + [(run_last <= (h + 1) * tok - 1).astype(jnp.int32)]
    ).astype(jnp.int32)

    (hid,) = run_kernel(first_norm_body, "first_norm", [shape((model, tok), bf)], sc, x, cols, flops=model * tok * 10)
    hid_peer = swap(theirs(hid, 0), "seq", 1)
    proj, qf, kf, va, st = [], [], [], [], []
    for j in range(nh):
        outs = run_kernel(
            functools.partial(project_body, hp, hs),
            f"project_{j}",
            [shape((pc, tok), bf), shape((hp, 2 * hs, tok), bf), shape((hp, 2 * hs, tok), bf),
             shape((hp, AUG, tok), bf), shape((hp, AUG, 2 * hs), bf)],
            sc, hid, qkv_m[j], qkv_o[j], qkv_cols[j], maps[j], starts,
            flops=2 * model * pc * tok + 4 * pc * hs * tok, trans=4 * hp * hs * tok,
        )
        for to, a in zip((proj, qf, kf, va, st), outs):
            to.append(a)
    states = jnp.concatenate(st)
    around = [states] + [swap(states, "head", m) for m in peers]

    def by_own_pieces(a, m):
        a = a.reshape(nh, hp, AUG, 2 * hs)
        return jnp.stack([a[j ^ m] for j in range(nh)]).reshape(heads, AUG, 2 * hs)

    ends_in = [((run_last <= (other[m] + 1) * tok - 1)).astype(f32) for m in range(nh)]
    whole = sum(by_own_pieces(a, m).astype(f32) * ends_in[m] for m, a in enumerate(around)).astype(bf)
    before = chain_seq(whole, True, lambda k: (start_of[0] <= -(k - 1) * length - 1).astype(f32))

    nums = []
    pair_flops = 2 * hp * tok * tok * 3 // 4
    for j in range(nh):
        (num,) = run_kernel(
            functools.partial(local_mix_body, hp), f"local_mix_{j}", [shape((hp, AUG, tok), f32)],
            sc, qf[j], kf[j], va[j], starts, flops=pair_flops * (2 * hs + AUG),
        )
        nums.append(num)
    sin, mixd, mix, res, hidt2, hid2 = run_kernel(
        functools.partial(mix_out_body, hp, hs, nh),
        "mix_out",
        [shape((heads, AUG, 2 * hs), bf), shape((heads, hs + 8, tok), f32), shape((model, tok), bf),
         shape((model, tok), f32), shape((model, tok), bf), shape((tok, model), bf)],
        sc, *nums, *qf, *around[1:], before, *out_m, *out_o, starts, x, cols,
        flops=2 * model * model * tok + 2 * heads * AUG * 2 * hs * tok,
    )
    (gy,) = run_kernel(turn_body, "turn_grad", [shape((tok, model), bf)], sc, gyt)
    act_m, ug_m, act_o, ug_o, ubs = [], [], [], [], []
    sums = ()
    for j in range(nh):
        outs = run_kernel(
            functools.partial(feed_body, j == 0),
            f"feed_{j}",
            [shape((tok, model), f32), shape((model, tok), f32)] + [shape((tok, hidden // 2), bf)] * 4
            + [shape((8, hidden), f32)],
            sc, hid2, gy, blk_m[j], blk_o[j], up_rows[j], *sums,
            flops=8 * model * hidden * tok, trans=hidden * tok,
        )
        sums = tuple(outs[:2])
        for to, a in zip((act_m, ug_m, act_o, ug_o, ubs), outs[2:]):
            to.append(a)
    mlp_out, sg = sums
    (bo,) = run_kernel(block_out_body, "block_out", [shape((model, tok), bf)], sc, res, mlp_out, cols)

    def to_runs(a):
        a = pieces_to_owners(a.reshape(nh, width, tok), "head")
        return a.transpose(1, 0, 2).reshape(width, length).T[None]

    rg, ag, vec2, na, sgt = run_kernel(
        functools.partial(second_back_body, hp, hs, nh),
        "second_back",
        [shape((model, tok), f32), shape((model, tok), bf), shape((model, 128), f32),
         shape((heads, AUG, tok), bf), shape((heads, AUG, 2 * hs), bf)],
        sc, sg, res, gyt, cols, mixd, starts, *out_m, *out_o, *qf,
        flops=2 * model * model * tok + 2 * heads * AUG * 2 * hs * tok,
    )
    g_around = [sgt] + [swap(sgt, "head", m) for m in peers]
    begins_in = [(firsts[other[m]] < 0).astype(f32) for m in range(nh)]
    g_whole = sum(by_own_pieces(a, m).astype(f32) * begins_in[m] for m, a in enumerate(g_around)).astype(bf)
    after = chain_seq(g_whole, False, lambda k: (start_of[0] <= -(k - 1) * length - 1).astype(f32))

    local_back = []
    for j in range(nh):
        local_back.append(
            run_kernel(
                functools.partial(local_back_body, hp, hs, j), f"local_back_{j}",
                [shape((hp, hs, tok), bf), shape((hp, 2 * hs, tok), f32), shape((hp, hs, tok), f32)],
                sc, qf[j], kf[j], va[j], na, sin, starts, flops=pair_flops * (6 * hs + 3 * AUG),
            )
        )
    fg = None
    pg, map_grads, pbs = [None] * nh, [None] * nh, [None] * nh
    for j in [*range(nh - 1, 0, -1), 0]:
        pg[j], fg, map_grads[j], pbs[j] = run_kernel(
            functools.partial(project_back_body, hp, hs, nh, j, fg is None),
            f"project_back_{j}",
            [shape((pc, tok), bf), shape((model, tok), f32), shape((2 * hp * hs, hs), f32), shape((pc, 128), f32)],
            sc, *g_around[1:], after, kf[j], va[j], *local_back[j], proj[j], maps[j], qkv_m[j], qkv_o[j], starts,
            *(() if fg is None else (fg,)),
            flops=2 * model * pc * tok + 12 * pc * hs * tok,
        )
    tg, vec1 = run_kernel(
        first_back_body, "first_back", [shape((model, tok), bf), shape((model, 128), f32)], sc, fg, x, rg, cols
    )
    tokens_grad = to_runs(tg)
    block_out = to_runs(bo)

    def over_head(parts):
        total = parts[0].astype(f32)
        for m in peers:
            total += swap(parts[m], "head", m).astype(f32)
        for k in range(1, ns // 2):
            n = ns
            total += lax.ppermute(total, "seq", [(i, (i + 2 * k) % n) for i in range(n)])
        return total.astype(bf)

    def over_dp(a):
        rows = a.shape[0] // nz
        got = pieces_to_owners(a.reshape(nz, rows, -1), "dp")
        total = got.astype(f32).sum(0).astype(bf)
        return pieces_to_owners(jnp.broadcast_to(total[None], (nz,) + total.shape), "dp").reshape(a.shape)

    hidt2_peer, gyt_peer = swap(hidt2, "seq", 1), swap(gyt, "seq", 1)
    feed_parts = []
    for j in range(nh):
        (part,) = run_kernel(
            feed_grads_body, f"feed_grads_{j}", [shape((model, hidden), bf)], sc,
            hidt2, gyt, ug_m[j], act_m[j], hidt2_peer, gyt_peer, swap(ug_o[j], "seq", 1), swap(act_o[j], "seq", 1),
            flops=4 * model * hidden * tok,
        )
        feed_parts.append(part)
    mix_peer, ag_peer = swap(mix, "seq", 1), swap(theirs(ag, 0), "seq", 1)
    rows = hp * hs
    out_parts, qkv_parts = [], [None] * nh
    for j in range(nh):
        (part,) = run_kernel(
            rows_grads_body, f"out_grads_{j}", [shape((rows, half), bf)], sc,
            mix[j * rows : (j + 1) * rows], ag, mix_peer[j * rows : (j + 1) * rows], ag_peer,
            flops=2 * model * rows * tok,
        )
        out_parts.append(part)
    for j in [*range(nh - 1, 0, -1), 0]:
        (qkv_parts[j],) = run_kernel(
            rows_grads_body, f"qkv_grads_{j}", [shape((pc, half), bf)], sc, pg[j], hid, swap(pg[j], "seq", 1), hid_peer,
            flops=2 * model * pc * tok,
        )

    def both_halves(a, axis):
        other_half = swap(a, "seq", 1)
        return jnp.where(
            s2 == 0,
            jnp.concatenate([a, other_half], axis=axis),
            jnp.concatenate([other_half, a], axis=axis),
        ).astype(f32)

    feed_sum = over_dp(over_head(feed_parts))
    out_sum = over_dp(over_head(out_parts))
    qkv_sum = over_dp(over_head(qkv_parts))
    upweight_grad = both_halves(feed_sum[:, : hidden // 2], 1)
    downweight_grad = both_halves(feed_sum[:, hidden // 2 :], 1).T
    outweight_grad = both_halves(out_sum, 1)
    qkvweight_grad = both_halves(qkv_sum, 1).T

    vectors = jnp.concatenate([vec1[:, 0:2], vec2[:, 0:4]], axis=1).T
    vectors = vectors.reshape(6, nh, width).transpose(1, 0, 2).reshape(nh, -1)
    vectors = vectors[order]
    packs = []
    for j in range(nh):
        one = jnp.concatenate([map_grads[j].reshape(-1), pbs[j][:, 0], ubs[j][0], vectors[j]])
        packs.append(jnp.pad(one, (0, -one.shape[0] % 1024)).reshape(-1, 128))
    total = packs[0]
    for m in peers:
        total += swap(packs[m], "head", m)
    for k in range(1, ns):
        total_k = lax.ppermute(total, "seq", [(i, i ^ 1) for i in range(ns)]) if k == 1 else None
        if k == 1:
            total = total + total_k
    base = total
    for k in range(1, ns // 2):
        total = total + lax.ppermute(base, "seq", [(i, (i + 2 * k) % ns) for i in range(ns)])
    base = total
    for k in range(1, nz):
        total = total + lax.ppermute(base, "dp", [(i, (i + k) % nz) for i in range(nz)])
    total = total.reshape(-1)
    nm = hp * hs * hs
    query_grad = total[:nm].reshape(hp, hs, hs)
    key_grad = total[nm : 2 * nm].reshape(hp, hs, hs)
    at = 2 * nm
    qkvbias_grad = total[at : at + pc]
    upbias_grad = total[at + pc : at + pc + hidden]
    vec = total[at + pc + hidden : at + pc + hidden + 6 * width].reshape(6, width)
    return (block_out, tokens_grad, vec[0], vec[1], qkvweight_grad, qkvbias_grad, query_grad, key_grad,
            outweight_grad, vec[4], vec[2], vec[3], upweight_grad, upbias_grad, downweight_grad, vec[5])


def solution(mesh):
    wide = P("dp", "seq", "head")
    return jax.shard_map(
        local,
        mesh=mesh,
        in_specs=(wide, P(), P(), P(None, "head"), P("head"), P("head", None, None), P("head", None, None),
                  P("head", None), P("head"), P(), P(), P(None, "head"), P("head"), P("head", None), P("head"),
                  P("dp", "seq"), wide),
        out_specs=(wide, wide, P("head"), P("head"), P(None, "head"), P("head"), P("head", None, None),
                   P("head", None, None), P("head", None), P("head"), P("head"), P("head"), P(None, "head"), P("head"),
                   P("head", None), P("head")),
        check_vma=False,
    )
```

time: 1210 us -> 558 us (0.46)
  waiting for transfers between devices: 806 us -> 177 us
  matrix products: 135 us -> 0 us
  Pallas kernels: 0 us -> 125 us
  starting transfers between devices: 1.15 us -> 102 us
  other arithmetic: 102 us -> 30.1 us
  local copies, waits for them, and re-layouts: 131 us -> 99.2 us
    unnamed x11 -> x0, waiting for transfers between devices: 347 us -> none
    psum x3 -> x0, waiting for transfers between devices: 331 us -> none  [the longest x2 194 us: local(): lax.psum((attngain_grad, attnshift_grad, qkvweight_grad, qkvbias_grad, qu...]
    dot_general x40 -> x0, matrix products: 135 us -> none  [the longest x1 10.7 us: local(): jnp.einsum('bld,fd->blf', grad_full, down_weight, preferred_element_type=...]
    ppermute x0 -> x66, waiting for transfers between devices: none -> 131 us  [the longest x60 119 us: swap(): return lax.ppermute(a, axis, [(i, i ^ k) for i in range(n)])]
    all_gather x4 -> x0, waiting for transfers between devices: 127 us -> none  [widen(): return lax.all_gather(part, 'head', axis=2, tiled=True)]
    pallas_call x0 -> x38, Pallas kernels: none -> 125 us  [run_kernel(): pl.pallas_call(body, out_shape=outs, in_specs=[pl.BlockSpec(memory_space=...]
    ppermute x0 -> x66, starting transfers between devices: none -> 62 us  [the longest x60 51.6 us: swap(): return lax.ppermute(a, axis, [(i, i ^ k) for i in range(n)])]
    reduce_sum x14 -> x3, other arithmetic: 56.3 us -> 2.92 us  [over_dp(): total = got.astype(f32).sum(0).astype(bf)]
  transfers between devices with their start and end apart: 9 -> 76, of which waited for: 9 -> 20; matrix products, arithmetic and copies ran while one was open for 9% -> 14% of each run, Pallas kernels for 0% -> 23%
where the time goes in v1:
time: 558 us; the launch traced here: 547 us
  waiting for transfers between devices  177 us (32%)
  Pallas kernels  125 us (22%)
  starting transfers between devices  102 us (18%)
  local copies, waits for them, and re-layouts  99.2 us (18%)
  other arithmetic  30.1 us (5%)
  between operations  12.9 us (2%)
    pallas_call x38, Pallas kernels, run_kernel(): pl.pallas_call(body, out_shape=outs, in_specs=[pl.BlockSpec(memory_space=...  125 us
    ppermute x60, waiting for transfers between devices, swap(): return lax.ppermute(a, axis, [(i, i ^ k) for i in range(n)])  119 us
    ppermute x60, starting transfers between devices, swap(): return lax.ppermute(a, axis, [(i, i ^ k) for i in range(n)])  51.6 us
    unnamed x372, local copies, waits for them, and re-layouts  46.6 us
    all_to_all x10, waiting for transfers between devices, pieces_to_owners(): return lax.all_to_all(a, axis, 0, 0, tiled=True)  46.1 us
    all_to_all x10, starting transfers between devices, pieces_to_owners(): return lax.all_to_all(a, axis, 0, 0, tiled=True)  40.2 us
  transfers between devices with their start and end apart: 76, of which 20 were waited for; matrix products, arithmetic and copies ran while one was open for 14% of the time, Pallas kernels for 23%

profile of v1, /device:TPU:0, one launch (start us, length us, event | category | flops | bytes accessed | tf_op | source)
XLA Modules:
  0.0 546.9 jit_solution(17223793862159276120)
XLA Ops:
  0.7 2.8 concatenate.67
  5.1 2.9 collective-permute-start
  15.3 3.5 all-to-all-start
  37.3 2.1 copy.78
  40.8 2.9 collective-permute-start.7
  49.2 3.2 collective-permute-done.7.wm_ref.refs_11_
  63.6 3.5 all-to-all-start.1
  72.7 2.9 collective-permute-start.19
  76.3 2.6 project_1.1
  81.9 2.6 project_2.1
  86.8 2.7 project_3.1
  93.1 33.2 %collective-permute-done.13.refs_13_.refs_7_ = bf16[192,384]{1,0:T(8,128)(2,1)S(1)} collective-permute-done((bf16[192,384]{1,0:T(8,128)(2,1)S(1)}, bf16[192,384]{1,0:T(8,128)(2,1)S(1)}, u32[]{:S(2)}, u32[]{:S(2)}) %collective-permute-start.13) | collective-permute-done | bytes 147488 | tf_op jit(solution)/shard_map/ppermute | solution.py:346
  129.3 3.1 collective-permute-done.11.refs_10_
  133.9 3.8 collective-permute-done.10.refs_9_
  138.0 5.5 %collective-permute-done.14.refs_14_.refs_8_ = bf16[192,384]{1,0:T(8,128)(2,1)} collective-permute-done((bf16[192,384]{1,0:T(8,128)(2,1)S(1)}, bf16[192,384]{1,0:T(8,128)(2,1)}, u32[]{:S(2)}, u32[]{:S(2)}) %collective-permute-start.14) | collective-permute-done | bytes 147488 | tf_op jit(solution)/shard_map/ppermute | solution.py:346
  146.4 3.1 collective-permute-done.15.refs_15_.refs_9_
  150.3 3.2 collective-permute-start.12
  171.5 5.0 mix_out.1
  177.8 7.1 %feed_0.1 = (f32[512,768]{1,0:T(8,128)}, f32[768,512]{1,0:T(8,128)}, bf16[512,384]{1,0:T(8,128)(2,1)S(1)}, bf16[512,384]{1,0:T(8,128)(2,1)S(1)}, bf16[512,384]{1...) custom-call(s32[10]{0:T(128)S(1)} %copy-done.89, bf16[512,768]{1,0:T(8,128)(2,1)S(1)} %copy-done.155, ...), custom_call_target="tpu_custom_call" | custom-call | flops 2415919104 | bytes 8678400 | tf_op jit(solution)/shard_map/feed_0/pallas_call | solution.py:32
  185.8 8.5 %feed_1.1 = (f32[512,768]{1,0:T(8,128)}, f32[768,512]{1,0:T(8,128)}, bf16[512,384]{1,0:T(8,128)(2,1)S(1)}, bf16[512,384]{1,0:T(8,128)(2,1)S(1)}, bf16[512,384]{1...) custom-call(s32[10]{0:T(128)S(1)} %copy-done.89, bf16[512,768]{1,0:T(8,128)(2,1)S(1)} %copy-done.156, ...), custom_call_target="tpu_custom_call" | custom-call | flops 2415919104 | bytes 11824128 | tf_op jit(solution)/shard_map/feed_1/pallas_call | solution.py:32
  195.8 8.0 %feed_2.1 = (f32[512,768]{1,0:T(8,128)}, f32[768,512]{1,0:T(8,128)}, bf16[512,384]{1,0:T(8,128)(2,1)S(1)}, bf16[512,384]{1,0:T(8,128)(2,1)S(1)}, bf16[512,384]{1...) custom-call(s32[10]{0:T(128)S(1)} %copy-done.89, bf16[512,768]{1,0:T(8,128)(2,1)S(1)} %copy-done.156, ...), custom_call_target="tpu_custom_call" | custom-call | flops 2415919104 | bytes 11824128 | tf_op jit(solution)/shard_map/feed_2/pallas_call | solution.py:32
  206.7 8.2 %feed_3.1 = (f32[512,768]{1,0:T(8,128)}, f32[768,512]{1,0:T(8,128)}, bf16[512,384]{1,0:T(8,128)(2,1)S(1)}, bf16[512,384]{1,0:T(8,128)(2,1)S(1)}, bf16[512,384]{1...) custom-call(s32[10]{0:T(128)S(1)} %copy-done.89, bf16[512,768]{1,0:T(8,128)(2,1)S(1)} %copy-done.156, ...), custom_call_target="tpu_custom_call" | custom-call | flops 2415919104 | bytes 11824128 | tf_op jit(solution)/shard_map/feed_3/pallas_call | solution.py:32
  214.9 7.4 %second_back.1 = (f32[768,512]{1,0:T(8,128)}, bf16[768,512]{1,0:T(8,128)(2,1)S(1)}, f32[768,128]{1,0:T(8,128)S(1)}, bf16[12,80,512]{2,1,0:T(8,128)(2,1)}, bf16[12,80,128]{2,1,0:T(8,128)(2,1)S(1)}) custom-call(s32[10]{0:T(128)S(1)} %copy-done.89, f32[768,512]{1,0:T(8,128)} %get-tuple-element.136.refs_0_, f32[768,512]{1,0:T(8,128)} %get-tuple-element.126.res_ref.refs_1_, ...), custom_call_target="tpu_custom_call" | custom-call | flops 729808896 | bytes 12476416 | tf_op jit(solution)/shard_map/second_back/pallas_call | solution.py:32
  226.4 3.1 local_back_3.1
  233.0 3.8 collective-permute-done.26.refs_1_
  236.8 2.2 collective-permute-done.25.refs_0_
  240.7 3.0 local_back_2.1
  245.2 3.0 local_back_1.1
  253.9 4.1 project_back_3.1
  260.4 4.7 project_back_2.1
  266.5 4.6 project_back_1.1
  280.3 3.0 local_back_0.1
  286.3 4.5 project_back_0.1
  295.1 3.4 feed_grads_1.1
  298.7 2.1 qkv_grads_1.1
  304.3 4.9 all-to-all-start.6
  314.4 3.4 feed_grads_2.1
  318.4 4.0 feed_grads_3.1
  322.8 2.5 collective-permute-start.63
  327.4 4.2 all-to-all-start.2
  332.6 2.9 qkv_grads_2.1
  337.4 2.8 qkv_grads_3.1
  347.1 55.4 %collective-permute-done.41 = bf16[576,384]{1,0:T(8,128)(2,1)} collective-permute-done((bf16[576,384]{1,0:T(8,128)(2,1)}, bf16[576,384]{1,0:T(8,128)(2,1)}, u32[]{:S(2)}, u32[]{:S(2)}) %collective-permute-start.41) | collective-permute-done | bytes 442400 | tf_op jit(solution)/shard_map/ppermute | solution.py:346
  404.5 4.8 all-to-all-start.7
  409.3 2.5 add_convert_fusion.1
  411.8 3.9 all-to-all-done.7
  415.7 4.1 all-to-all-start.4
  421.8 2.9 feed_grads_0.1
  424.8 3.6 add_convert_fusion
  428.3 3.0 all-to-all-done.4
  431.3 3.5 all-to-all-start.8
  436.0 25.3 %all-to-all-done.8 = bf16[4,192,768]{2,1,0:T(8,128)(2,1)S(1)} async-done(((bf16[4,192,768]{2,1,0:T(8,128)(2,1)}), bf16[4,192,768]{2,1,0:T(8,128)(2,1)S(1)}, u32[]{:S(2)}, u32[]{:S(2)}) %all-to-all-start.8) | async-done | bytes 1179680 | tf_op jit(solution)/shard_map/all_to_all | solution.py:350
  462.1 3.5 all-to-all-start.5
  469.9 7.9 %all-to-all-done.5 = bf16[4,144,384]{2,1,0:T(8,128)(2,1)S(1)} async-done(((bf16[4,144,384]{2,1,0:T(8,128)(2,1)}), bf16[4,144,384]{2,1,0:T(8,128)(2,1)S(1)}, u32[]{:S(2)}, u32[]{:S(2)}) %all-to-all-start.5) | async-done | bytes 442400 | tf_op jit(solution)/shard_map/all_to_all | solution.py:350
  479.6 4.6 all-to-all-start.9
  487.2 2.9 first_back.1
  496.7 2.5 collective-permute-done.30
  501.9 2.0 collective-permute-start.33
  504.0 2.4 collective-permute-start.34
  507.8 2.1 copy.73
  509.9 10.5 %collective-permute-done.34 = f32[216,128]{1,0:T(8,128)S(1)} collective-permute-done((f32[216,128]{1,0:T(8,128)S(1)}, f32[216,128]{1,0:T(8,128)S(1)}, u32[]{:S(2)}, u32[]{:S(2)}) %collective-permute-start.34) | collective-permute-done | bytes 110624 | tf_op jit(solution)/shard_map/ppermute | solution.py:628
  520.6 3.5 all-to-all-start.3
  529.9 5.9 %all-to-all-done.3 = bf16[4,192,512]{2,1,0:T(8,128)(2,1)S(1)} async-done(((bf16[4,192,512]{2,1,0:T(8,128)(2,1)}), bf16[4,192,512]{2,1,0:T(8,128)(2,1)S(1)}, u32[]{:S(2)}, u32[]{:S(2)}) %all-to-all-start.3) | async-done | bytes 786464 | tf_op jit(solution)/shard_map/all_to_all | solution.py:350
  543.6 2.9 fusion
  (624 shorter events, 180.3 us)
Async XLA Ops:
  5.1 35.7 %collective-permute-start = (bf16[416,64]{1,0:T(8,128)(2,1)}, bf16[416,64]{1,0:T(8,128)(2,1)}, u32[]{:S(2)}, u32[]{:S(2)}) collective-permute-start(bf16[416,64]{1,0:T(8,128)(2,1)} %fusion.9), channel_id=1, source_target_pairs={{0,4},{4,0},{8,12},{12,8},{1,5},{5,1},{9,13},{13,9},{2,6},{6,2},{1... | collective-permute-start | bytes 159752 | tf_op jit(solution)/shard_map/ppermute | solution.py:346
  8.0 36.4 %collective-permute-start.1 = (bf16[416,64]{1,0:T(8,128)(2,1)}, bf16[416,64]{1,0:T(8,128)(2,1)}, u32[]{:S(2)}, u32[]{:S(2)}) collective-permute-start(bf16[416,64]{1,0:T(8,128)(2,1)} %fusion.9), channel_id=1, source_target_pairs={{0,8},{4,12},{8,0},{12,4},{1,9},{5,13},{9,1},{13,5},{2,10},{6,14},... | collective-permute-start | bytes 159752 | tf_op jit(solution)/shard_map/ppermute | solution.py:346
  9.5 37.1 %collective-permute-start.2 = (bf16[416,64]{1,0:T(8,128)(2,1)}, bf16[416,64]{1,0:T(8,128)(2,1)}, u32[]{:S(2)}, u32[]{:S(2)}) collective-permute-start(bf16[416,64]{1,0:T(8,128)(2,1)} %fusion.9), channel_id=1, source_target_pairs={{0,12},{4,8},{8,4},{12,0},{1,13},{5,9},{9,5},{13,1},{2,14},{6,10},... | collective-permute-start | bytes 159752 | tf_op jit(solution)/shard_map/ppermute | solution.py:346
  10.8 37.3 %collective-permute-start.3 = (bf16[576,384]{1,0:T(8,128)(2,1)S(1)}, bf16[576,384]{1,0:T(8,128)(2,1)}, u32[]{:S(2)}, u32[]{:S(2)}) collective-permute-start(bf16[576,384]{1,0:T(8,128)(2,1)S(1)} %get-tuple-element.261.wm_ref.refs_11_), channel_id=1, source_target_pairs={{0,4},{4,0},{8,12},{12,8},{1,5},{5,1},{9,13},{13,9},{2,6},{6,2},{1... | collective-permute-start | bytes 1327112 | tf_op jit(solution)/shard_map/ppermute | solution.py:346
  12.8 35.3 %collective-permute-start.5 = (bf16[576,384]{1,0:T(8,128)(2,1)S(1)}, bf16[576,384]{1,0:T(8,128)(2,1)}, u32[]{:S(2)}, u32[]{:S(2)}) collective-permute-start(bf16[576,384]{1,0:T(8,128)(2,1)S(1)} %get-tuple-element.261.wm_ref.refs_11_), channel_id=1, source_target_pairs={{0,8},{4,12},{8,0},{12,4},{1,9},{5,13},{9,1},{13,5},{2,10},{6,14},... | collective-permute-start | bytes 1327112 | tf_op jit(solution)/shard_map/ppermute | solution.py:346
  15.3 48.3 %all-to-all-start = ((bf16[4,192,512]{2,1,0:T(8,128)(2,1)}), bf16[4,192,512]{2,1,0:T(8,128)(2,1)S(1)}, u32[]{:S(2)}, u32[]{:S(2)}) async-start(bf16[4,192,512]{2,1,0:T(8,128)(2,1)} %bitcast.150), calls=%async_computation | async-start | bytes 1572864 | tf_op jit(solution)/shard_map/all_to_all | solution.py:350
  40.8 11.6 %collective-permute-start.7 = (bf16[576,384]{1,0:T(8,128)(2,1)S(1)}, bf16[576,384]{1,0:T(8,128)(2,1)}, u32[]{:S(2)}, u32[]{:S(2)}) collective-permute-start(bf16[576,384]{1,0:T(8,128)(2,1)S(1)} %get-tuple-element.261.wm_ref.refs_11_), channel_id=1, source_target_pairs={{0,12},{4,8},{8,4},{12,0},{1,13},{5,9},{9,5},{13,1},{2,14},{6,10},... | collective-permute-start | bytes 1327112 | tf_op jit(solution)/shard_map/ppermute | solution.py:346
  48.1 24.6 %collective-permute-start.4 = (bf16[576,384]{1,0:T(8,128)(2,1)}, bf16[576,384]{1,0:T(8,128)(2,1)}, u32[]{:S(2)}, u32[]{:S(2)}) collective-permute-start(bf16[576,384]{1,0:T(8,128)(2,1)} %collective-permute-done.3.wm_ref.refs_11_), channel_id=1, source_target_pairs={{0,16},{16,0},{1,17},{17,1},{2,18},{18,2},{3,19},{19,3},{4,20},{20... | collective-permute-start | bytes 1327112 | tf_op jit(solution)/shard_map/ppermute | solution.py:346
  48.1 33.1 %collective-permute-start.6 = (bf16[576,384]{1,0:T(8,128)(2,1)}, bf16[576,384]{1,0:T(8,128)(2,1)}, u32[]{:S(2)}, u32[]{:S(2)}) collective-permute-start(bf16[576,384]{1,0:T(8,128)(2,1)} %collective-permute-done.5.wm_ref.refs_11_), channel_id=1, source_target_pairs={{0,16},{16,0},{1,17},{17,1},{2,18},{18,2},{3,19},{19,3},{4,20},{20... | collective-permute-start | bytes 1327112 | tf_op jit(solution)/shard_map/ppermute | solution.py:346
  52.4 34.4 %collective-permute-start.8 = (bf16[576,384]{1,0:T(8,128)(2,1)}, bf16[576,384]{1,0:T(8,128)(2,1)}, u32[]{:S(2)}, u32[]{:S(2)}) collective-permute-start(bf16[576,384]{1,0:T(8,128)(2,1)} %collective-permute-done.7.wm_ref.refs_11_), channel_id=1, source_target_pairs={{0,16},{16,0},{1,17},{17,1},{2,18},{18,2},{3,19},{19,3},{4,20},{20... | collective-permute-start | bytes 1327112 | tf_op jit(solution)/shard_map/ppermute | solution.py:346
  60.4 77.5 %collective-permute-start.23 = (bf16[768,768]{1,0:T(8,128)(2,1)}, bf16[768,768]{1,0:T(8,128)(2,1)}, u32[]{:S(2)}, u32[]{:S(2)}) collective-permute-start(bf16[768,768]{1,0:T(8,128)(2,1)} %maximum_maximum_fusion.bm_ref), channel_id=1, source_target_pairs={{0,4},{4,0},{8,12},{12,8},{1,5},{5,1},{9,13},{13,9},{2,6},{6,2},{1... | collective-permute-start | bytes 3538952 | tf_op jit(solution)/shard_map/ppermute | solution.py:346
  62.1 82.8 %collective-permute-start.21 = (bf16[768,768]{1,0:T(8,128)(2,1)}, bf16[768,768]{1,0:T(8,128)(2,1)}, u32[]{:S(2)}, u32[]{:S(2)}) collective-permute-start(bf16[768,768]{1,0:T(8,128)(2,1)} %maximum_maximum_fusion.bm_ref), channel_id=1, source_target_pairs={{0,8},{4,12},{8,0},{12,4},{1,9},{5,13},{9,1},{13,5},{2,10},{6,14},... | collective-permute-start | bytes 3538952 | tf_op jit(solution)/shard_map/ppermute | solution.py:346
  63.6 95.4 %all-to-all-start.1 = ((bf16[4,192,512]{2,1,0:T(8,128)(2,1)}), bf16[4,192,512]{2,1,0:T(8,128)(2,1)S(1)}, u32[]{:S(2)}, u32[]{:S(2)}) async-start(bf16[4,192,512]{2,1,0:T(8,128)(2,1)} %bitcast.148), calls=%async_computation.1 | async-start | bytes 1572864 | tf_op jit(solution)/shard_map/all_to_all | solution.py:350
  72.7 80.8 %collective-permute-start.19 = (bf16[768,768]{1,0:T(8,128)(2,1)}, bf16[768,768]{1,0:T(8,128)(2,1)}, u32[]{:S(2)}, u32[]{:S(2)}) collective-permute-start(bf16[768,768]{1,0:T(8,128)(2,1)} %maximum_maximum_fusion.bm_ref), channel_id=1, source_target_pairs={{0,12},{4,8},{8,4},{12,0},{1,13},{5,9},{9,5},{13,1},{2,14},{6,10},... | collective-permute-start | bytes 3538952 | tf_op jit(solution)/shard_map/ppermute | solution.py:346
  81.2 45.1 %collective-permute-start.13 = (bf16[192,384]{1,0:T(8,128)(2,1)S(1)}, bf16[192,384]{1,0:T(8,128)(2,1)S(1)}, u32[]{:S(2)}, u32[]{:S(2)}) collective-permute-start(bf16[192,384]{1,0:T(8,128)(2,1)S(1)} %copy-done.39), channel_id=1, source_target_pairs={{0,4},{4,0},{8,12},{12,8},{1,5},{5,1},{9,13},{13,9},{2,6},{6,2},{1... | collective-permute-start | bytes 442376 | tf_op jit(solution)/shard_map/ppermute | solution.py:346
  90.3 42.1 %collective-permute-start.11 = (bf16[12,80,128]{2,1,0:T(8,128)(2,1)S(1)}, bf16[12,80,128]{2,1,0:T(8,128)(2,1)S(1)}, u32[]{:S(2)}, u32[]{:S(2)}) collective-permute-start(bf16[12,80,128]{2,1,0:T(8,128)(2,1)S(1)} %constant_dynamic-update-slice_fusion), channel_id=1, source_target_pairs={{0,12},{4,8},{8,4},{12,0},{1,13},{5,9},{9,5},{13,1},{2,14},{6,10},... | collective-permute-start | bytes 737288 | tf_op jit(solution)/shard_map/ppermute | solution.py:346
  126.4 11.3 %collective-permute-start.10 = (bf16[12,80,128]{2,1,0:T(8,128)(2,1)S(1)}, bf16[12,80,128]{2,1,0:T(8,128)(2,1)S(1)}, u32[]{:S(2)}, u32[]{:S(2)}) collective-permute-start(bf16[12,80,128]{2,1,0:T(8,128)(2,1)S(1)} %constant_dynamic-update-slice_fusion), channel_id=1, source_target_pairs={{0,8},{4,12},{8,0},{12,4},{1,9},{5,13},{9,1},{13,5},{2,10},{6,14},... | collective-permute-start | bytes 737288 | tf_op jit(solution)/shard_map/ppermute | solution.py:346
  132.5 12.5 %collective-permute-start.9 = (bf16[12,80,128]{2,1,0:T(8,128)(2,1)S(1)}, bf16[12,80,128]{2,1,0:T(8,128)(2,1)S(1)}, u32[]{:S(2)}, u32[]{:S(2)}) collective-permute-start(bf16[12,80,128]{2,1,0:T(8,128)(2,1)S(1)} %constant_dynamic-update-slice_fusion), channel_id=1, source_target_pairs={{0,4},{4,0},{8,12},{12,8},{1,5},{5,1},{9,13},{13,9},{2,6},{6,2},{1... | collective-permute-start | bytes 737288 | tf_op jit(solution)/shard_map/ppermute | solution.py:346
  138.0 47.6 %collective-permute-start.24 = (bf16[768,768]{1,0:T(8,128)(2,1)}, bf16[768,768]{1,0:T(8,128)(2,1)}, u32[]{:S(2)}, u32[]{:S(2)}) collective-permute-start(bf16[768,768]{1,0:T(8,128)(2,1)} %collective-permute-done.23.bm_ref), channel_id=1, source_target_pairs={{0,16},{16,0},{1,17},{17,1},{2,18},{18,2},{3,19},{19,3},{4,20},{20... | collective-permute-start | bytes 3538952 | tf_op jit(solution)/shard_map/ppermute | solution.py:346
  144.9 50.8 %collective-permute-start.22 = (bf16[768,768]{1,0:T(8,128)(2,1)}, bf16[768,768]{1,0:T(8,128)(2,1)}, u32[]{:S(2)}, u32[]{:S(2)}) collective-permute-start(bf16[768,768]{1,0:T(8,128)(2,1)} %collective-permute-done.21.bm_ref), channel_id=1, source_target_pairs={{0,16},{16,0},{1,17},{17,1},{2,18},{18,2},{3,19},{19,3},{4,20},{20... | collective-permute-start | bytes 3538952 | tf_op jit(solution)/shard_map/ppermute | solution.py:346
  149.5 13.1 %collective-permute-start.17 = (bf16[192,384]{1,0:T(8,128)(2,1)}, bf16[192,384]{1,0:T(8,128)(2,1)}, u32[]{:S(2)}, u32[]{:S(2)}) collective-permute-start(bf16[192,384]{1,0:T(8,128)(2,1)} %collective-permute-done.14.refs_14_.refs_8_), channel_id=1, source_target_pairs={{0,16},{16,0},{1,17},{17,1},{2,18},{18,2},{3,19},{19,3},{4,20},{20... | collective-permute-start | bytes 442376 | tf_op jit(solution)/shard_map/ppermute | solution.py:346
  150.3 20.7 %collective-permute-start.12 = (bf16[12,80,128]{2,1,0:T(8,128)(2,1)}, bf16[12,80,128]{2,1,0:T(8,128)(2,1)}, u32[]{:S(2)}, u32[]{:S(2)}) collective-permute-start(bf16[12,80,128]{2,1,0:T(8,128)(2,1)} %bitcast.40), channel_id=1, source_target_pairs={{0,16},{1,17},{2,18},{3,19},{4,20},{5,21},{6,22},{7,23},{8,24},{9,... | collective-permute-start | bytes 737288 | tf_op jit(solution)/shard_map/ppermute | solution.py:359
  153.6 53.1 %collective-permute-start.20 = (bf16[768,768]{1,0:T(8,128)(2,1)}, bf16[768,768]{1,0:T(8,128)(2,1)}, u32[]{:S(2)}, u32[]{:S(2)}) collective-permute-start(bf16[768,768]{1,0:T(8,128)(2,1)} %collective-permute-done.19.bm_ref), channel_id=1, source_target_pairs={{0,16},{16,0},{1,17},{17,1},{2,18},{18,2},{3,19},{19,3},{4,20},{20... | collective-permute-start | bytes 3538952 | tf_op jit(solution)/shard_map/ppermute | solution.py:346
  170.9 101.0 %collective-permute-start.52 = (bf16[768,512]{1,0:T(8,128)(2,1)S(1)}, bf16[768,512]{1,0:T(8,128)(2,1)S(1)}, u32[]{:S(2)}, u32[]{:S(2)}) collective-permute-start(bf16[768,512]{1,0:T(8,128)(2,1)S(1)} %bitcast.155), channel_id=1, source_target_pairs={{0,16},{16,0},{1,17},{17,1},{2,18},{18,2},{3,19},{19,3},{4,20},{20... | collective-permute-start | bytes 2359304 | tf_op jit(solution)/shard_map/ppermute | solution.py:346
  171.0 79.6 %collective-permute-start.37 = (bf16[384,512]{1,0:T(8,128)(2,1)}, bf16[384,512]{1,0:T(8,128)(2,1)S(1)}, u32[]{:S(2)}, u32[]{:S(2)}) collective-permute-start(bf16[384,512]{1,0:T(8,128)(2,1)} %constant_dynamic-slice_fusion.2), channel_id=1, source_target_pairs={{0,16},{16,0},{1,17},{17,1},{2,18},{18,2},{3,19},{19,3},{4,20},{20... | collective-permute-start | bytes 1179656 | tf_op jit(solution)/shard_map/ppermute | solution.py:346
  185.6 86.7 %collective-permute-start.51 = (bf16[768,512]{1,0:T(8,128)(2,1)S(1)}, bf16[768,512]{1,0:T(8,128)(2,1)S(1)}, u32[]{:S(2)}, u32[]{:S(2)}) collective-permute-start(bf16[768,512]{1,0:T(8,128)(2,1)S(1)} %copy-done), channel_id=1, source_target_pairs={{0,16},{16,0},{1,17},{17,1},{2,18},{18,2},{3,19},{19,3},{4,20},{20... | collective-permute-start | bytes 2359304 | tf_op jit(solution)/shard_map/ppermute | solution.py:346
  222.2 9.4 %collective-permute-start.27 = (bf16[12,80,128]{2,1,0:T(8,128)(2,1)S(1)}, bf16[12,80,128]{2,1,0:T(8,128)(2,1)S(1)}, u32[]{:S(2)}, u32[]{:S(2)}) collective-permute-start(bf16[12,80,128]{2,1,0:T(8,128)(2,1)S(1)} %get-tuple-element.138), channel_id=1, source_target_pairs={{0,12},{4,8},{8,4},{12,0},{1,13},{5,9},{9,5},{13,1},{2,14},{6,10},... | collective-permute-start | bytes 737288 | tf_op jit(solution)/shard_map/ppermute | solution.py:346
  223.7 13.0 %collective-permute-start.26 = (bf16[12,80,128]{2,1,0:T(8,128)(2,1)S(1)}, bf16[12,80,128]{2,1,0:T(8,128)(2,1)S(1)}, u32[]{:S(2)}, u32[]{:S(2)}) collective-permute-start(bf16[12,80,128]{2,1,0:T(8,128)(2,1)S(1)} %get-tuple-element.138), channel_id=1, source_target_pairs={{0,8},{4,12},{8,0},{12,4},{1,9},{5,13},{9,1},{13,5},{2,10},{6,14},... | collective-permute-start | bytes 737288 | tf_op jit(solution)/shard_map/ppermute | solution.py:346
  236.8 37.1 %collective-permute-start.45 = (bf16[768,512]{1,0:T(8,128)(2,1)}, bf16[768,512]{1,0:T(8,128)(2,1)}, u32[]{:S(2)}, u32[]{:S(2)}) collective-permute-start(bf16[768,512]{1,0:T(8,128)(2,1)} %get-tuple-element.181), channel_id=1, source_target_pairs={{0,16},{16,0},{1,17},{17,1},{2,18},{18,2},{3,19},{19,3},{4,20},{20... | collective-permute-start | bytes 2359304 | tf_op jit(solution)/shard_map/ppermute | solution.py:346
  239.4 12.4 %collective-permute-start.28 = (bf16[12,80,128]{2,1,0:T(8,128)(2,1)S(1)}, bf16[12,80,128]{2,1,0:T(8,128)(2,1)S(1)}, u32[]{:S(2)}, u32[]{:S(2)}) collective-permute-start(bf16[12,80,128]{2,1,0:T(8,128)(2,1)S(1)} %bitcast.183), channel_id=1, source_target_pairs={{16,0},{17,1},{18,2},{19,3},{20,4},{21,5},{22,6},{23,7},{24,8},{25... | collective-permute-start | bytes 737288 | tf_op jit(solution)/shard_map/ppermute | solution.py:359
  250.5 23.7 %collective-permute-start.55 = (bf16[512,384]{1,0:T(8,128)(2,1)}, bf16[512,384]{1,0:T(8,128)(2,1)S(1)}, u32[]{:S(2)}, u32[]{:S(2)}) collective-permute-start(bf16[512,384]{1,0:T(8,128)(2,1)} %get-tuple-element.190), channel_id=1, source_target_pairs={{0,16},{16,0},{1,17},{17,1},{2,18},{18,2},{3,19},{19,3},{4,20},{20... | collective-permute-start | bytes 1179656 | tf_op jit(solution)/shard_map/ppermute | solution.py:346
  251.7 22.8 %collective-permute-start.46 = (bf16[384,512]{1,0:T(8,128)(2,1)}, bf16[384,512]{1,0:T(8,128)(2,1)S(1)}, u32[]{:S(2)}, u32[]{:S(2)}) collective-permute-start(bf16[384,512]{1,0:T(8,128)(2,1)} %constant_dynamic-slice_fusion.1), channel_id=1, source_target_pairs={{0,16},{16,0},{1,17},{17,1},{2,18},{18,2},{3,19},{19,3},{4,20},{20... | collective-permute-start | bytes 1179656 | tf_op jit(solution)/shard_map/ppermute | solution.py:346
  272.3 26.3 %collective-permute-start.38 = (bf16[576,512]{1,0:T(8,128)(2,1)S(1)}, bf16[576,512]{1,0:T(8,128)(2,1)S(1)}, u32[]{:S(2)}, u32[]{:S(2)}) collective-permute-start(bf16[576,512]{1,0:T(8,128)(2,1)S(1)} %get-tuple-element.178.a_ref), channel_id=1, source_target_pairs={{0,16},{16,0},{1,17},{17,1},{2,18},{18,2},{3,19},{19,3},{4,20},{20... | collective-permute-start | bytes 1769480 | tf_op jit(solution)/shard_map/ppermute | solution.py:346
  273.9 17.6 %collective-permute-start.58 = (bf16[512,384]{1,0:T(8,128)(2,1)}, bf16[512,384]{1,0:T(8,128)(2,1)S(1)}, u32[]{:S(2)}, u32[]{:S(2)}) collective-permute-start(bf16[512,384]{1,0:T(8,128)(2,1)} %get-tuple-element.194), channel_id=1, source_target_pairs={{0,16},{16,0},{1,17},{17,1},{2,18},{18,2},{3,19},{19,3},{4,20},{20... | collective-permute-start | bytes 1179656 | tf_op jit(solution)/shard_map/ppermute | solution.py:346
  274.2 17.9 %collective-permute-start.59 = (bf16[512,384]{1,0:T(8,128)(2,1)S(1)}, bf16[512,384]{1,0:T(8,128)(2,1)S(1)}, u32[]{:S(2)}, u32[]{:S(2)}) collective-permute-start(bf16[512,384]{1,0:T(8,128)(2,1)S(1)} %copy-done.158), channel_id=1, source_target_pairs={{0,16},{16,0},{1,17},{17,1},{2,18},{18,2},{3,19},{19,3},{4,20},{20... | collective-permute-start | bytes 1179656 | tf_op jit(solution)/shard_map/ppermute | solution.py:346
  274.5 19.1 %collective-permute-start.61 = (bf16[512,384]{1,0:T(8,128)(2,1)}, bf16[512,384]{1,0:T(8,128)(2,1)S(1)}, u32[]{:S(2)}, u32[]{:S(2)}) collective-permute-start(bf16[512,384]{1,0:T(8,128)(2,1)} %get-tuple-element.198), channel_id=1, source_target_pairs={{0,16},{16,0},{1,17},{17,1},{2,18},{18,2},{3,19},{19,3},{4,20},{20... | collective-permute-start | bytes 1179656 | tf_op jit(solution)/shard_map/ppermute | solution.py:346
  277.7 15.9 %collective-permute-start.47 = (bf16[192,384]{1,0:T(8,128)(2,1)S(1)}, bf16[192,384]{1,0:T(8,128)(2,1)}, u32[]{:S(2)}, u32[]{:S(2)}) collective-permute-start(bf16[192,384]{1,0:T(8,128)(2,1)S(1)} %out_grads_1.1), channel_id=1, source_target_pairs={{0,4},{4,0},{8,12},{12,8},{1,5},{5,1},{9,13},{13,9},{2,6},{6,2},{1... | collective-permute-start | bytes 442376 | tf_op jit(solution)/shard_map/ppermute | solution.py:346
  291.5 9.4 %collective-permute-start.48 = (bf16[192,384]{1,0:T(8,128)(2,1)S(1)}, bf16[192,384]{1,0:T(8,128)(2,1)S(1)}, u32[]{:S(2)}, u32[]{:S(2)}) collective-permute-start(bf16[192,384]{1,0:T(8,128)(2,1)S(1)} %out_grads_2.1), channel_id=1, source_target_pairs={{0,8},{4,12},{8,0},{12,4},{1,9},{5,13},{9,1},{13,5},{2,10},{6,14},... | collective-permute-start | bytes 442376 | tf_op jit(solution)/shard_map/ppermute | solution.py:346
  292.1 9.2 %collective-permute-start.49 = (bf16[192,384]{1,0:T(8,128)(2,1)S(1)}, bf16[192,384]{1,0:T(8,128)(2,1)S(1)}, u32[]{:S(2)}, u32[]{:S(2)}) collective-permute-start(bf16[192,384]{1,0:T(8,128)(2,1)S(1)} %out_grads_3.1), channel_id=1, source_target_pairs={{0,12},{4,8},{8,4},{12,0},{1,13},{5,9},{9,5},{13,1},{2,14},{6,10},... | collective-permute-start | bytes 442376 | tf_op jit(solution)/shard_map/ppermute | solution.py:346
  293.6 28.8 %collective-permute-start.36 = (bf16[576,512]{1,0:T(8,128)(2,1)}, bf16[576,512]{1,0:T(8,128)(2,1)}, u32[]{:S(2)}, u32[]{:S(2)}) collective-permute-start(bf16[576,512]{1,0:T(8,128)(2,1)} %get-tuple-element.177.a_ref), channel_id=1, source_target_pairs={{0,16},{16,0},{1,17},{17,1},{2,18},{18,2},{3,19},{19,3},{4,20},{20... | collective-permute-start | bytes 1769480 | tf_op jit(solution)/shard_map/ppermute | solution.py:346
  293.6 29.1 %collective-permute-start.40 = (bf16[576,512]{1,0:T(8,128)(2,1)}, bf16[576,512]{1,0:T(8,128)(2,1)}, u32[]{:S(2)}, u32[]{:S(2)}) collective-permute-start(bf16[576,512]{1,0:T(8,128)(2,1)} %get-tuple-element.179.a_ref), channel_id=1, source_target_pairs={{0,16},{16,0},{1,17},{17,1},{2,18},{18,2},{3,19},{19,3},{4,20},{20... | collective-permute-start | bytes 1769480 | tf_op jit(solution)/shard_map/ppermute | solution.py:346
  298.6 19.2 %collective-permute-start.62 = (bf16[512,384]{1,0:T(8,128)(2,1)}, bf16[512,384]{1,0:T(8,128)(2,1)}, u32[]{:S(2)}, u32[]{:S(2)}) collective-permute-start(bf16[512,384]{1,0:T(8,128)(2,1)} %get-tuple-element.199), channel_id=1, source_target_pairs={{0,16},{16,0},{1,17},{17,1},{2,18},{18,2},{3,19},{19,3},{4,20},{20... | collective-permute-start | bytes 1179656 | tf_op jit(solution)/shard_map/ppermute | solution.py:346
  300.9 34.6 %collective-permute-start.42 = (bf16[576,512]{1,0:T(8,128)(2,1)}, bf16[576,512]{1,0:T(8,128)(2,1)}, u32[]{:S(2)}, u32[]{:S(2)}) collective-permute-start(bf16[576,512]{1,0:T(8,128)(2,1)} %get-tuple-element.180.a_ref), channel_id=1, source_target_pairs={{0,16},{16,0},{1,17},{17,1},{2,18},{18,2},{3,19},{19,3},{4,20},{20... | collective-permute-start | bytes 1769480 | tf_op jit(solution)/shard_map/ppermute | solution.py:346
  301.3 39.0 %collective-permute-start.39 = (bf16[576,384]{1,0:T(8,128)(2,1)}, bf16[576,384]{1,0:T(8,128)(2,1)}, u32[]{:S(2)}, u32[]{:S(2)}) collective-permute-start(bf16[576,384]{1,0:T(8,128)(2,1)} %qkv_grads_1.1), channel_id=1, source_target_pairs={{0,4},{4,0},{8,12},{12,8},{1,5},{5,1},{9,13},{13,9},{2,6},{6,2},{1... | collective-permute-start | bytes 1327112 | tf_op jit(solution)/shard_map/ppermute | solution.py:346
  304.3 23.0 %all-to-all-start.6 = ((bf16[4,48,384]{2,1,0:T(8,128)(2,1)}), bf16[4,48,384]{2,1,0:T(8,128)(2,1)}, u32[]{:S(2)}, u32[]{:S(2)}) async-start(bf16[4,48,384]{2,1,0:T(8,128)(2,1)} %bitcast.179), calls=%async_computation.6 | async-start | bytes 294912 | tf_op jit(solution)/shard_map/all_to_all | solution.py:350
  317.8 106.9 %collective-permute-start.57 = (bf16[768,768]{1,0:T(8,128)(2,1)}, bf16[768,768]{1,0:T(8,128)(2,1)}, u32[]{:S(2)}, u32[]{:S(2)}) collective-permute-start(bf16[768,768]{1,0:T(8,128)(2,1)} %feed_grads_1.1), channel_id=1, source_target_pairs={{0,4},{4,0},{8,12},{12,8},{1,5},{5,1},{9,13},{13,9},{2,6},{6,2},{1... | collective-permute-start | bytes 3538952 | tf_op jit(solution)/shard_map/ppermute | solution.py:346
  322.4 102.3 %collective-permute-start.60 = (bf16[768,768]{1,0:T(8,128)(2,1)}, bf16[768,768]{1,0:T(8,128)(2,1)}, u32[]{:S(2)}, u32[]{:S(2)}) collective-permute-start(bf16[768,768]{1,0:T(8,128)(2,1)} %feed_grads_2.1), channel_id=1, source_target_pairs={{0,8},{4,12},{8,0},{12,4},{1,9},{5,13},{9,1},{13,5},{2,10},{6,14},... | collective-permute-start | bytes 3538952 | tf_op jit(solution)/shard_map/ppermute | solution.py:346
  322.8 102.0 %collective-permute-start.63 = (bf16[768,768]{1,0:T(8,128)(2,1)}, bf16[768,768]{1,0:T(8,128)(2,1)}, u32[]{:S(2)}, u32[]{:S(2)}) collective-permute-start(bf16[768,768]{1,0:T(8,128)(2,1)} %feed_grads_3.1), channel_id=1, source_target_pairs={{0,12},{4,8},{8,4},{12,0},{1,13},{5,9},{9,5},{13,1},{2,14},{6,10},... | collective-permute-start | bytes 3538952 | tf_op jit(solution)/shard_map/ppermute | solution.py:346
  327.4 75.6 %all-to-all-start.2 = ((bf16[4,192,512]{2,1,0:T(8,128)(2,1)}), bf16[4,192,512]{2,1,0:T(8,128)(2,1)}, u32[]{:S(2)}, u32[]{:S(2)}) async-start(bf16[4,192,512]{2,1,0:T(8,128)(2,1)} %bitcast.164), calls=%async_computation.2 | async-start | bytes 1572864 | tf_op jit(solution)/shard_map/all_to_all | solution.py:350
  335.5 67.0 %collective-permute-start.41 = (bf16[576,384]{1,0:T(8,128)(2,1)}, bf16[576,384]{1,0:T(8,128)(2,1)}, u32[]{:S(2)}, u32[]{:S(2)}) collective-permute-start(bf16[576,384]{1,0:T(8,128)(2,1)} %qkv_grads_2.1), channel_id=1, source_target_pairs={{0,8},{4,12},{8,0},{12,4},{1,9},{5,13},{9,1},{13,5},{2,10},{6,14},... | collective-permute-start | bytes 1327112 | tf_op jit(solution)/shard_map/ppermute | solution.py:346
  340.3 62.3 %collective-permute-start.43 = (bf16[576,384]{1,0:T(8,128)(2,1)}, bf16[576,384]{1,0:T(8,128)(2,1)}, u32[]{:S(2)}, u32[]{:S(2)}) collective-permute-start(bf16[576,384]{1,0:T(8,128)(2,1)} %qkv_grads_3.1), channel_id=1, source_target_pairs={{0,12},{4,8},{8,4},{12,0},{1,13},{5,9},{9,5},{13,1},{2,14},{6,10},... | collective-permute-start | bytes 1327112 | tf_op jit(solution)/shard_map/ppermute | solution.py:346
  402.5 17.3 %collective-permute-start.53 = (bf16[512,384]{1,0:T(8,128)(2,1)}, bf16[512,384]{1,0:T(8,128)(2,1)}, u32[]{:S(2)}, u32[]{:S(2)}) collective-permute-start(bf16[512,384]{1,0:T(8,128)(2,1)} %get-tuple-element.186), channel_id=1, source_target_pairs={{0,16},{16,0},{1,17},{17,1},{2,18},{18,2},{3,19},{19,3},{4,20},{20... | collective-permute-start | bytes 1179656 | tf_op jit(solution)/shard_map/ppermute | solution.py:346
  402.5 17.3 %collective-permute-start.54 = (bf16[512,384]{1,0:T(8,128)(2,1)}, bf16[512,384]{1,0:T(8,128)(2,1)}, u32[]{:S(2)}, u32[]{:S(2)}) collective-permute-start(bf16[512,384]{1,0:T(8,128)(2,1)} %get-tuple-element.187), channel_id=1, source_target_pairs={{0,16},{16,0},{1,17},{17,1},{2,18},{18,2},{3,19},{19,3},{4,20},{20... | collective-permute-start | bytes 1179656 | tf_op jit(solution)/shard_map/ppermute | solution.py:346
  404.5 11.2 %all-to-all-start.7 = ((bf16[4,48,384]{2,1,0:T(8,128)(2,1)}), bf16[4,48,384]{2,1,0:T(8,128)(2,1)}, u32[]{:S(2)}, u32[]{:S(2)}) async-start(bf16[4,48,384]{2,1,0:T(8,128)(2,1)} %broadcast_in_dim.16), calls=%async_computation.7 | async-start | bytes 294912 | tf_op jit(solution)/shard_map/all_to_all | solution.py:350
  415.7 15.6 %all-to-all-start.4 = ((bf16[4,144,384]{2,1,0:T(8,128)(2,1)}), bf16[4,144,384]{2,1,0:T(8,128)(2,1)}, u32[]{:S(2)}, u32[]{:S(2)}) async-start(bf16[4,144,384]{2,1,0:T(8,128)(2,1)} %bitcast.174), calls=%async_computation.4 | async-start | bytes 884736 | tf_op jit(solution)/shard_map/all_to_all | solution.py:350
  431.3 30.0 %all-to-all-start.8 = ((bf16[4,192,768]{2,1,0:T(8,128)(2,1)}), bf16[4,192,768]{2,1,0:T(8,128)(2,1)S(1)}, u32[]{:S(2)}, u32[]{:S(2)}) async-start(bf16[4,192,768]{2,1,0:T(8,128)(2,1)} %bitcast.83), calls=%async_computation.8 | async-start | bytes 2359296 | tf_op jit(solution)/shard_map/all_to_all | solution.py:350
  462.1 15.7 %all-to-all-start.5 = ((bf16[4,144,384]{2,1,0:T(8,128)(2,1)}), bf16[4,144,384]{2,1,0:T(8,128)(2,1)S(1)}, u32[]{:S(2)}, u32[]{:S(2)}) async-start(bf16[4,144,384]{2,1,0:T(8,128)(2,1)} %broadcast_in_dim.15), calls=%async_computation.5 | async-start | bytes 884736 | tf_op jit(solution)/shard_map/all_to_all | solution.py:350
  479.6 40.9 %all-to-all-start.9 = ((bf16[4,192,768]{2,1,0:T(8,128)(2,1)}), bf16[4,192,768]{2,1,0:T(8,128)(2,1)}, u32[]{:S(2)}, u32[]{:S(2)}) async-start(bf16[4,192,768]{2,1,0:T(8,128)(2,1)} %broadcast_in_dim.17), calls=%async_computation.9 | async-start | bytes 2359296 | tf_op jit(solution)/shard_map/all_to_all | solution.py:350
  504.0 16.5 %collective-permute-start.34 = (f32[216,128]{1,0:T(8,128)S(1)}, f32[216,128]{1,0:T(8,128)S(1)}, u32[]{:S(2)}, u32[]{:S(2)}) collective-permute-start(f32[216,128]{1,0:T(8,128)S(1)} %add.182), channel_id=1, source_target_pairs={{0,2},{1,3},{2,0},{3,1},{4,6},{5,7},{6,4},{7,5},{8,10},{9,11},{10,... | collective-permute-start | bytes 331784 | tf_op jit(solution)/shard_map/ppermute | solution.py:628
  506.3 14.1 %collective-permute-start.35 = (f32[216,128]{1,0:T(8,128)S(1)}, f32[216,128]{1,0:T(8,128)S(1)}, u32[]{:S(2)}, u32[]{:S(2)}) collective-permute-start(f32[216,128]{1,0:T(8,128)S(1)} %add.182), channel_id=1, source_target_pairs={{0,3},{1,0},{2,1},{3,2},{4,7},{5,4},{6,5},{7,6},{8,11},{9,8},{10,9... | collective-permute-start | bytes 331784 | tf_op jit(solution)/shard_map/ppermute | solution.py:628
  520.5 18.2 %collective-permute-start.44 = (bf16[576,384]{1,0:T(8,128)(2,1)S(1)}, bf16[576,384]{1,0:T(8,128)(2,1)S(1)}, u32[]{:S(2)}, u32[]{:S(2)}) collective-permute-start(bf16[576,384]{1,0:T(8,128)(2,1)S(1)} %bitcast.172), channel_id=1, source_target_pairs={{0,16},{16,0},{1,17},{17,1},{2,18},{18,2},{3,19},{19,3},{4,20},{20... | collective-permute-start | bytes 1327112 | tf_op jit(solution)/shard_map/ppermute | solution.py:346
  520.6 15.2 %all-to-all-start.3 = ((bf16[4,192,512]{2,1,0:T(8,128)(2,1)}), bf16[4,192,512]{2,1,0:T(8,128)(2,1)S(1)}, u32[]{:S(2)}, u32[]{:S(2)}) async-start(bf16[4,192,512]{2,1,0:T(8,128)(2,1)} %bitcast.67), calls=%async_computation.3 | async-start | bytes 1572864 | tf_op jit(solution)/shard_map/all_to_all | solution.py:350
  525.4 14.6 %collective-permute-start.65 = (bf16[768,384]{1,0:T(8,128)(2,1)S(1)}, bf16[768,384]{1,0:T(8,128)(2,1)}, u32[]{:S(2)}, u32[]{:S(2)}) collective-permute-start(bf16[768,384]{1,0:T(8,128)(2,1)S(1)} %get-tuple-element.252), channel_id=1, source_target_pairs={{0,16},{16,0},{1,17},{17,1},{2,18},{18,2},{3,19},{19,3},{4,20},{20... | collective-permute-start | bytes 1769480 | tf_op jit(solution)/shard_map/ppermute | solution.py:346
  528.7 14.8 %collective-permute-start.64 = (bf16[768,384]{1,0:T(8,128)(2,1)S(1)}, bf16[768,384]{1,0:T(8,128)(2,1)}, u32[]{:S(2)}, u32[]{:S(2)}) collective-permute-start(bf16[768,384]{1,0:T(8,128)(2,1)S(1)} %get-tuple-element.253), channel_id=1, source_target_pairs={{0,16},{16,0},{1,17},{17,1},{2,18},{18,2},{3,19},{19,3},{4,20},{20... | collective-permute-start | bytes 1769480 | tf_op jit(solution)/shard_map/ppermute | solution.py:346
  (196 other events, 1560.8 us)

commit v2 on v1

v2 whole, which is shorter than its diff:
```python
import functools

import jax
import jax.numpy as jnp
from jax import lax
from jax.experimental import pallas as pl
from jax.experimental.pallas import tpu as pltpu
from jax.sharding import PartitionSpec as P

eps = 1e-05
gelu_scale = 0.7978845608028654
bf = jnp.bfloat16
f32 = jnp.float32
AUG = 80
TILE = 16


def nn(a, b):
    return lax.dot_general(a, b, (((1,), (0,)), ((), ())), preferred_element_type=f32)


def nt(a, b):
    return lax.dot_general(a, b, (((1,), (1,)), ((), ())), preferred_element_type=f32)


def tn(a, b):
    return lax.dot_general(a, b, (((0,), (0,)), ((), ())), preferred_element_type=f32)


def shape(dims, dtype):
    return jax.ShapeDtypeStruct(tuple(dims), dtype)


def whole(a):
    dims = tuple(a.shape)
    return pl.BlockSpec(dims, lambda *_: (0,) * len(dims))


def lead(count, *dims):
    return pl.BlockSpec((count,) + dims, lambda p, sc: (p,) + (0,) * len(dims))


def run_kernel(body, name, grid, scalars, ins, outs, flops=0, trans=0, scratch=()):
    moved = sum(a.size * jnp.dtype(a.dtype).itemsize for a, _ in ins + outs)
    return pl.pallas_call(
        body,
        out_shape=[o for o, _ in outs],
        grid_spec=pltpu.PrefetchScalarGridSpec(
            num_scalar_prefetch=1,
            grid=grid,
            in_specs=[spec or whole(a) for a, spec in ins],
            out_specs=[spec or whole(o) for o, spec in outs],
            scratch_shapes=list(scratch),
        ),
        compiler_params=pltpu.CompilerParams(vmem_limit_bytes=50 * 2**20),
        cost_estimate=pl.CostEstimate(flops=flops, bytes_accessed=moved, transcendentals=trans),
        name=name,
    )(scalars, *[a for a, _ in ins])


def norm_columns(values):
    center = values - jnp.mean(values, axis=0, keepdims=True)
    inv_std = lax.rsqrt(jnp.mean(center * center, axis=0, keepdims=True) + eps)
    return center * inv_std, inv_std


def norm_columns_back(grad, normed, inv_std, gain):
    scaled = grad * gain
    return inv_std * (
        scaled
        - jnp.mean(scaled, axis=0, keepdims=True)
        - normed * jnp.mean(scaled * normed, axis=0, keepdims=True)
    )


def column(rows, at, width):
    only = jnp.where(lax.broadcasted_iota(jnp.int32, rows.shape, 0) == at, rows.astype(f32), 0.0).astype(bf)
    upright = tn(only, jnp.ones((TILE, 128), bf))
    return jnp.concatenate([upright] * (width // 128), axis=1)


def row_sums(values):
    ones = jnp.ones((8, values.shape[1]), bf)
    if values.dtype == bf:
        return nt(ones, values)
    high = values.astype(bf)
    return nt(ones, high) + nt(ones, (values - high.astype(f32)).astype(bf))


def gelu_pair(up_pre):
    square = up_pre * up_pre
    tanh_value = jnp.tanh(gelu_scale * (up_pre + 0.044715 * square * up_pre))
    half_one = 0.5 * (1.0 + tanh_value)
    slope = half_one + 0.5 * up_pre * (1.0 - tanh_value * tanh_value) * gelu_scale * (
        1.0 + 3.0 * 0.044715 * square
    )
    return up_pre * half_one, slope


def soft_columns(logits):
    top = jnp.exp(logits - jnp.max(logits, axis=0, keepdims=True))
    return top / jnp.sum(top, axis=0, keepdims=True)


def ahead_mask(starts, rows, first_column, columns):
    j = lax.broadcasted_iota(jnp.int32, (rows, columns), 0)
    i = lax.broadcasted_iota(jnp.int32, (rows, columns), 1) + first_column
    return (j <= i) & (j >= starts[0:1, first_column : first_column + columns])


def causal_pieces(tokens):
    step = tokens // 2
    return ((0, step, step), (step, step, tokens))


HBM = pl.BlockSpec(memory_space=pl.ANY)


def load_all(refs, places, sems):
    copies = [pltpu.make_async_copy(ref, place, sems.at[k]) for k, (ref, place) in enumerate(zip(refs, places))]
    for copy in copies:
        copy.start()
    return copies


def part_places(refs, scratch, core):
    return [scratch.at[2 * (k // 2) + (core if k % 2 == 0 else 1 - core)] for k in range(len(refs))]


def pack_body(sc, qkv_ref, qm_ref, km_ref, rows_ref, out_ref, up_ref, down_ref, *outs):
    pc, model = qkv_ref.shape
    hs = qm_ref.shape[1]
    for core, (first_ref, wo_ref, wd_ref, wu_ref) in ((sc[0], outs[0:4]), (1 - sc[0], outs[4:8])):
        cut = pc // 2
        first_ref[0:cut, :] = qkv_ref[pl.ds(pl.multiple_of(core * cut, TILE), cut), :]
        first_ref[cut : cut + hs // 2, :] = jnp.zeros((hs // 2, model), bf)
        for i in range(qm_ref.shape[0] // hs):
            for k in range(2):
                rows = slice(i * hs + k * hs // 2, i * hs + (k + 1) * hs // 2)
                at = k * (model // 2) + 128 * i
                own = jnp.where(core == 0, qm_ref[rows, :].astype(f32), km_ref[rows, :].astype(f32))
                first_ref[cut : cut + hs // 2, at : at + hs] = own.astype(bf)
        first_ref[cut + hs // 2 :, :] = rows_ref[...]
        cut = out_ref.shape[0] // 2
        wo_ref[...] = out_ref[pl.ds(pl.multiple_of(core * cut, TILE), cut), :]
        half = down_ref.shape[0] // 2
        wd_ref[...] = down_ref[pl.ds(pl.multiple_of(core * half, TILE), half), :]
        at = pl.ds(pl.multiple_of(core * half, 128), half)
        wu_ref[:, 0 : model // 2] = up_ref[0 : model // 2, at]
        wu_ref[:, model // 2 :] = up_ref[model // 2 :, at]


def first_norm_body(sc, x_ref, gain_ref, hid_ref):
    normed, _ = norm_columns(x_ref[...].astype(f32))
    width = x_ref.shape[1]
    gains = gain_ref[...]
    hid_ref[...] = (normed * column(gains, 0, width) + column(gains, 1, width)).astype(bf)


def turn_body(sc, a_ref, o_ref):
    o_ref[...] = a_ref[...].T


def map_of(first_ref, at, i, hs, cut):
    model = first_ref.shape[2]
    rows = slice(cut, cut + hs // 2)
    return jnp.concatenate(
        [first_ref[at, rows, k * (model // 2) + 128 * i : k * (model // 2) + 128 * i + hs] for k in range(2)], axis=0
    )


def project_body(hp, hs, nh, sc, hid_ref, starts_ref, *refs):
    first_refs, (proj_ref, qf_ref, kf_ref, va_ref, st_ref, w_ref, sems) = refs[0 : 2 * nh], refs[2 * nh :]
    p = pl.program_id(0)
    wait_for_piece(first_refs, w_ref, sems, sc)
    pc, tokens = proj_ref.shape[1:]
    cut = pc // 2
    bias = column(w_ref[2 * p, cut + hs // 2 :, 0:pc], 0, tokens)
    for k in range(2):
        rows = slice(k * cut, (k + 1) * cut)
        proj_ref[0, rows, :] = (nn(w_ref[2 * p + k, 0:cut, :], hid_ref[...]) + bias[rows, :]).astype(bf)
    included = (starts_ref[0:1, :] == sc[1]).astype(f32)
    extra = lax.broadcasted_iota(jnp.int32, (AUG - hs, tokens), 0)
    extra = jnp.where(extra < 2, 1.0, 0.0).astype(bf)
    for i in range(hp):
        row = 3 * hs * i
        for part, out in ((0, qf_ref), (1, kf_ref)):
            own_map = map_of(w_ref, 2 * p + part, i, hs, cut)
            logits = tn(own_map, proj_ref[0, row + part * hs : row + (part + 1) * hs, :])
            out[i, 0:hs, :] = soft_columns(logits).astype(bf)
            out[i, hs : 2 * hs, :] = soft_columns(-logits).astype(bf)
        va_ref[i, 0:hs, :] = proj_ref[0, row + 2 * hs : row + 3 * hs, :]
        va_ref[i, hs:AUG, :] = extra
        kept = (va_ref[i].astype(f32) * included).astype(bf)
        st_ref[i] = nt(kept, kf_ref[i]).astype(bf)


def wait_for_piece(first_refs, w_ref, sems, sc):
    p = pl.program_id(0)
    places = part_places(first_refs, w_ref, sc[0])
    copies = [pltpu.make_async_copy(ref, place, sems.at[k]) for k, (ref, place) in enumerate(zip(first_refs, places))]

    @pl.when(p == 0)
    def _():
        for copy in copies:
            copy.start()

    for k, copy in enumerate(copies):

        @pl.when(p == k // 2)
        def _(copy=copy):
            copy.wait()


def local_mix_body(hp, sc, qf_ref, kf_ref, va_ref, starts_ref, num_ref):
    tokens = qf_ref.shape[2]
    starts = starts_ref[...]
    for first, width, rows in causal_pieces(tokens):
        mask = ahead_mask(starts, rows, first, width)
        for i in range(hp):
            scores = tn(kf_ref[i, :, 0:rows], qf_ref[i, :, first : first + width])
            scores = jnp.where(mask, scores, 0.0).astype(bf)
            num_ref[i, :, first : first + width] = nn(va_ref[i, :, 0:rows], scores)


def weighted_state(sc, slot, refs, i, hp):
    total = jnp.where(sc[slot + len(refs) - 1] > 0, refs[-1][i].astype(f32), 0.0)
    for m, ref in enumerate(refs[:-1], 1):
        total += jnp.where(sc[slot + m - 1] > 0, ref[((i // hp) ^ m) * hp + i % hp].astype(f32), 0.0)
    return total


def load_out_weight(sc, wo_refs, w_ref, sems):
    rows = wo_refs[0].shape[0]
    places = [
        w_ref.at[pl.ds(pl.multiple_of(rows * (2 * (k // 2) + (sc[0] if k % 2 == 0 else 1 - sc[0])), TILE), rows), :]
        for k in range(len(wo_refs))
    ]
    return load_all(wo_refs, places, sems)


def mix_out_body(hp, hs, nh, sc, num_ref, qf_ref, starts_ref, x_ref, gain_ref, *refs):
    state_refs, row_refs, wo_refs = refs[0:nh], refs[nh : 2 * nh], refs[2 * nh : 4 * nh]
    sin_ref, mixd_ref, mix_ref, res_ref, hidt_ref, hid_ref, w_ref, sems = refs[4 * nh :]
    copies = load_out_weight(sc, wo_refs, w_ref, sems)
    uses = starts_ref[0:1, :] < 0
    model, tokens = x_ref.shape
    for i in range(num_ref.shape[0]):
        state = weighted_state(sc, 2, state_refs, i, hp).astype(bf)
        sin_ref[i] = state
        num = num_ref[i] + jnp.where(uses, nn(state, qf_ref[i]), 0.0)
        mixture = num[0:hs, :] / num[hs : hs + 1, :]
        mixd_ref[i, 0:hs, :] = mixture
        mixd_ref[i, hs : hs + 8, :] = num[hs : hs + 8, :]
        mix_ref[i * hs : (i + 1) * hs, :] = mixture.astype(bf)
    for copy in copies:
        copy.wait()
    res_ref[...] = x_ref[...].astype(f32) + tn(w_ref[...], mix_ref[...])
    width = model // nh
    h = sc[2 + 2 * nh]
    for j in range(nh):
        rows = pl.ds(pl.multiple_of((h ^ j) * width, TILE), width)
        res_ref[rows, :] += column(row_refs[j][:, 0:width], 2, tokens)
    normed, _ = norm_columns(res_ref[...].astype(bf).astype(f32))
    gains = gain_ref[...]
    hidden = (normed * column(gains, 2, tokens) + column(gains, 3, tokens)).astype(bf)
    hidt_ref[...] = hidden
    hid_ref[...] = hidden.T


def feed_body(count, first, sc, hid_ref, gy_ref, *refs):
    row_refs, down_refs, up_refs = refs[0:count], refs[count : 3 * count], refs[3 * count : 5 * count]
    refs = refs[5 * count :]
    if not first:
        out_in, sg_in = refs[0:2]
        refs = refs[2:]
    out_ref, sg_ref, mine_ref, theirs_ref, ub_ref, down_ref, up_ref, bias_ref, sems = refs
    tokens, model = hid_ref.shape
    mh = model // 2
    half = mine_ref.shape[2] // 2
    downs = load_all(down_refs, [down_ref.at[k] for k in range(2 * count)], sems.at[0])
    ups = load_all(up_refs, [up_ref.at[k] for k in range(2 * count)], sems.at[1])
    for k in range(2 * count):
        core = sc[0] if k % 2 == 0 else 1 - sc[0]
        bias_ref[k] = row_refs[k // 2][:, pl.ds(pl.multiple_of(core * half, 128), half)].astype(f32)
    for k in range(2 * count):
        ups[k].wait()
        downs[k].wait()
        bias = bias_ref[k, 1:2, :]
        up_pre = nn(hid_ref[:, 0:mh], up_ref[k, :, 0:mh]) + nn(hid_ref[:, mh:], up_ref[k, :, mh:]) + bias
        value, slope = gelu_pair(up_pre)
        act = value.astype(bf)
        up_grad = (nt(gy_ref[...], down_ref[k]) * slope).astype(bf)
        into = mine_ref if k % 2 == 0 else theirs_ref
        into[k // 2, :, 0:half] = act
        into[k // 2, :, half:] = up_grad
        ub_ref[k // 2, 8 * (k % 2) : 8 * (k % 2) + 8, :] = nn(jnp.ones((8, tokens), bf), up_grad)
        out, left, right = nn(act, down_ref[k]), nt(up_ref[k, :, 0:mh], up_grad), nt(up_ref[k, :, mh:], up_grad)
        if k == 0:
            if not first:
                out, left, right = out + out_in[...], left + sg_in[0:mh, :], right + sg_in[mh:, :]
            out_ref[...] = out
            sg_ref[0:mh, :] = left
            sg_ref[mh:, :] = right
        else:
            out_ref[...] += out
            sg_ref[0:mh, :] += left
            sg_ref[mh:, :] += right


def block_out_body(nh, sc, res_ref, out_ref, *refs):
    row_refs, o_ref, total_ref = refs[0:nh], refs[nh], refs[nh + 1]
    model, tokens = res_ref.shape
    width = model // nh
    total_ref[...] = res_ref[...] + out_ref[...].T
    h = sc[2 + 2 * nh]
    for j in range(nh):
        bias = column(row_refs[j][:, 0 : 2 * width], 2, tokens)[width:, :]
        rows = pl.ds(pl.multiple_of((h ^ j) * width, TILE), width)
        o_ref[h ^ j] = (total_ref[rows, :] + bias).astype(bf)


def second_back_body(hs, nh, sc, sg_ref, res_ref, gyt_ref, gain_ref, mixd_ref, starts_ref, qf_ref, *refs):
    wo_refs, (rg_ref, ag_ref, vec_ref, na_ref, sgt_ref, w_ref, sems) = refs[0 : 2 * nh], refs[2 * nh :]
    copies = load_out_weight(sc, wo_refs, w_ref, sems)
    model, tokens = sg_ref.shape
    width = model // nh
    normed, inv_std = norm_columns(res_ref[...].astype(bf).astype(f32))
    sg = sg_ref[...]
    res_grad = gyt_ref[...].astype(f32) + norm_columns_back(sg, normed, inv_std, column(gain_ref[...], 2, tokens))
    rg_ref[...] = res_grad
    ag_ref[...] = res_grad.astype(bf)
    uses = (starts_ref[0:1, :] < 0).astype(f32)
    for copy in copies:
        copy.wait()
    mg = nn(w_ref[...], ag_ref[...])
    row = lax.broadcasted_iota(jnp.int32, (AUG - hs, tokens), 0)
    for i in range(qf_ref.shape[0]):
        num = mg[i * hs : (i + 1) * hs, :] / mixd_ref[i, hs : hs + 1, :]
        den = -jnp.sum(num * mixd_ref[i, 0:hs, :], axis=0, keepdims=True)
        high = den.astype(bf).astype(f32)
        extra = jnp.where(row == 0, high, jnp.where(row == 1, den - high, 0.0))
        na_ref[i, 0:hs, :] = num.astype(bf)
        na_ref[i, hs:AUG, :] = extra.astype(bf)
        kept = (na_ref[i].astype(f32) * uses).astype(bf)
        sgt_ref[i] = nt(kept, qf_ref[i]).astype(bf)
    for at, value in enumerate((sg * normed, sg, ag_ref[...], gyt_ref[...])):
        sums = row_sums(value)
        for p in range(nh):
            vec_ref[p, at : at + 1, :] = sums[0:1, p * width : (p + 1) * width]


def halves_back(feat, grad, hs):
    parts = []
    for k in range(2):
        soft = feat[k * hs : (k + 1) * hs, :].astype(f32)
        own = grad[k * hs : (k + 1) * hs, :]
        weight = jnp.sum(soft * own, axis=0, keepdims=True) / jnp.sum(soft, axis=0, keepdims=True)
        parts.append(soft * (own - weight))
    return (parts[0] - parts[1]).astype(bf)


def local_back_body(hp, hs, sc, qf_ref, kf_ref, va_ref, na_ref, sin_ref, starts_ref, ql_ref, kfg_ref, vg_ref):
    tokens = qf_ref.shape[2]
    starts = starts_ref[...]
    step = tokens // 2
    uses = starts[0:1, :] < 0
    masks = [ahead_mask(starts, rows, first, width) for first, width, rows in causal_pieces(tokens)]
    for i in range(hp):
        na = na_ref[i]
        through = tn(sin_ref[i], na)
        for which, (first, width, rows) in enumerate(causal_pieces(tokens)):
            at = slice(first, first + width)
            mask = masks[which]
            scores = jnp.where(mask, tn(kf_ref[i, :, 0:rows], qf_ref[i, :, at]), 0.0).astype(bf)
            sgrad = jnp.where(mask, tn(va_ref[i, :, 0:rows], na[:, at]), 0.0).astype(bf)
            qfg = nn(kf_ref[i, :, 0:rows], sgrad) + jnp.where(uses[:, at], through[:, at], 0.0)
            ql_ref[i, :, at] = halves_back(qf_ref[i, :, at], qfg, hs)
            kfg = nt(qf_ref[i, :, at], sgrad)
            vg = nt(na[:, at], scores)[0:hs, :]
            if which == 0:
                kfg_ref[i, :, 0:rows] = kfg
                vg_ref[i, :, 0:rows] = vg
            else:
                kfg_ref[i, :, 0:step] += kfg[:, 0:step]
                vg_ref[i, :, 0:step] += vg[:, 0:step]
                kfg_ref[i, :, step:] = kfg[:, step:]
                vg_ref[i, :, step:] = vg[:, step:]


def join_extra(state, hs):
    row = lax.broadcasted_iota(jnp.int32, state.shape, 0)
    both = state[hs : hs + 1, :] + state[hs + 1 : hs + 2, :]
    return jnp.where(row < hs, state, jnp.where(row == hs, both, 0.0))


def project_back_body(hp, hs, nh, sc, *refs):
    state_refs, first_refs, refs = refs[0:nh], refs[nh : 3 * nh], refs[3 * nh :]
    kf_ref, va_ref, ql_ref, kfg_ref, vg_ref, proj_ref, starts_ref, pg_ref, fg_ref, mg_ref, pb_ref, first_ref, sems = refs
    p = pl.program_id(0)
    wait_for_piece(first_refs, first_ref, sems, sc)
    included = starts_ref[0:1, :] == sc[1]
    cut = pg_ref.shape[1] // 2
    for i in range(hp):
        total = jnp.where(sc[1 + 2 * nh] > 0, state_refs[-1][i].astype(f32), 0.0)
        for m in range(1, nh):
            total += jnp.where(sc[1 + nh + m] > 0, state_refs[m - 1][i].astype(f32), 0.0)
        state = join_extra(total, hs).astype(bf)
        kfg = kfg_ref[i] + jnp.where(included, tn(state, va_ref[i]), 0.0)
        vg = vg_ref[i] + jnp.where(included, nn(state, kf_ref[i])[0:hs, :], 0.0)
        klg = halves_back(kf_ref[i], kfg, hs)
        qlg = ql_ref[i]
        row = 3 * hs * i
        pg_ref[0, row : row + hs, :] = nn(map_of(first_ref, 2 * p, i, hs, cut), qlg).astype(bf)
        pg_ref[0, row + hs : row + 2 * hs, :] = nn(map_of(first_ref, 2 * p + 1, i, hs, cut), klg).astype(bf)
        pg_ref[0, row + 2 * hs : row + 3 * hs, :] = vg.astype(bf)
        q_grad = nt(proj_ref[0, row : row + hs, :], qlg)
        k_grad = nt(proj_ref[0, row + hs : row + 2 * hs, :], klg)
        mg_ref[0, :, 128 * i : 128 * (i + 1)] = jnp.concatenate([q_grad, k_grad], axis=1)
    pb_ref[0] = row_sums(pg_ref[0])
    grad = tn(first_ref[2 * p, 0:cut, :], pg_ref[0, 0:cut, :]) + tn(first_ref[2 * p + 1, 0:cut, :], pg_ref[0, cut:, :])

    @pl.when(pl.program_id(0) == 0)
    def _():
        fg_ref[...] = grad

    @pl.when(pl.program_id(0) > 0)
    def _():
        fg_ref[...] += grad


def first_back_body(nh, sc, fg_ref, x_ref, rg_ref, gain_ref, tg_ref, vec_ref):
    model, tokens = fg_ref.shape
    width = model // nh
    normed, inv_std = norm_columns(x_ref[...].astype(f32))
    fg = fg_ref[...]
    gain = column(gain_ref[...], 0, tokens)
    tg = (rg_ref[...] + norm_columns_back(fg, normed, inv_std, gain)).astype(bf)
    for p in range(nh):
        tg_ref[p] = tg[p * width : (p + 1) * width, :]
    for at, value in enumerate((fg * normed, fg)):
        sums = row_sums(value)
        for p in range(nh):
            vec_ref[p, at : at + 1, :] = sums[0:1, p * width : (p + 1) * width]


def up_grads_body(nh, sc, hidt_ref, hidt2_ref, early_ref, late_ref, early2_ref, late2_ref, *o_refs):
    for j in range(nh):
        own, peer, k = (early_ref, early2_ref, j) if j < nh - 1 else (late_ref, late2_ref, 0)
        o_refs[j][...] = (nn(hidt_ref[...], own[k]) + nn(hidt2_ref[...], peer[k])).astype(bf)


def down_grads_body(nh, sc, gyt_ref, gyt2_ref, early_ref, late_ref, early2_ref, late2_ref,
                    mix_ref, mix2_ref, ag_ref, ag2_ref, *o_refs):
    model = gyt_ref.shape[0]
    width = model // nh
    for j in range(nh):
        own, peer, k = (early_ref, early2_ref, j) if j < nh - 1 else (late_ref, late2_ref, 0)
        o_refs[j][0:model, :] = (nn(gyt_ref[...], own[k]) + nn(gyt2_ref[...], peer[k])).astype(bf)
        rows = slice(j * width, (j + 1) * width)
        o_refs[j][model:, :] = (nt(mix_ref[rows, :], ag_ref[...]) + nt(mix2_ref[rows, :], ag2_ref[...])).astype(bf)


def last_grads_body(nh, sc, pg_ref, pg2_ref, hid_ref, hid2_ref, mg_ref, pb_ref, early_ref, late_ref, vec1_ref, vec2_ref,
                    *refs):
    o_refs, rows_ref = refs[0:nh], refs[nh]
    pc, half = pg_ref.shape[1], hid_ref.shape[0]
    hs = mg_ref.shape[1]
    width = vec1_ref.shape[2]
    h = sc[2 + 2 * nh]
    for j in range(nh):
        o_ref = o_refs[j]
        o_ref[0:pc, :] = (nt(pg_ref[j], hid_ref[...]) + nt(pg2_ref[j], hid2_ref[...])).astype(bf)
        o_ref[pc : pc + hs, :] = mg_ref[j].astype(bf)
        ub_ref, k = (early_ref, j) if j < nh - 1 else (late_ref, 0)
        first = jnp.where(sc[0] == 0, ub_ref[k, 0:1, :], ub_ref[k, 8:9, :])
        second = jnp.where(sc[0] == 0, ub_ref[k, 8:9, :], ub_ref[k, 0:1, :])
        rows_ref[...] = jnp.zeros_like(rows_ref)
        rows_ref[0:1, :] = pb_ref[j, 0:1, 0:half]
        rows_ref[1:2, 0 : pc - half] = pb_ref[j, 0:1, half:]
        rows_ref[2:3, :] = first
        rows_ref[3:4, :] = second
        rows_ref[4:8, 0:width] = vec2_ref[h ^ j, 0:4, :]
        rows_ref[8:10, 0:width] = vec1_ref[h ^ j, 0:2, :]
        o_ref[pc + hs :, :] = rows_ref[...].astype(bf)


def side_by_side_body(sc, mine_ref, theirs_ref, o_ref):
    half = mine_ref.shape[1]
    o_ref[:, pl.ds(pl.multiple_of(sc[0] * half, 128), half)] = mine_ref[...].astype(f32)
    o_ref[:, pl.ds(pl.multiple_of((1 - sc[0]) * half, 128), half)] = theirs_ref[...].astype(f32)


def down_out_body(sc, mine_ref, theirs_ref, down_ref, out_ref):
    model = down_ref.shape[1]
    half = mine_ref.shape[1]
    for core, ref in ((sc[0], mine_ref), (1 - sc[0], theirs_ref)):
        at = pl.ds(pl.multiple_of(core * half, 128), half)
        down_ref[at, :] = ref[0:model, :].astype(f32).T
        out_ref[:, at] = ref[model:, :].astype(f32)


def last_out_body(hs, sc, mine_ref, theirs_ref, qkv_ref, qm_ref, km_ref, rows_ref):
    pc = qkv_ref.shape[0]
    half = mine_ref.shape[1]
    for core, ref in ((sc[0], mine_ref), (1 - sc[0], theirs_ref)):
        at = pl.ds(pl.multiple_of(core * half, 128), half)
        qkv_ref[:, at] = ref[0:pc, :].astype(f32)
    maps = mine_ref[pc : pc + hs, :].astype(f32) + theirs_ref[pc : pc + hs, :].astype(f32)
    for i in range(qm_ref.shape[0]):
        qm_ref[i] = maps[:, 128 * i : 128 * i + hs]
        km_ref[i] = maps[:, 128 * i + hs : 128 * i + 2 * hs]
    rows = slice(pc + hs, pc + hs + TILE)
    rows_ref[...] = mine_ref[rows, :].astype(f32) + theirs_ref[rows, :].astype(f32)


def swap(a, axis, k):
    n = lax.axis_size(axis)
    return lax.ppermute(a, axis, [(i, i ^ k) for i in range(n)])


def trade(a, axis):
    return lax.all_to_all(a, axis, 0, 0, tiled=True)


def after(a, *others):
    return lax.optimization_barrier((a,) + others)[0]


def chain_seq(part, forward, weight_of):
    n = lax.axis_size("seq")
    total = None
    for k in range(1, n):
        pairs = [(i, i + k) if forward else (i + k, i) for i in range(n - k)]
        if n == 2:
            return lax.ppermute(part, "seq", pairs)
        sent = part if forward else part * weight_of(k).astype(part.dtype)
        got = lax.ppermute(sent, "seq", pairs).astype(f32) * (weight_of(k) if forward else 1.0)
        total = got if total is None else total + got
    return total.astype(bf)


def local(tokens, attn_gain, attn_shift, qkv_weight, qkv_bias, query_map, key_map, out_weight, out_bias,
          mlp_gain, mlp_shift, up_weight, up_bias, down_weight, down_bias, positions, out_grad):
    nh, ns, nz = lax.axis_size("head"), lax.axis_size("seq"), lax.axis_size("dp")
    length, width = tokens.shape[1], tokens.shape[2]
    model = width * nh
    half = model // 2
    hp, hs = query_map.shape[0], query_map.shape[1]
    heads = hp * nh
    pc = qkv_weight.shape[1]
    hidden = up_weight.shape[1]
    hh = hidden // 2
    tok = length // nh
    h = lax.axis_index("head")
    s2 = lax.axis_index("seq") % 2
    peers = range(1, nh)

    run = positions[0]
    start_of = jnp.arange(length, dtype=jnp.int32) - run
    chunk_starts = lax.dynamic_slice_in_dim(start_of, h * tok, tok, 0) - h * tok
    starts = jnp.broadcast_to(chunk_starts[None, :], (8, tok))
    firsts = start_of[::tok]
    run_last = start_of[length - 1]
    other = [h ^ m for m in range(nh)]
    fwd = [(other[m] < h) & (firsts[h] <= (other[m] + 1) * tok - 1) for m in peers]
    bwd = [(other[m] > h) & (firsts[other[m]] <= (h + 1) * tok - 1) for m in peers]
    sc = jnp.stack(
        [s2, chunk_starts[tok - 1]]
        + [a.astype(jnp.int32) for a in fwd]
        + [(firsts[h] < 0).astype(jnp.int32)]
        + [a.astype(jnp.int32) for a in bwd]
        + [(run_last <= (h + 1) * tok - 1).astype(jnp.int32), h]
    ).astype(jnp.int32)

    def to_chunks(a):
        a = a[0].T.reshape(width, nh, tok).transpose(1, 0, 2)
        return trade(a, "head").reshape(model, tok)

    def to_runs(a):
        return trade(a, "head").transpose(1, 0, 2).reshape(width, length).T[None]

    own_rows = jnp.stack(
        [jnp.pad(qkv_bias, (0, model - pc)), jnp.pad(up_bias, (0, model - hidden)),
         jnp.pad(jnp.concatenate([out_bias, down_bias]), (0, model - 2 * width))]
    )
    own_rows = jnp.pad(own_rows, ((0, TILE - 3), (0, 0)))
    gains = jnp.pad(jnp.stack([attn_gain, attn_shift, mlp_gain, mlp_shift]), ((0, TILE - 4), (0, 0)))
    fr = pc // 2 + hs // 2 + TILE
    parts = [shape((fr, model), bf), shape((width // 2, model), bf), shape((hh, model), bf), shape((hh, model), bf)]
    packed = run_kernel(
        pack_body, "pack_weights", (1,), sc,
        [(a, None) for a in (qkv_weight.T, query_map.reshape(-1, hs), key_map.reshape(-1, hs), own_rows, out_weight,
                             up_weight, down_weight)],
        [(a, None) for a in parts * 2],
    )
    x = to_chunks(tokens)

    def halves(own, other, arrived):
        return [[own, other]] + [[a, swap(a, "seq", 1)] for a in arrived]

    first_got = [swap(packed[0], "head", m) for m in peers]
    first = halves(packed[0], packed[4], first_got)
    wo_own = after(packed[1], *first_got)
    wo_got = [swap(wo_own, "head", m) for m in peers]
    wo = halves(packed[1], packed[5], wo_got)
    all_first = [a for pair in first for a in pair]
    all_wo = [a for pair in wo for a in pair]
    row_specs = [(pair[0], pl.BlockSpec((TILE, model), lambda *_: (fr // TILE - 1, 0))) for pair in first]
    in_hbm = lambda arrays: [(a, HBM) for a in arrays]
    first_scratch = [pltpu.VMEM((2 * nh, fr, model), bf), pltpu.SemaphoreType.DMA((2 * nh,))]
    wo_scratch = [pltpu.VMEM((model, model), bf), pltpu.SemaphoreType.DMA((2 * nh,))]

    (hid,) = run_kernel(first_norm_body, "first_norm", (1,), sc, [(x, None), (gains, None)], [(shape((model, tok), bf), None)])
    va_spec, state_spec, feat_spec = lead(hp, AUG, tok), lead(hp, AUG, 2 * hs), lead(hp, 2 * hs, tok)
    feat = (shape((heads, 2 * hs, tok), bf), feat_spec)
    proj, qf, kf, va, states = run_kernel(
        functools.partial(project_body, hp, hs, nh), "project", (nh,), sc,
        [(hid, None), (starts, None)] + in_hbm(all_first),
        [(shape((nh, pc, tok), bf), lead(1, pc, tok)), feat, feat,
         (shape((heads, AUG, tok), bf), va_spec), (shape((heads, AUG, 2 * hs), bf), state_spec)],
        flops=nh * (2 * model * pc * tok + 4 * pc * hs * tok), trans=4 * heads * hs * tok, scratch=first_scratch,
    )
    pair_flops = 2 * heads * tok * tok * 3 // 4
    (num,) = run_kernel(
        functools.partial(local_mix_body, hp), "local_mix", (nh,), sc,
        [(qf, feat_spec), (kf, feat_spec), (va, va_spec), (starts, None)],
        [(shape((heads, AUG, tok), f32), va_spec)], flops=pair_flops * (2 * hs + AUG),
    )
    around = [after(swap(states, "head", m), num) for m in peers]

    def to_own_pieces(a, m):
        a = a.reshape(nh, hp, AUG, 2 * hs)
        return jnp.stack([a[j ^ m] for j in range(nh)]).reshape(heads, AUG, 2 * hs)

    ends_in = [(run_last <= (other[m] + 1) * tok - 1).astype(f32) for m in range(nh)]
    whole_run = sum(to_own_pieces(a, m).astype(f32) * ends_in[m] for m, a in enumerate([states] + around)).astype(bf)
    before = chain_seq(whole_run, True, lambda k: (start_of[0] <= -(k - 1) * length - 1).astype(f32))

    down_own, up_own = after(packed[2], *wo_got), after(packed[3], *wo_got)
    down_got, up_got = {1: swap(down_own, "head", 1)}, {2: swap(up_own, "head", 2)}
    down_late, up_late = after(down_own, states), after(up_own, states)
    down_got[2] = swap(down_late, "head", 2)
    up_got[1] = swap(up_late, "head", 1)
    down_got[3] = swap(after(down_got[1], num), "head", 2)
    up_got[3] = swap(after(up_got[2], num), "head", 1)
    down = halves(packed[2], packed[6], [down_got[m] for m in peers])
    up = halves(packed[3], packed[7], [up_got[m] for m in peers])
    gyt = to_chunks(out_grad)

    sin, mixd, mix, res, hidt2, hid2 = run_kernel(
        functools.partial(mix_out_body, hp, hs, nh), "mix_out", (1,), sc,
        [(a, None) for a in (num, qf, starts, x, gains, *around, before)] + row_specs + in_hbm(all_wo),
        [(shape((heads, AUG, 2 * hs), bf), None), (shape((heads, hs + 8, tok), f32), None), (shape((model, tok), bf), None),
         (shape((model, tok), f32), None), (shape((model, tok), bf), None), (shape((tok, model), bf), None)],
        flops=2 * model * model * tok + 2 * heads * AUG * 2 * hs * tok, scratch=wo_scratch,
    )
    hidt2_peer, gyt_peer, mix_peer = swap(hidt2, "seq", 1), swap(gyt, "seq", 1), swap(mix, "seq", 1)
    hid_peer = swap(lax.dynamic_slice_in_dim(hid, (1 - s2) * half, half, 0), "seq", 1)

    (gy,) = run_kernel(turn_body, "turn_grad", (1,), sc, [(gyt, None)], [(shape((tok, model), bf), None)])

    def feed(which, sums):
        count = len(which)
        return run_kernel(
            functools.partial(feed_body, count, not sums), f"feed_{which[0]}", (1,), sc,
            [(hid2, None), (gy, None)] + [row_specs[j] for j in which]
            + in_hbm([a for j in which for a in down[j]]) + in_hbm([a for j in which for a in up[j]])
            + [(a, None) for a in sums],
            [(shape((tok, model), f32), None), (shape((model, tok), f32), None), (shape((count, tok, hidden), bf), None),
             (shape((count, tok, hidden), bf), None), (shape((count, TILE, hh), f32), None)],
            flops=count * 8 * model * hidden * tok, trans=count * hidden * tok,
            scratch=[pltpu.VMEM((2 * count, hh, model), bf), pltpu.VMEM((2 * count, hh, model), bf),
                     pltpu.VMEM((2 * count, TILE, hh), f32), pltpu.SemaphoreType.DMA((2, 2 * count))],
        )

    part_out, part_sg, early, early_theirs, early_ub = feed(list(range(nh - 1)), ())
    early_peer = swap(early_theirs, "seq", 1)
    mlp_out, sg, late, late_theirs, late_ub = feed([nh - 1], (part_out, part_sg))
    late_peer = swap(late_theirs, "seq", 1)
    run_block = (shape((nh, width, tok), bf), None)
    (bo,) = run_kernel(
        functools.partial(block_out_body, nh), "block_out", (1,), sc,
        [(res, None), (mlp_out, None)] + row_specs, [run_block], scratch=[pltpu.VMEM((model, tok), f32)],
    )

    vec_block = (shape((nh, 8, width), f32), None)
    rg, ag, vec2, na, sgt = run_kernel(
        functools.partial(second_back_body, hs, nh), "second_back", (1,), sc,
        [(a, None) for a in (sg, res, gyt, gains, mixd, starts, qf)] + in_hbm(all_wo),
        [(shape((model, tok), f32), None), (shape((model, tok), bf), None), vec_block,
         (shape((heads, AUG, tok), bf), None), (shape((heads, AUG, 2 * hs), bf), None)],
        flops=2 * model * model * tok + 2 * heads * AUG * 2 * hs * tok, scratch=wo_scratch,
    )
    g_sent = [swap(sgt, "head", m) for m in peers]
    ag_peer = swap(lax.dynamic_slice_in_dim(ag, (1 - s2) * half, half, 0), "seq", 1)
    def over_head(own, got):
        total = sum(a.astype(f32) for a in got) + own.astype(f32)
        base = total
        for k in range(1, ns // 2):
            total += lax.ppermute(base, "seq", [(i, (i + 2 * k) % ns) for i in range(ns)])
        return total.astype(bf)

    def over_dp(total):
        total = (total.astype(f32) + swap(total, "dp", 1).astype(f32)).astype(bf)
        across = lax.ppermute(total, "dp", [(1, 2), (2, 1)])
        total = (total.astype(f32) + across.astype(f32)).astype(bf)
        out = lax.ppermute(total, "dp", [(1, 0), (2, 3)])
        z = lax.axis_index("dp")
        return jnp.where((z == 1) | (z == 2), total, out)

    def over_dp_traded(total):
        rows = total.shape[0] // nz
        own = trade(total.reshape(nz, rows, -1), "dp").astype(f32).sum(0).astype(bf)
        return trade(jnp.broadcast_to(own[None], (nz,) + own.shape), "dp").reshape(total.shape)

    def both_halves(a):
        return a, swap(a, "seq", 1)

    def columns_of(a, at):
        return (a, pl.BlockSpec((a.shape[0], tok, hh), lambda p, sc: (0, 0, at)))

    half_spec = pl.BlockSpec((half, tok), lambda p, sc: (sc[0], 0))
    up_parts = run_kernel(
        functools.partial(up_grads_body, nh), "up_grads", (1,), sc,
        [(hidt2, None), (hidt2_peer, None)] + [columns_of(a, 1) for a in (early, late, early_peer, late_peer)],
        [(shape((model, hh), bf), None)] * nh, flops=nh * 2 * model * hidden * tok,
    )
    up_got = [swap(up_parts[m], "head", m) for m in peers]
    down_parts = run_kernel(
        functools.partial(down_grads_body, nh), "down_grads", (1,), sc,
        [(gyt, None), (gyt_peer, None)] + [columns_of(a, 0) for a in (early, late, early_peer, late_peer)]
        + [(mix, None), (mix_peer, None), (ag, half_spec), (ag_peer, None)],
        [(shape((model + width, hh), bf), None)] * nh, flops=nh * 2 * model * (hidden + width) * tok,
    )

    down_got_sum = [swap(down_parts[m], "head", m) for m in peers]

    g_around = [after(a, up_parts[0], down_parts[0]) for a in g_sent]
    begins_in = [(firsts[other[m]] < 0).astype(f32) for m in range(nh)]
    g_whole = sum(to_own_pieces(a, m).astype(f32) * begins_in[m] for m, a in enumerate([sgt] + g_around)).astype(bf)
    after_run = chain_seq(g_whole, False, lambda k: (start_of[0] <= -(k - 1) * length - 1).astype(f32))
    na_late = after(na, g_whole)
    ql, kfg, vg = run_kernel(
        functools.partial(local_back_body, hp, hs), "local_back", (nh,), sc,
        [(qf, feat_spec), (kf, feat_spec), (va, va_spec), (na_late, va_spec), (sin, state_spec), (starts, None)],
        [(shape((heads, hs, tok), bf), lead(hp, hs, tok)), (shape((heads, 2 * hs, tok), f32), feat_spec),
         (shape((heads, hs, tok), f32), lead(hp, hs, tok))],
        flops=pair_flops * (6 * hs + 3 * AUG),
    )

    def peer_states(a, m):
        return (a, pl.BlockSpec((hp, AUG, 2 * hs), lambda p, sc: (p ^ m, 0, 0)))

    pg, fg, map_grads, pb = run_kernel(
        functools.partial(project_back_body, hp, hs, nh), "project_back", (nh,), sc,
        [peer_states(a, m) for a, m in zip(g_around + [after_run], [*peers, 0])] + in_hbm(all_first)
        + [(kf, feat_spec), (va, va_spec), (ql, lead(hp, hs, tok)), (kfg, feat_spec), (vg, lead(hp, hs, tok)),
           (proj, lead(1, pc, tok)), (starts, None)],
        [(shape((nh, pc, tok), bf), lead(1, pc, tok)), (shape((model, tok), f32), None),
         (shape((nh, hs, 128 * hp), f32), lead(1, hs, 128 * hp)), (shape((nh, 8, pc), f32), lead(1, 8, pc))],
        flops=nh * (2 * model * pc * tok + 12 * pc * hs * tok), scratch=first_scratch,
    )
    pg_peer = swap(pg, "seq", 1)
    up_mid = over_head(after(up_parts[0], pg), up_got)
    tg, vec1 = run_kernel(
        functools.partial(first_back_body, nh), "first_back", (1,), sc,
        [(after(fg, up_mid), None), (x, None), (rg, None), (gains, None)], [run_block, vec_block],
    )
    tokens_grad = to_runs(tg)
    block_out = to_runs(bo)
    last_rows = -(-(pc + hs + TILE) // (nz * TILE)) * nz * TILE
    last_parts = run_kernel(
        functools.partial(last_grads_body, nh), "last_grads", (1,), sc,
        [(pg, None), (pg_peer, None), (hid, half_spec), (hid_peer, None)]
        + [(a, None) for a in (map_grads, pb, early_ub, late_ub, vec1, vec2)],
        [(shape((last_rows, half), bf), None)] * nh, flops=nh * 2 * model * pc * tok,
        scratch=[pltpu.VMEM((last_rows - pc - hs, half), f32)],
    )

    up_sum = both_halves(over_dp(up_mid))
    down_sum = both_halves(over_dp(over_head(after(down_parts[0], *last_parts), down_got_sum)))
    last_mid = over_head(last_parts[0], [swap(last_parts[m], "head", m) for m in peers])
    last_sum = both_halves(over_dp_traded(last_mid))
    (upweight_grad,) = run_kernel(
        side_by_side_body, "up_result", (1,), sc, [(a, None) for a in up_sum], [(shape((model, hidden), f32), None)]
    )
    downweight_grad, outweight_grad = run_kernel(
        down_out_body, "down_result", (1,), sc, [(a, None) for a in down_sum],
        [(shape((hidden, model), f32), None), (shape((width, model), f32), None)],
    )
    qkv_grad, query_grad, key_grad, rows = run_kernel(
        functools.partial(last_out_body, hs), "last_result", (1,), sc, [(a, None) for a in last_sum],
        [(shape((pc, model), f32), None), (shape((hp, hs, hs), f32), None), (shape((hp, hs, hs), f32), None),
         (shape((TILE, half), f32), None)],
    )
    qkvbias_grad = jnp.concatenate([rows[0], rows[1, 0 : pc - half]])
    upbias_grad = jnp.concatenate([rows[2], rows[3]])
    vec = rows[4:10, 0:width]
    return (block_out, tokens_grad, vec[4], vec[5], qkv_grad.T, qkvbias_grad, query_grad, key_grad,
            outweight_grad, vec[2], vec[0], vec[1], upweight_grad, upbias_grad, downweight_grad, vec[3])


def solution(mesh):
    wide = P("dp", "seq", "head")
    return jax.shard_map(
        local,
        mesh=mesh,
        in_specs=(wide, P(), P(), P(None, "head"), P("head"), P("head", None, None), P("head", None, None),
                  P("head", None), P("head"), P(), P(), P(None, "head"), P("head"), P("head", None), P("head"),
                  P("dp", "seq"), wide),
        out_specs=(wide, wide, P("head"), P("head"), P(None, "head"), P("head"), P("head", None, None),
                   P("head", None, None), P("head", None), P("head"), P("head"), P("head"), P(None, "head"), P("head"),
                   P("head", None), P("head")),
        check_vma=False,
    )
```

time: 558 us -> 449 us (0.80)
  local copies, waits for them, and re-layouts: 99.2 us -> 37.1 us
  starting transfers between devices: 102 us -> 73 us
  other arithmetic: 30.1 us -> 18.5 us
  waiting for transfers between devices: 177 us -> 167 us
  Pallas kernels: 125 us -> 134 us
    all_to_all x10 -> x6, waiting for transfers between devices: 46.1 us -> 21.6 us  [trade(): return lax.all_to_all(a, axis, 0, 0, tiled=True)]
    unnamed x372 -> x146, local copies, waits for them, and re-layouts: 46.6 us -> 23.5 us
    ppermute x60 -> x52, waiting for transfers between devices: 119 us -> 136 us  [swap(): return lax.ppermute(a, axis, [(i, i ^ k) for i in range(n)])]
    slice x34 -> x10, local copies, waits for them, and re-layouts: 21.1 us -> 4.16 us  [the longest x7 2.9 us: to_own_pieces(): return jnp.stack([a[j ^ m] for j in range(nh)]).reshape(heads, AUG, 2 * hs)]
    all_to_all x10 -> x6, starting transfers between devices: 40.2 us -> 24.1 us  [trade(): return lax.all_to_all(a, axis, 0, 0, tiled=True)]
    ppermute x60 -> x52, starting transfers between devices: 51.6 us -> 39.2 us  [swap(): return lax.ppermute(a, axis, [(i, i ^ k) for i in range(n)])]
    pallas_call x38 -> x19, Pallas kernels: 125 us -> 134 us  [run_kernel(): pl.pallas_call(body, out_shape=[o for o, _ in outs], grid_spec=pltpu.Pref...]
    convert_element_type x8 -> x0, local copies, waits for them, and re-layouts: 7.71 us -> none  [the longest x4 4.67 us: local(): up_rows = [a[pc:pc + hidden].astype(f32)[None, :] for a in flat]]
  transfers between devices with their start and end apart: 76 -> 64, of which waited for: 20 -> 21; matrix products, arithmetic and copies ran while one was open for 14% -> 6% of each run, Pallas kernels for 23% -> 20%
where the time goes in v2:
time: 449 us; the launch traced here: 440 us
  waiting for transfers between devices  167 us (37%)
  Pallas kernels  134 us (30%)
  starting transfers between devices  73 us (16%)
  local copies, waits for them, and re-layouts  37.1 us (8%)
  other arithmetic  18.5 us (4%)
  between operations  10.8 us (2%)
    ppermute x52, waiting for transfers between devices, swap(): return lax.ppermute(a, axis, [(i, i ^ k) for i in range(n)])  136 us
    pallas_call x19, Pallas kernels, run_kernel(): pl.pallas_call(body, out_shape=[o for o, _ in outs], grid_spec=pltpu.Pref...  134 us
    ppermute x52, starting transfers between devices, swap(): return lax.ppermute(a, axis, [(i, i ^ k) for i in range(n)])  39.2 us
    all_to_all x6, starting transfers between devices, trade(): return lax.all_to_all(a, axis, 0, 0, tiled=True)  24.1 us
    unnamed x146, local copies, waits for them, and re-layouts  23.5 us
    all_to_all x6, waiting for transfers between devices, trade(): return lax.all_to_all(a, axis, 0, 0, tiled=True)  21.6 us
  transfers between devices with their start and end apart: 64, of which 21 were waited for; matrix products, arithmetic and copies ran while one was open for 6% of the time, Pallas kernels for 20%

profile of v2, /device:TPU:0, one launch (start us, length us, event | category | flops | bytes accessed | tf_op | source)
XLA Modules:
  0.0 439.8 jit_solution(73164912104176087)
XLA Ops:
  14.1 3.7 pack_weights.1
  20.9 2.9 collective-permute-start
  23.9 1.5 collective-permute-start.2
  26.4 4.2 all-to-all-start
  30.6 5.9 %collective-permute-done.refs_2_.refs_5_.refs_1_.refs_6_ = bf16[336,768]{1,0:T(8,128)(2,1)S(1)} collective-permute-done((bf16[336,768]{1,0:T(8,128)(2,1)S(1)}, bf16[336,768]{1,0:T(8,128)(2,1)S(1)}, u32[]{:S(2)}, u32[]{:S(2)}) %collective-permute-start) | collective-permute-done | bytes 516128 | tf_op jit(solution)/shard_map/ppermute | solution.py:519
  36.5 17.4 %collective-permute-done.2.refs_4_.refs_6_.refs_2_.refs_8_ = bf16[336,768]{1,0:T(8,128)(2,1)S(1)} collective-permute-done((bf16[336,768]{1,0:T(8,128)(2,1)S(1)}, bf16[336,768]{1,0:T(8,128)(2,1)S(1)}, u32[]{:S(2)}, u32[]{:S(2)}) %collective-permute-start.2) | collective-permute-done | bytes 516128 | tf_op jit(solution)/shard_map/ppermute | solution.py:519
  54.5 2.0 all-to-all-done
  59.8 10.6 %project.1 = (bf16[4,576,512]{2,1,0:T(8,128)(2,1)}, bf16[12,128,512]{2,1,0:T(8,128)(2,1)}, bf16[12,128,512]{2,1,0:T(8,128)(2,1)}, bf16[12,80,512]{2,1,0:T(8,128)(2,1)}, bf16[12,80,128]{2,1,0:T(8,128)(2,1)}) custom-call(s32[11]{0:T(128)S(1)} %stack.126.sc, bf16[768,512]{1,0:T(8,128)(2,1)} %copy-done.11, s32[8,512]{1,0:T(8,128)S(1)} %broadcast_in_dim.8.starts_ref.refs_18_, ...), custom_call_target="tpu_custom_call" | custom-call | flops 2113929216 | bytes 11665408 | tf_op jit(solution)/shard_map/project/pallas_call | solution.py:45
  70.4 1.6 collective-permute-start.8
  74.0 1.5 collective-permute-start.12
  76.7 12.9 %collective-permute-done.12.refs_12_.refs_4_ = bf16[96,768]{1,0:T(8,128)(2,1)S(1)} collective-permute-done((bf16[96,768]{1,0:T(8,128)(2,1)S(1)}, bf16[96,768]{1,0:T(8,128)(2,1)S(1)}, u32[]{:S(2)}, u32[]{:S(2)}) %collective-permute-start.12) | collective-permute-done | bytes 147488 | tf_op jit(solution)/shard_map/ppermute | solution.py:519
  89.7 1.6 collective-permute-start.19
  95.0 3.5 all-to-all-start.1
  102.6 8.1 %local_mix.1.num_ref = f32[12,80,512]{2,1,0:T(8,128)} custom-call(s32[11]{0:T(128)S(1)} %stack.126.sc, bf16[12,128,512]{2,1,0:T(8,128)(2,1)S(1)} %copy-done, bf16[12,128,512]{2,1,0:T(8,128)(2,1)} %get-tuple-element.97.kf_ref.refs_12_, bf16[12,80,512]{2,1,0:T(8,128)(2,1)S(1)} %copy-done.9, s32[8,512]{1,0:T(8,128)S(1)} %broadcast_in_dim.8.starts_ref.refs_18_), custom_call_target="tpu_custom_call" | custom-call | flops 981467136 | bytes 6111232 | tf_op jit(solution)/shard_map/local_mix/pallas_call | solution.py:45
  113.2 7.3 %collective-permute-done.25.refs_11_ = bf16[384,768]{1,0:T(8,128)(2,1)} collective-permute-done((bf16[384,768]{1,0:T(8,128)(2,1)}, bf16[384,768]{1,0:T(8,128)(2,1)}, u32[]{:S(2)}, u32[]{:S(2)}) %collective-permute-start.25) | collective-permute-done | bytes 589856 | tf_op jit(solution)/shard_map/ppermute | solution.py:519
  123.6 2.6 collective-permute-start.9
  126.2 1.4 all-to-all-done.1
  130.3 8.0 %mix_out.1 = (bf16[12,80,128]{2,1,0:T(8,128)(2,1)S(1)}, f32[12,72,512]{2,1,0:T(8,128)}, bf16[768,512]{1,0:T(8,128)(2,1)}, f32[768,512]{1,0:T(8,128)}, bf16[768,5...) custom-call(s32[11]{0:T(128)S(1)} %stack.126.sc, f32[12,80,512]{2,1,0:T(8,128)} %local_mix.1.num_ref, ...), custom_call_target="tpu_custom_call" | custom-call | flops 729808896 | bytes 14540800 | tf_op jit(solution)/shard_map/mix_out/pallas_call | solution.py:45
  138.4 19.2 %feed_0.1 = (f32[512,768]{1,0:T(8,128)}, f32[768,512]{1,0:T(8,128)}, bf16[3,512,768]{2,1,0:T(8,128)(2,1)}, bf16[3,512,768]{2,1,0:T(8,128)(2,1)}, f32[3,16,384]{2,1,0:T(8,128)S(1)}) custom-call(s32[11]{0:T(128)S(1)} %stack.126.sc, bf16[512,768]{1,0:T(8,128)(2,1)} %get-tuple-element.107.hid_ref, bf16[512,768]{1,0:T(8,128)(2,1)} %copy-done.20, ...), custom_call_target="tpu_custom_call" | custom-call | flops 7247757312 | bytes 18137088 | tf_op jit(solution)/shard_map/feed_0/pallas_call | solution.py:45
  157.7 1.6 collective-permute-start.20
  159.6 14.0 %collective-permute-done.20.refs_3_ = bf16[384,768]{1,0:T(8,128)(2,1)S(1)} collective-permute-done((bf16[384,768]{1,0:T(8,128)(2,1)}, bf16[384,768]{1,0:T(8,128)(2,1)S(1)}, u32[]{:S(2)}, u32[]{:S(2)}) %collective-permute-start.20) | collective-permute-done | bytes 589856 | tf_op jit(solution)/shard_map/ppermute | solution.py:519
  175.6 2.0 collective-permute-done.18.refs_2_
  177.6 9.8 %feed_3.1 = (f32[512,768]{1,0:T(8,128)}, f32[768,512]{1,0:T(8,128)}, bf16[1,512,768]{2,1,0:T(8,128)(2,1)S(1)}, bf16[1,512,768]{2,1,0:T(8,128)(2,1)}, f32[1,16,384]{2,1,0:T(8,128)S(1)}) custom-call(s32[11]{0:T(128)S(1)} %stack.126.sc, bf16[512,768]{1,0:T(8,128)(2,1)} %get-tuple-element.107.hid_ref, bf16[512,768]{1,0:T(8,128)(2,1)} %copy-done.20, ...), custom_call_target="tpu_custom_call" | custom-call | flops 2415919104 | bytes 12337152 | tf_op jit(solution)/shard_map/feed_3/pallas_call | solution.py:45
  193.1 9.1 %second_back.1 = (f32[768,512]{1,0:T(8,128)}, bf16[768,512]{1,0:T(8,128)(2,1)S(1)}, f32[4,8,192]{2,1,0:T(8,128)S(1)}, bf16[12,80,512]{2,1,0:T(8,128)(2,1)S(1)}, bf16[12,80,128]{2,1,0:T(8,128)(2,1)}) custom-call(s32[11]{0:T(128)S(1)} %stack.126.sc, f32[768,512]{1,0:T(8,128)} %get-tuple-element.121.sg_ref, f32[768,512]{1,0:T(8,128)} %get-tuple-element.106.res_ref, ...), custom_call_target="tpu_custom_call" | custom-call | flops 729808896 | bytes 12107776 | tf_op jit(solution)/shard_map/second_back/pallas_call | solution.py:45
  208.8 2.5 collective-permute-start.35
  212.3 8.7 %down_grads.1 = (bf16[960,384]{1,0:T(8,128)(2,1)S(1)}, bf16[960,384]{1,0:T(8,128)(2,1)}, bf16[960,384]{1,0:T(8,128)(2,1)}, bf16[960,384]{1,0:T(8,128)(2,1)}) custom-call(s32[11]{0:T(128)S(1)} %stack.126.sc, bf16[768,512]{1,0:T(8,128)(2,1)} %bitcast.137, bf16[768,512]{1,0:T(8,128)(2,1)} %collective-permute-done.32.gyt2_ref, ...), custom_call_target="tpu_custom_call" | custom-call | flops 3019898880 | bytes 13565952 | tf_op jit(solution)/shard_map/down_grads/pallas_call | solution.py:45
  221.9 6.0 %up_grads.1 = (bf16[768,384]{1,0:T(8,128)(2,1)S(1)}, bf16[768,384]{1,0:T(8,128)(2,1)S(1)}, bf16[768,384]{1,0:T(8,128)(2,1)S(1)}, bf16[768,384]{1,0:T(8,128)(2,1)S(1)}) custom-call(s32[11]{0:T(128)S(1)} %stack.126.sc, bf16[768,512]{1,0:T(8,128)(2,1)S(1)} %copy-done.53, bf16[768,512]{1,0:T(8,128)(2,1)} %collective-permute-done.29.hidt2_ref, ...), custom_call_target="tpu_custom_call" | custom-call | flops 2415919104 | bytes 10223616 | tf_op jit(solution)/shard_map/up_grads/pallas_call | solution.py:45
  228.4 1.4 collective-permute-start.37
  229.8 12.8 %local_back.1 = (bf16[12,64,512]{2,1,0:T(8,128)(2,1)S(1)}, f32[12,128,512]{2,1,0:T(8,128)}, f32[12,64,512]{2,1,0:T(8,128)}) custom-call(s32[11]{0:T(128)S(1)} %stack.126.sc, bf16[12,128,512]{2,1,0:T(8,128)(2,1)} %get-tuple-element.96.qf_ref, bf16[12,128,512]{2,1,0:T(8,128)(2,1)} %get-tuple-element.97.kf_ref.refs_12_, bf16[12,80,512]{2,1,0:T(8,128)(2,1)S(1)} %copy-done.10, ...), custom_call_target="tpu_custom_call" | custom-call | flops 2944401408 | bytes 10878976 | tf_op jit(solution)/shard_map/local_back/pallas_call | solution.py:45
  243.6 13.9 %project_back.1 = (bf16[4,576,512]{2,1,0:T(8,128)(2,1)}, f32[768,512]{1,0:T(8,128)}, f32[4,64,384]{2,1,0:T(8,128)S(1)}, f32[4,8,576]{2,1,0:T(8,128)S(1)}) custom-call(s32[11]{0:T(128)S(1)} %stack.126.sc, bf16[12,80,128]{2,1,0:T(8,128)(2,1)S(1)} %collective-permute-done.28.refs_0_, bf16[12,80,128]{2,1,0:T(8,128)(2,1)S(1)} %collective-permute-done.35.refs_1_, ...), custom_call_target="tpu_custom_call" | custom-call | flops 2717908992 | bytes 19947520 | tf_op jit(solution)/shard_map/project_back/pallas_call | solution.py:45
  258.7 2.0 collective-permute-start.38
  260.7 1.5 collective-permute-start.40
  262.3 12.5 %collective-permute-done.38 = bf16[768,384]{1,0:T(8,128)(2,1)S(1)} collective-permute-done((bf16[768,384]{1,0:T(8,128)(2,1)S(1)}, bf16[768,384]{1,0:T(8,128)(2,1)S(1)}, u32[]{:S(2)}, u32[]{:S(2)}) %collective-permute-start.38) | collective-permute-done | bytes 589856 | tf_op jit(solution)/shard_map/ppermute | solution.py:519
  274.9 13.5 %collective-permute-done.39 = bf16[768,384]{1,0:T(8,128)(2,1)S(1)} collective-permute-done((bf16[768,384]{1,0:T(8,128)(2,1)S(1)}, bf16[768,384]{1,0:T(8,128)(2,1)S(1)}, u32[]{:S(2)}, u32[]{:S(2)}) %collective-permute-start.39) | collective-permute-done | bytes 589856 | tf_op jit(solution)/shard_map/ppermute | solution.py:519
  289.5 4.5 %first_back.1 = (bf16[4,192,512]{2,1,0:T(8,128)(2,1)}, f32[4,8,192]{2,1,0:T(8,128)S(1)}) custom-call(s32[11]{0:T(128)S(1)} %stack.126.sc, f32[768,512]{1,0:T(8,128)S(1)} %copy-done.13, bf16[768,512]{1,0:T(8,128)(2,1)S(1)} %bitcast.133, f32[768,512]{1,0:T(8,128)} %get-tuple-element.150.rg_ref, bf16[16,768]{1,0:T(8,128)(2,1)S(1)} %fusion.9.gain_ref), custom_call_target="tpu_custom_call" | custom-call | bytes 4767744 | tf_op jit(solution)/shard_map/first_back/pallas_call | solution.py:45
  294.1 1.4 copy-done.72
  295.5 5.6 %last_grads.1 = (bf16[704,384]{1,0:T(8,128)(2,1)S(1)}, bf16[704,384]{1,0:T(8,128)(2,1)S(1)}, bf16[704,384]{1,0:T(8,128)(2,1)S(1)}, bf16[704,384]{1,0:T(8,128)(2,1)S(1)}) custom-call(s32[11]{0:T(128)S(1)} %stack.126.sc, bf16[4,576,512]{2,1,0:T(8,128)(2,1)} %get-tuple-element.147.pg_ref, bf16[4,576,512]{2,1,0:T(8,128)(2,1)} %copy-done.72, ...), custom_call_target="tpu_custom_call" | custom-call | flops 1811939328 | bytes 8675328 | tf_op jit(solution)/shard_map/last_grads/pallas_call | solution.py:45
  301.5 1.4 collective-permute-start.44
  302.8 1.7 collective-permute-start.45
  304.9 1.4 collective-permute-start.48
  306.3 10.0 %collective-permute-done.43 = bf16[704,384]{1,0:T(8,128)(2,1)S(1)} collective-permute-done((bf16[704,384]{1,0:T(8,128)(2,1)S(1)}, bf16[704,384]{1,0:T(8,128)(2,1)S(1)}, u32[]{:S(2)}, u32[]{:S(2)}) %collective-permute-start.43) | collective-permute-done | bytes 540704 | tf_op jit(solution)/shard_map/ppermute | solution.py:519
  317.5 10.8 %collective-permute-done.44 = bf16[704,384]{1,0:T(8,128)(2,1)S(1)} collective-permute-done((bf16[704,384]{1,0:T(8,128)(2,1)S(1)}, bf16[704,384]{1,0:T(8,128)(2,1)S(1)}, u32[]{:S(2)}, u32[]{:S(2)}) %collective-permute-start.44) | collective-permute-done | bytes 540704 | tf_op jit(solution)/shard_map/ppermute | solution.py:519
  328.3 1.6 collective-permute-start.54
  330.9 4.2 all-to-all-start.4
  335.1 8.8 %collective-permute-done.47 = bf16[960,384]{1,0:T(8,128)(2,1)} collective-permute-done((bf16[960,384]{1,0:T(8,128)(2,1)}, bf16[960,384]{1,0:T(8,128)(2,1)}, u32[]{:S(2)}, u32[]{:S(2)}) %collective-permute-start.47) | collective-permute-done | bytes 737312 | tf_op jit(solution)/shard_map/ppermute | solution.py:519
  343.9 13.8 %collective-permute-done.49 = bf16[960,384]{1,0:T(8,128)(2,1)} collective-permute-done((bf16[960,384]{1,0:T(8,128)(2,1)}, bf16[960,384]{1,0:T(8,128)(2,1)}, u32[]{:S(2)}, u32[]{:S(2)}) %collective-permute-start.49) | collective-permute-done | bytes 737312 | tf_op jit(solution)/shard_map/ppermute | solution.py:519
  357.6 2.8 add_convert_fusion.2
  360.4 1.6 collective-permute-start.50
  362.0 4.1 block_out.1
  366.1 1.4 add_convert_fusion.4
  367.5 1.5 collective-permute-start.55
  369.0 3.5 all-to-all-start.2
  372.5 4.9 %collective-permute-done.50 = bf16[960,384]{1,0:T(8,128)(2,1)S(1)} collective-permute-done((bf16[960,384]{1,0:T(8,128)(2,1)}, bf16[960,384]{1,0:T(8,128)(2,1)S(1)}, u32[]{:S(2)}, u32[]{:S(2)}) %collective-permute-start.50) | collective-permute-done | bytes 737312 | tf_op jit(solution)/shard_map/ppermute | solution.py:519
  378.7 1.5 collective-permute-start.51
  382.8 4.6 %all-to-all-start.5 = ((bf16[4,176,384]{2,1,0:T(8,128)(2,1)}), bf16[4,176,384]{2,1,0:T(8,128)(2,1)S(1)}, u32[]{:S(2)}, u32[]{:S(2)}) async-start(bf16[4,176,384]{2,1,0:T(8,128)(2,1)} %broadcast_in_dim.21), calls=%async_computation.5 | async-start | bytes 1081344 | tf_op jit(solution)/shard_map/all_to_all | solution.py:523
  387.4 2.0 add_convert_fusion.3
  390.7 1.3 add_convert_fusion
  393.3 17.7 %all-to-all-done.5 = bf16[4,176,384]{2,1,0:T(8,128)(2,1)S(1)} async-done(((bf16[4,176,384]{2,1,0:T(8,128)(2,1)}), bf16[4,176,384]{2,1,0:T(8,128)(2,1)S(1)}, u32[]{:S(2)}, u32[]{:S(2)}) %all-to-all-start.5) | async-done | bytes 540704 | tf_op jit(solution)/shard_map/all_to_all | solution.py:523
  411.0 4.2 all-to-all-start.3
  417.0 8.8 %collective-permute-done.52 = bf16[960,384]{1,0:T(8,128)(2,1)} collective-permute-done((bf16[960,384]{1,0:T(8,128)(2,1)S(1)}, bf16[960,384]{1,0:T(8,128)(2,1)}, u32[]{:S(2)}, u32[]{:S(2)}) %collective-permute-start.52) | collective-permute-done | bytes 737312 | tf_op jit(solution)/shard_map/ppermute | solution.py:708
  428.1 2.1 copy.42
  430.2 2.1 up_result.1
  432.3 2.9 last_result.1
  437.1 2.5 down_result.1
  (278 shorter events, 67.1 us)
Async XLA Ops:
  20.9 15.5 %collective-permute-start = (bf16[336,768]{1,0:T(8,128)(2,1)S(1)}, bf16[336,768]{1,0:T(8,128)(2,1)S(1)}, u32[]{:S(2)}, u32[]{:S(2)}) collective-permute-start(bf16[336,768]{1,0:T(8,128)(2,1)S(1)} %get-tuple-element.94.refs_0_.refs_4_), channel_id=1, source_target_pairs={{0,4},{4,0},{8,12},{12,8},{1,5},{5,1},{9,13},{13,9},{2,6},{6,2},{1... | collective-permute-start | bytes 1548296 | tf_op jit(solution)/shard_map/ppermute | solution.py:519
  23.9 29.9 %collective-permute-start.2 = (bf16[336,768]{1,0:T(8,128)(2,1)S(1)}, bf16[336,768]{1,0:T(8,128)(2,1)S(1)}, u32[]{:S(2)}, u32[]{:S(2)}) collective-permute-start(bf16[336,768]{1,0:T(8,128)(2,1)S(1)} %get-tuple-element.94.refs_0_.refs_4_), channel_id=1, source_target_pairs={{0,8},{4,12},{8,0},{12,4},{1,9},{5,13},{9,1},{13,5},{2,10},{6,14},... | collective-permute-start | bytes 1548296 | tf_op jit(solution)/shard_map/ppermute | solution.py:519
  25.4 28.4 %collective-permute-start.4 = (bf16[336,768]{1,0:T(8,128)(2,1)S(1)}, bf16[336,768]{1,0:T(8,128)(2,1)S(1)}, u32[]{:S(2)}, u32[]{:S(2)}) collective-permute-start(bf16[336,768]{1,0:T(8,128)(2,1)S(1)} %get-tuple-element.94.refs_0_.refs_4_), channel_id=1, source_target_pairs={{0,12},{4,8},{8,4},{12,0},{1,13},{5,9},{9,5},{13,1},{2,14},{6,10},... | collective-permute-start | bytes 1548296 | tf_op jit(solution)/shard_map/ppermute | solution.py:519
  26.4 30.2 %all-to-all-start = ((bf16[4,192,512]{2,1,0:T(8,128)(2,1)}), bf16[4,192,512]{2,1,0:T(8,128)(2,1)S(1)}, u32[]{:S(2)}, u32[]{:S(2)}) async-start(bf16[4,192,512]{2,1,0:T(8,128)(2,1)} %bitcast.144), calls=%async_computation | async-start | bytes 1572864 | tf_op jit(solution)/shard_map/all_to_all | solution.py:523
  36.5 22.2 %collective-permute-start.1 = (bf16[336,768]{1,0:T(8,128)(2,1)S(1)}, bf16[336,768]{1,0:T(8,128)(2,1)}, u32[]{:S(2)}, u32[]{:S(2)}) collective-permute-start(bf16[336,768]{1,0:T(8,128)(2,1)S(1)} %collective-permute-done.refs_2_.refs_5_.refs_1_.refs_6_), channel_id=1, source_target_pairs={{0,16},{16,0},{1,17},{17,1},{2,18},{18,2},{3,19},{19,3},{4,20},{20... | collective-permute-start | bytes 1548296 | tf_op jit(solution)/shard_map/ppermute | solution.py:519
  53.8 4.9 %collective-permute-start.3 = (bf16[336,768]{1,0:T(8,128)(2,1)S(1)}, bf16[336,768]{1,0:T(8,128)(2,1)}, u32[]{:S(2)}, u32[]{:S(2)}) collective-permute-start(bf16[336,768]{1,0:T(8,128)(2,1)S(1)} %collective-permute-done.2.refs_4_.refs_6_.refs_2_.refs_8_), channel_id=1, source_target_pairs={{0,16},{16,0},{1,17},{17,1},{2,18},{18,2},{3,19},{19,3},{4,20},{20... | collective-permute-start | bytes 1548296 | tf_op jit(solution)/shard_map/ppermute | solution.py:519
  53.9 4.9 %collective-permute-start.5 = (bf16[336,768]{1,0:T(8,128)(2,1)S(1)}, bf16[336,768]{1,0:T(8,128)(2,1)}, u32[]{:S(2)}, u32[]{:S(2)}) collective-permute-start(bf16[336,768]{1,0:T(8,128)(2,1)S(1)} %collective-permute-done.4.refs_6_.refs_7_.refs_0_.refs_3_.refs_10_), channel_id=1, source_target_pairs={{0,16},{16,0},{1,17},{17,1},{2,18},{18,2},{3,19},{19,3},{4,20},{20... | collective-permute-start | bytes 1548296 | tf_op jit(solution)/shard_map/ppermute | solution.py:519
  54.5 21.0 %collective-permute-start.10 = (bf16[96,768]{1,0:T(8,128)(2,1)S(1)}, bf16[96,768]{1,0:T(8,128)(2,1)}, u32[]{:S(2)}, u32[]{:S(2)}) collective-permute-start(bf16[96,768]{1,0:T(8,128)(2,1)S(1)} %get-tuple-element.105.refs_8_.refs_0_), channel_id=1, source_target_pairs={{0,4},{4,0},{8,12},{12,8},{1,5},{5,1},{9,13},{13,9},{2,6},{6,2},{1... | collective-permute-start | bytes 442376 | tf_op jit(solution)/shard_map/ppermute | solution.py:519
  70.4 21.6 %collective-permute-start.8 = (bf16[12,80,128]{2,1,0:T(8,128)(2,1)}, bf16[12,80,128]{2,1,0:T(8,128)(2,1)S(1)}, u32[]{:S(2)}, u32[]{:S(2)}) collective-permute-start(bf16[12,80,128]{2,1,0:T(8,128)(2,1)} %get-tuple-element.99), channel_id=1, source_target_pairs={{0,12},{4,8},{8,4},{12,0},{1,13},{5,9},{9,5},{13,1},{2,14},{6,10},... | collective-permute-start | bytes 737288 | tf_op jit(solution)/shard_map/ppermute | solution.py:519
  72.0 21.3 %collective-permute-start.7 = (bf16[12,80,128]{2,1,0:T(8,128)(2,1)}, bf16[12,80,128]{2,1,0:T(8,128)(2,1)S(1)}, u32[]{:S(2)}, u32[]{:S(2)}) collective-permute-start(bf16[12,80,128]{2,1,0:T(8,128)(2,1)} %get-tuple-element.99), channel_id=1, source_target_pairs={{0,8},{4,12},{8,0},{12,4},{1,9},{5,13},{9,1},{13,5},{2,10},{6,14},... | collective-permute-start | bytes 737288 | tf_op jit(solution)/shard_map/ppermute | solution.py:519
  73.2 27.1 %collective-permute-start.6 = (bf16[12,80,128]{2,1,0:T(8,128)(2,1)}, bf16[12,80,128]{2,1,0:T(8,128)(2,1)}, u32[]{:S(2)}, u32[]{:S(2)}) collective-permute-start(bf16[12,80,128]{2,1,0:T(8,128)(2,1)} %get-tuple-element.99), channel_id=1, source_target_pairs={{0,4},{4,0},{8,12},{12,8},{1,5},{5,1},{9,13},{13,9},{2,6},{6,2},{1... | collective-permute-start | bytes 737288 | tf_op jit(solution)/shard_map/ppermute | solution.py:519
  74.0 15.7 %collective-permute-start.12 = (bf16[96,768]{1,0:T(8,128)(2,1)S(1)}, bf16[96,768]{1,0:T(8,128)(2,1)S(1)}, u32[]{:S(2)}, u32[]{:S(2)}) collective-permute-start(bf16[96,768]{1,0:T(8,128)(2,1)S(1)} %get-tuple-element.105.refs_8_.refs_0_), channel_id=1, source_target_pairs={{0,8},{4,12},{8,0},{12,4},{1,9},{5,13},{9,1},{13,5},{2,10},{6,14},... | collective-permute-start | bytes 442376 | tf_op jit(solution)/shard_map/ppermute | solution.py:519
  75.5 14.2 %collective-permute-start.14 = (bf16[96,768]{1,0:T(8,128)(2,1)S(1)}, bf16[96,768]{1,0:T(8,128)(2,1)S(1)}, u32[]{:S(2)}, u32[]{:S(2)}) collective-permute-start(bf16[96,768]{1,0:T(8,128)(2,1)S(1)} %get-tuple-element.105.refs_8_.refs_0_), channel_id=1, source_target_pairs={{0,12},{4,8},{8,4},{12,0},{1,13},{5,9},{9,5},{13,1},{2,14},{6,10},... | collective-permute-start | bytes 442376 | tf_op jit(solution)/shard_map/ppermute | solution.py:519
  89.7 23.0 %collective-permute-start.19 = (bf16[384,768]{1,0:T(8,128)(2,1)}, bf16[384,768]{1,0:T(8,128)(2,1)}, u32[]{:S(2)}, u32[]{:S(2)}) collective-permute-start(bf16[384,768]{1,0:T(8,128)(2,1)} %get-tuple-element.117.refs_9_), channel_id=1, source_target_pairs={{0,8},{4,12},{8,0},{12,4},{1,9},{5,13},{9,1},{13,5},{2,10},{6,14},... | collective-permute-start | bytes 1769480 | tf_op jit(solution)/shard_map/ppermute | solution.py:519
  91.3 21.6 %collective-permute-start.16 = (bf16[384,768]{1,0:T(8,128)(2,1)}, bf16[384,768]{1,0:T(8,128)(2,1)}, u32[]{:S(2)}, u32[]{:S(2)}) collective-permute-start(bf16[384,768]{1,0:T(8,128)(2,1)} %get-tuple-element.115.refs_3_), channel_id=1, source_target_pairs={{0,4},{4,0},{8,12},{12,8},{1,5},{5,1},{9,13},{13,9},{2,6},{6,2},{1... | collective-permute-start | bytes 1769480 | tf_op jit(solution)/shard_map/ppermute | solution.py:519
  92.1 28.4 %collective-permute-start.25 = (bf16[384,768]{1,0:T(8,128)(2,1)}, bf16[384,768]{1,0:T(8,128)(2,1)}, u32[]{:S(2)}, u32[]{:S(2)}) collective-permute-start(bf16[384,768]{1,0:T(8,128)(2,1)} %get-tuple-element.117.refs_9_), channel_id=1, source_target_pairs={{0,4},{4,0},{8,12},{12,8},{1,5},{5,1},{9,13},{13,9},{2,6},{6,2},{1... | collective-permute-start | bytes 1769480 | tf_op jit(solution)/shard_map/ppermute | solution.py:519
  93.3 27.2 %collective-permute-start.23 = (bf16[384,768]{1,0:T(8,128)(2,1)}, bf16[384,768]{1,0:T(8,128)(2,1)}, u32[]{:S(2)}, u32[]{:S(2)}) collective-permute-start(bf16[384,768]{1,0:T(8,128)(2,1)} %get-tuple-element.115.refs_3_), channel_id=1, source_target_pairs={{0,8},{4,12},{8,0},{12,4},{1,9},{5,13},{9,1},{13,5},{2,10},{6,14},... | collective-permute-start | bytes 1769480 | tf_op jit(solution)/shard_map/ppermute | solution.py:519
  95.0 32.6 %all-to-all-start.1 = ((bf16[4,192,512]{2,1,0:T(8,128)(2,1)}), bf16[4,192,512]{2,1,0:T(8,128)(2,1)S(1)}, u32[]{:S(2)}, u32[]{:S(2)}) async-start(bf16[4,192,512]{2,1,0:T(8,128)(2,1)} %bitcast.142), calls=%async_computation.1 | async-start | bytes 1572864 | tf_op jit(solution)/shard_map/all_to_all | solution.py:523
  100.3 10.4 %collective-permute-start.11 = (bf16[96,768]{1,0:T(8,128)(2,1)}, bf16[96,768]{1,0:T(8,128)(2,1)S(1)}, u32[]{:S(2)}, u32[]{:S(2)}) collective-permute-start(bf16[96,768]{1,0:T(8,128)(2,1)} %collective-permute-done.10.refs_10_.refs_2_), channel_id=1, source_target_pairs={{0,16},{16,0},{1,17},{17,1},{2,18},{18,2},{3,19},{19,3},{4,20},{20... | collective-permute-start | bytes 442376 | tf_op jit(solution)/shard_map/ppermute | solution.py:519
  110.7 1.6 collective-permute-start.13
  112.3 10.6 %collective-permute-start.15 = (bf16[96,768]{1,0:T(8,128)(2,1)S(1)}, bf16[96,768]{1,0:T(8,128)(2,1)S(1)}, u32[]{:S(2)}, u32[]{:S(2)}) collective-permute-start(bf16[96,768]{1,0:T(8,128)(2,1)S(1)} %copy-done.32), channel_id=1, source_target_pairs={{0,16},{16,0},{1,17},{17,1},{2,18},{18,2},{3,19},{19,3},{4,20},{20... | collective-permute-start | bytes 442376 | tf_op jit(solution)/shard_map/ppermute | solution.py:519
  112.7 25.6 %collective-permute-start.27 = (bf16[384,768]{1,0:T(8,128)(2,1)}, bf16[384,768]{1,0:T(8,128)(2,1)}, u32[]{:S(2)}, u32[]{:S(2)}) collective-permute-start(bf16[384,768]{1,0:T(8,128)(2,1)} %collective-permute-done.19.refs_13_), channel_id=1, source_target_pairs={{0,16},{16,0},{1,17},{17,1},{2,18},{18,2},{3,19},{19,3},{4,20},{20... | collective-permute-start | bytes 1769480 | tf_op jit(solution)/shard_map/ppermute | solution.py:519
  112.8 25.5 %collective-permute-start.22 = (bf16[384,768]{1,0:T(8,128)(2,1)}, bf16[384,768]{1,0:T(8,128)(2,1)}, u32[]{:S(2)}, u32[]{:S(2)}) collective-permute-start(bf16[384,768]{1,0:T(8,128)(2,1)} %collective-permute-done.16.refs_5_), channel_id=1, source_target_pairs={{0,16},{16,0},{1,17},{17,1},{2,18},{18,2},{3,19},{19,3},{4,20},{20... | collective-permute-start | bytes 1769480 | tf_op jit(solution)/shard_map/ppermute | solution.py:519
  120.5 17.9 %collective-permute-start.26 = (bf16[384,768]{1,0:T(8,128)(2,1)}, bf16[384,768]{1,0:T(8,128)(2,1)}, u32[]{:S(2)}, u32[]{:S(2)}) collective-permute-start(bf16[384,768]{1,0:T(8,128)(2,1)} %collective-permute-done.25.refs_11_), channel_id=1, source_target_pairs={{0,16},{16,0},{1,17},{17,1},{2,18},{18,2},{3,19},{19,3},{4,20},{20... | collective-permute-start | bytes 1769480 | tf_op jit(solution)/shard_map/ppermute | solution.py:519
  120.5 17.9 %collective-permute-start.24 = (bf16[384,768]{1,0:T(8,128)(2,1)}, bf16[384,768]{1,0:T(8,128)(2,1)}, u32[]{:S(2)}, u32[]{:S(2)}) collective-permute-start(bf16[384,768]{1,0:T(8,128)(2,1)} %collective-permute-done.23.refs_7_), channel_id=1, source_target_pairs={{0,16},{16,0},{1,17},{17,1},{2,18},{18,2},{3,19},{19,3},{4,20},{20... | collective-permute-start | bytes 1769480 | tf_op jit(solution)/shard_map/ppermute | solution.py:519
  123.6 5.7 %collective-permute-start.9 = (bf16[12,80,128]{2,1,0:T(8,128)(2,1)}, bf16[12,80,128]{2,1,0:T(8,128)(2,1)}, u32[]{:S(2)}, u32[]{:S(2)}) collective-permute-start(bf16[12,80,128]{2,1,0:T(8,128)(2,1)} %bitcast.39), channel_id=1, source_target_pairs={{0,16},{1,17},{2,18},{3,19},{4,20},{5,21},{6,22},{7,23},{8,24},{9,... | collective-permute-start | bytes 737288 | tf_op jit(solution)/shard_map/ppermute | solution.py:536
  157.6 53.8 %collective-permute-start.30 = (bf16[3,512,768]{2,1,0:T(8,128)(2,1)}, bf16[3,512,768]{2,1,0:T(8,128)(2,1)}, u32[]{:S(2)}, u32[]{:S(2)}) collective-permute-start(bf16[3,512,768]{2,1,0:T(8,128)(2,1)} %get-tuple-element.127), channel_id=1, source_target_pairs={{0,16},{16,0},{1,17},{17,1},{2,18},{18,2},{3,19},{19,3},{4,20},{20... | collective-permute-start | bytes 7077896 | tf_op jit(solution)/shard_map/ppermute | solution.py:519
  157.7 16.0 %collective-permute-start.20 = (bf16[384,768]{1,0:T(8,128)(2,1)}, bf16[384,768]{1,0:T(8,128)(2,1)S(1)}, u32[]{:S(2)}, u32[]{:S(2)}) collective-permute-start(bf16[384,768]{1,0:T(8,128)(2,1)} %collective-permute-done.19.refs_13_), channel_id=1, source_target_pairs={{0,4},{4,0},{8,12},{12,8},{1,5},{5,1},{9,13},{13,9},{2,6},{6,2},{1... | collective-permute-start | bytes 1769480 | tf_op jit(solution)/shard_map/ppermute | solution.py:519
  159.2 15.6 %collective-permute-start.17 = (bf16[384,768]{1,0:T(8,128)(2,1)}, bf16[384,768]{1,0:T(8,128)(2,1)S(1)}, u32[]{:S(2)}, u32[]{:S(2)}) collective-permute-start(bf16[384,768]{1,0:T(8,128)(2,1)} %collective-permute-done.16.refs_5_), channel_id=1, source_target_pairs={{0,8},{4,12},{8,0},{12,4},{1,9},{5,13},{9,1},{13,5},{2,10},{6,14},... | collective-permute-start | bytes 1769480 | tf_op jit(solution)/shard_map/ppermute | solution.py:519
  173.6 2.0 collective-permute-start.21
  174.8 2.8 collective-permute-start.18
  174.8 28.3 %collective-permute-start.32 = (bf16[768,512]{1,0:T(8,128)(2,1)S(1)}, bf16[768,512]{1,0:T(8,128)(2,1)}, u32[]{:S(2)}, u32[]{:S(2)}) collective-permute-start(bf16[768,512]{1,0:T(8,128)(2,1)S(1)} %bitcast.135), channel_id=1, source_target_pairs={{0,16},{16,0},{1,17},{17,1},{2,18},{18,2},{3,19},{19,3},{4,20},{20... | collective-permute-start | bytes 2359304 | tf_op jit(solution)/shard_map/ppermute | solution.py:519
  175.3 31.7 %collective-permute-start.33 = (bf16[768,512]{1,0:T(8,128)(2,1)}, bf16[768,512]{1,0:T(8,128)(2,1)}, u32[]{:S(2)}, u32[]{:S(2)}) collective-permute-start(bf16[768,512]{1,0:T(8,128)(2,1)} %get-tuple-element.130.mix_ref), channel_id=1, source_target_pairs={{0,16},{16,0},{1,17},{17,1},{2,18},{18,2},{3,19},{19,3},{4,20},{20... | collective-permute-start | bytes 2359304 | tf_op jit(solution)/shard_map/ppermute | solution.py:519
  188.9 22.4 %collective-permute-start.31 = (bf16[1,512,768]{2,1,0:T(8,128)(2,1)}, bf16[1,512,768]{2,1,0:T(8,128)(2,1)}, u32[]{:S(2)}, u32[]{:S(2)}) collective-permute-start(bf16[1,512,768]{2,1,0:T(8,128)(2,1)} %get-tuple-element.128), channel_id=1, source_target_pairs={{0,16},{16,0},{1,17},{17,1},{2,18},{18,2},{3,19},{19,3},{4,20},{20... | collective-permute-start | bytes 2359304 | tf_op jit(solution)/shard_map/ppermute | solution.py:519
  189.0 32.9 %collective-permute-start.29 = (bf16[768,512]{1,0:T(8,128)(2,1)}, bf16[768,512]{1,0:T(8,128)(2,1)}, u32[]{:S(2)}, u32[]{:S(2)}) collective-permute-start(bf16[768,512]{1,0:T(8,128)(2,1)} %get-tuple-element.124.hidt_ref), channel_id=1, source_target_pairs={{0,16},{16,0},{1,17},{17,1},{2,18},{18,2},{3,19},{19,3},{4,20},{20... | collective-permute-start | bytes 2359304 | tf_op jit(solution)/shard_map/ppermute | solution.py:519
  204.0 4.1 collective-permute-start.34
  207.0 21.0 %collective-permute-start.36 = (bf16[12,80,128]{2,1,0:T(8,128)(2,1)}, bf16[12,80,128]{2,1,0:T(8,128)(2,1)S(1)}, u32[]{:S(2)}, u32[]{:S(2)}) collective-permute-start(bf16[12,80,128]{2,1,0:T(8,128)(2,1)} %get-tuple-element.123), channel_id=1, source_target_pairs={{0,12},{4,8},{8,4},{12,0},{1,13},{5,9},{9,5},{13,1},{2,14},{6,10},... | collective-permute-start | bytes 737288 | tf_op jit(solution)/shard_map/ppermute | solution.py:519
  208.8 19.2 %collective-permute-start.35 = (bf16[12,80,128]{2,1,0:T(8,128)(2,1)}, bf16[12,80,128]{2,1,0:T(8,128)(2,1)S(1)}, u32[]{:S(2)}, u32[]{:S(2)}) collective-permute-start(bf16[12,80,128]{2,1,0:T(8,128)(2,1)} %get-tuple-element.123), channel_id=1, source_target_pairs={{0,8},{4,12},{8,0},{12,4},{1,9},{5,13},{9,1},{13,5},{2,10},{6,14},... | collective-permute-start | bytes 737288 | tf_op jit(solution)/shard_map/ppermute | solution.py:519
  211.3 16.8 %collective-permute-start.28 = (bf16[12,80,128]{2,1,0:T(8,128)(2,1)}, bf16[12,80,128]{2,1,0:T(8,128)(2,1)S(1)}, u32[]{:S(2)}, u32[]{:S(2)}) collective-permute-start(bf16[12,80,128]{2,1,0:T(8,128)(2,1)} %get-tuple-element.123), channel_id=1, source_target_pairs={{0,4},{4,0},{8,12},{12,8},{1,5},{5,1},{9,13},{13,9},{2,6},{6,2},{1... | collective-permute-start | bytes 737288 | tf_op jit(solution)/shard_map/ppermute | solution.py:519
  228.4 15.2 %collective-permute-start.37 = (bf16[12,80,128]{2,1,0:T(8,128)(2,1)S(1)}, bf16[12,80,128]{2,1,0:T(8,128)(2,1)S(1)}, u32[]{:S(2)}, u32[]{:S(2)}) collective-permute-start(bf16[12,80,128]{2,1,0:T(8,128)(2,1)S(1)} %bitcast.150), channel_id=1, source_target_pairs={{16,0},{17,1},{18,2},{19,3},{20,4},{21,5},{22,6},{23,7},{24,8},{25... | collective-permute-start | bytes 737288 | tf_op jit(solution)/shard_map/ppermute | solution.py:536
  257.5 36.5 %collective-permute-start.41 = (bf16[4,576,512]{2,1,0:T(8,128)(2,1)}, bf16[4,576,512]{2,1,0:T(8,128)(2,1)S(1)}, u32[]{:S(2)}, u32[]{:S(2)}) collective-permute-start(bf16[4,576,512]{2,1,0:T(8,128)(2,1)} %get-tuple-element.147.pg_ref), channel_id=1, source_target_pairs={{0,16},{16,0},{1,17},{17,1},{2,18},{18,2},{3,19},{19,3},{4,20},{20... | collective-permute-start | bytes 7077896 | tf_op jit(solution)/shard_map/ppermute | solution.py:519
  258.7 16.1 %collective-permute-start.38 = (bf16[768,384]{1,0:T(8,128)(2,1)S(1)}, bf16[768,384]{1,0:T(8,128)(2,1)S(1)}, u32[]{:S(2)}, u32[]{:S(2)}) collective-permute-start(bf16[768,384]{1,0:T(8,128)(2,1)S(1)} %get-tuple-element.144), channel_id=1, source_target_pairs={{0,4},{4,0},{8,12},{12,8},{1,5},{5,1},{9,13},{13,9},{2,6},{6,2},{1... | collective-permute-start | bytes 1769480 | tf_op jit(solution)/shard_map/ppermute | solution.py:519
  260.7 27.7 %collective-permute-start.39 = (bf16[768,384]{1,0:T(8,128)(2,1)S(1)}, bf16[768,384]{1,0:T(8,128)(2,1)S(1)}, u32[]{:S(2)}, u32[]{:S(2)}) collective-permute-start(bf16[768,384]{1,0:T(8,128)(2,1)S(1)} %get-tuple-element.145), channel_id=1, source_target_pairs={{0,8},{4,12},{8,0},{12,4},{1,9},{5,13},{9,1},{13,5},{2,10},{6,14},... | collective-permute-start | bytes 1769480 | tf_op jit(solution)/shard_map/ppermute | solution.py:519
  260.7 27.7 %collective-permute-start.40 = (bf16[768,384]{1,0:T(8,128)(2,1)S(1)}, bf16[768,384]{1,0:T(8,128)(2,1)S(1)}, u32[]{:S(2)}, u32[]{:S(2)}) collective-permute-start(bf16[768,384]{1,0:T(8,128)(2,1)S(1)} %get-tuple-element.146), channel_id=1, source_target_pairs={{0,12},{4,8},{8,4},{12,0},{1,13},{5,9},{9,5},{13,1},{2,14},{6,10},... | collective-permute-start | bytes 1769480 | tf_op jit(solution)/shard_map/ppermute | solution.py:519
  262.3 31.8 %collective-permute-start.42 = (bf16[384,512]{1,0:T(8,128)(2,1)S(1)}, bf16[384,512]{1,0:T(8,128)(2,1)S(1)}, u32[]{:S(2)}, u32[]{:S(2)}) collective-permute-start(bf16[384,512]{1,0:T(8,128)(2,1)S(1)} %constant_dynamic-slice_fusion), channel_id=1, source_target_pairs={{0,16},{16,0},{1,17},{17,1},{2,18},{18,2},{3,19},{19,3},{4,20},{20... | collective-permute-start | bytes 1179656 | tf_op jit(solution)/shard_map/ppermute | solution.py:519
  301.0 15.3 %collective-permute-start.43 = (bf16[704,384]{1,0:T(8,128)(2,1)S(1)}, bf16[704,384]{1,0:T(8,128)(2,1)S(1)}, u32[]{:S(2)}, u32[]{:S(2)}) collective-permute-start(bf16[704,384]{1,0:T(8,128)(2,1)S(1)} %get-tuple-element.158), channel_id=1, source_target_pairs={{0,4},{4,0},{8,12},{12,8},{1,5},{5,1},{9,13},{13,9},{2,6},{6,2},{1... | collective-permute-start | bytes 1622024 | tf_op jit(solution)/shard_map/ppermute | solution.py:519
  301.5 26.8 %collective-permute-start.44 = (bf16[704,384]{1,0:T(8,128)(2,1)S(1)}, bf16[704,384]{1,0:T(8,128)(2,1)S(1)}, u32[]{:S(2)}, u32[]{:S(2)}) collective-permute-start(bf16[704,384]{1,0:T(8,128)(2,1)S(1)} %get-tuple-element.159), channel_id=1, source_target_pairs={{0,8},{4,12},{8,0},{12,4},{1,9},{5,13},{9,1},{13,5},{2,10},{6,14},... | collective-permute-start | bytes 1622024 | tf_op jit(solution)/shard_map/ppermute | solution.py:519
  302.8 27.0 %collective-permute-start.45 = (bf16[704,384]{1,0:T(8,128)(2,1)S(1)}, bf16[704,384]{1,0:T(8,128)(2,1)S(1)}, u32[]{:S(2)}, u32[]{:S(2)}) collective-permute-start(bf16[704,384]{1,0:T(8,128)(2,1)S(1)} %get-tuple-element.160), channel_id=1, source_target_pairs={{0,12},{4,8},{8,4},{12,0},{1,13},{5,9},{9,5},{13,1},{2,14},{6,10},... | collective-permute-start | bytes 1622024 | tf_op jit(solution)/shard_map/ppermute | solution.py:519
  304.6 39.3 %collective-permute-start.47 = (bf16[960,384]{1,0:T(8,128)(2,1)}, bf16[960,384]{1,0:T(8,128)(2,1)}, u32[]{:S(2)}, u32[]{:S(2)}) collective-permute-start(bf16[960,384]{1,0:T(8,128)(2,1)} %get-tuple-element.166), channel_id=1, source_target_pairs={{0,4},{4,0},{8,12},{12,8},{1,5},{5,1},{9,13},{13,9},{2,6},{6,2},{1... | collective-permute-start | bytes 2211848 | tf_op jit(solution)/shard_map/ppermute | solution.py:519
  304.9 38.9 %collective-permute-start.48 = (bf16[960,384]{1,0:T(8,128)(2,1)}, bf16[960,384]{1,0:T(8,128)(2,1)}, u32[]{:S(2)}, u32[]{:S(2)}) collective-permute-start(bf16[960,384]{1,0:T(8,128)(2,1)} %get-tuple-element.167), channel_id=1, source_target_pairs={{0,8},{4,12},{8,0},{12,4},{1,9},{5,13},{9,1},{13,5},{2,10},{6,14},... | collective-permute-start | bytes 2211848 | tf_op jit(solution)/shard_map/ppermute | solution.py:519
  316.3 41.3 %collective-permute-start.49 = (bf16[960,384]{1,0:T(8,128)(2,1)}, bf16[960,384]{1,0:T(8,128)(2,1)}, u32[]{:S(2)}, u32[]{:S(2)}) collective-permute-start(bf16[960,384]{1,0:T(8,128)(2,1)} %get-tuple-element.168), channel_id=1, source_target_pairs={{0,12},{4,8},{8,4},{12,0},{1,13},{5,9},{9,5},{13,1},{2,14},{6,10},... | collective-permute-start | bytes 2211848 | tf_op jit(solution)/shard_map/ppermute | solution.py:519
  328.3 37.8 %collective-permute-start.54 = (bf16[768,384]{1,0:T(8,128)(2,1)}, bf16[768,384]{1,0:T(8,128)(2,1)}, u32[]{:S(2)}, u32[]{:S(2)}) collective-permute-start(bf16[768,384]{1,0:T(8,128)(2,1)} %add_convert_fusion.5), channel_id=1, source_target_pairs={{0,1},{1,0},{2,3},{3,2},{4,5},{5,4},{6,7},{7,6},{8,9},{9,8},{10,11... | collective-permute-start | bytes 1769480 | tf_op jit(solution)/shard_map/ppermute | solution.py:519
  330.9 38.1 %all-to-all-start.4 = ((bf16[4,176,384]{2,1,0:T(8,128)(2,1)}), bf16[4,176,384]{2,1,0:T(8,128)(2,1)}, u32[]{:S(2)}, u32[]{:S(2)}) async-start(bf16[4,176,384]{2,1,0:T(8,128)(2,1)} %bitcast.67), calls=%async_computation.4 | async-start | bytes 1081344 | tf_op jit(solution)/shard_map/all_to_all | solution.py:523
  360.4 17.0 %collective-permute-start.50 = (bf16[960,384]{1,0:T(8,128)(2,1)}, bf16[960,384]{1,0:T(8,128)(2,1)S(1)}, u32[]{:S(2)}, u32[]{:S(2)}) collective-permute-start(bf16[960,384]{1,0:T(8,128)(2,1)} %add_convert_fusion.2), channel_id=1, source_target_pairs={{0,1},{1,0},{2,3},{3,2},{4,5},{5,4},{6,7},{7,6},{8,9},{9,8},{10,11... | collective-permute-start | bytes 2211848 | tf_op jit(solution)/shard_map/ppermute | solution.py:519
  367.5 19.9 %collective-permute-start.55 = (bf16[768,384]{1,0:T(8,128)(2,1)S(1)}, bf16[768,384]{1,0:T(8,128)(2,1)}, u32[]{:S(2)}, u32[]{:S(2)}) collective-permute-start(bf16[768,384]{1,0:T(8,128)(2,1)S(1)} %add_convert_fusion.4), channel_id=1, source_target_pairs={{1,2},{2,1},{5,6},{6,5},{9,10},{10,9},{13,14},{14,13},{17,18},{18,... | collective-permute-start | bytes 1769480 | tf_op jit(solution)/shard_map/ppermute | solution.py:706
  369.0 12.8 %all-to-all-start.2 = ((bf16[4,192,512]{2,1,0:T(8,128)(2,1)}), bf16[4,192,512]{2,1,0:T(8,128)(2,1)S(1)}, u32[]{:S(2)}, u32[]{:S(2)}) async-start(bf16[4,192,512]{2,1,0:T(8,128)(2,1)} %block_out.1), calls=%async_computation.2 | async-start | bytes 1572864 | tf_op jit(solution)/shard_map/all_to_all | solution.py:523
  378.7 12.0 %collective-permute-start.51 = (bf16[960,384]{1,0:T(8,128)(2,1)S(1)}, bf16[960,384]{1,0:T(8,128)(2,1)}, u32[]{:S(2)}, u32[]{:S(2)}) collective-permute-start(bf16[960,384]{1,0:T(8,128)(2,1)S(1)} %add_convert_fusion.1), channel_id=1, source_target_pairs={{1,2},{2,1},{5,6},{6,5},{9,10},{10,9},{13,14},{14,13},{17,18},{18,... | collective-permute-start | bytes 2211848 | tf_op jit(solution)/shard_map/ppermute | solution.py:706
  382.8 28.3 %all-to-all-start.5 = ((bf16[4,176,384]{2,1,0:T(8,128)(2,1)}), bf16[4,176,384]{2,1,0:T(8,128)(2,1)S(1)}, u32[]{:S(2)}, u32[]{:S(2)}) async-start(bf16[4,176,384]{2,1,0:T(8,128)(2,1)} %broadcast_in_dim.21), calls=%async_computation.5 | async-start | bytes 1081344 | tf_op jit(solution)/shard_map/all_to_all | solution.py:523
  389.4 25.8 %collective-permute-start.56 = (bf16[768,384]{1,0:T(8,128)(2,1)}, bf16[768,384]{1,0:T(8,128)(2,1)}, u32[]{:S(2)}, u32[]{:S(2)}) collective-permute-start(bf16[768,384]{1,0:T(8,128)(2,1)} %add_convert_fusion.3), channel_id=1, source_target_pairs={{1,0},{2,3},{5,4},{6,7},{9,8},{10,11},{13,12},{14,15},{17,16},{18,... | collective-permute-start | bytes 1769480 | tf_op jit(solution)/shard_map/ppermute | solution.py:708
  392.0 33.8 %collective-permute-start.52 = (bf16[960,384]{1,0:T(8,128)(2,1)S(1)}, bf16[960,384]{1,0:T(8,128)(2,1)}, u32[]{:S(2)}, u32[]{:S(2)}) collective-permute-start(bf16[960,384]{1,0:T(8,128)(2,1)S(1)} %add_convert_fusion), channel_id=1, source_target_pairs={{1,0},{2,3},{5,4},{6,7},{9,8},{10,11},{13,12},{14,15},{17,16},{18,... | collective-permute-start | bytes 2211848 | tf_op jit(solution)/shard_map/ppermute | solution.py:708
  411.0 17.0 %all-to-all-start.3 = ((bf16[4,192,512]{2,1,0:T(8,128)(2,1)}), bf16[4,192,512]{2,1,0:T(8,128)(2,1)}, u32[]{:S(2)}, u32[]{:S(2)}) async-start(bf16[4,192,512]{2,1,0:T(8,128)(2,1)} %get-tuple-element.151), calls=%async_computation.3 | async-start | bytes 1572864 | tf_op jit(solution)/shard_map/all_to_all | solution.py:523
  416.4 13.8 %collective-permute-start.57 = (bf16[768,384]{1,0:T(8,128)(2,1)S(1)}, bf16[768,384]{1,0:T(8,128)(2,1)S(1)}, u32[]{:S(2)}, u32[]{:S(2)}) collective-permute-start(bf16[768,384]{1,0:T(8,128)(2,1)S(1)} %broadcast_select_fusion.1.mine_ref), channel_id=1, source_target_pairs={{0,16},{16,0},{1,17},{17,1},{2,18},{18,2},{3,19},{19,3},{4,20},{20... | collective-permute-start | bytes 1769480 | tf_op jit(solution)/shard_map/ppermute | solution.py:519
  416.5 15.8 %collective-permute-start.46 = (bf16[704,384]{1,0:T(8,128)(2,1)S(1)}, bf16[704,384]{1,0:T(8,128)(2,1)}, u32[]{:S(2)}, u32[]{:S(2)}) collective-permute-start(bf16[704,384]{1,0:T(8,128)(2,1)S(1)} %bitcast.138), channel_id=1, source_target_pairs={{0,16},{16,0},{1,17},{17,1},{2,18},{18,2},{3,19},{19,3},{4,20},{20... | collective-permute-start | bytes 1622024 | tf_op jit(solution)/shard_map/ppermute | solution.py:519
  427.0 10.0 %collective-permute-start.53 = (bf16[960,384]{1,0:T(8,128)(2,1)S(1)}, bf16[960,384]{1,0:T(8,128)(2,1)S(1)}, u32[]{:S(2)}, u32[]{:S(2)}) collective-permute-start(bf16[960,384]{1,0:T(8,128)(2,1)S(1)} %broadcast_select_fusion.mine_ref), channel_id=1, source_target_pairs={{0,16},{16,0},{1,17},{17,1},{2,18},{18,2},{3,19},{19,3},{4,20},{20... | collective-permute-start | bytes 2211848 | tf_op jit(solution)/shard_map/ppermute | solution.py:519
  (73 other events, 735.2 us)
